TPU v7x, 128 devices: a whole 4x4x4 slice. The times are simulated.
128 devices in a mesh: row: 16 (over x, y_hi, core), col: 8 (over z, y_lo).
Axes of the slice: x: 4, y: 4 (y_hi: 2, y_lo: 2; y = y_hi * 2 + y_lo), z: 4, core: 2. Of those that a mesh axis runs over, the one named last changes fastest.
Arguments:
- features: bfloat16 [131072, 128], P(('row', 'col')), may hold values from -6 to 6
- weight: bfloat16 [128, 128], replicated, may hold values from -0.5 to 0.5
- layer_bias: float32 [128], replicated, may hold values from -3 to 3
- cotangent: bfloat16 [131072, 128], P(('col', 'row')), may hold values from -6 to 6
- tile_out: int32 [16, 8, 128], P('row', 'col'), may hold values from 0 to 63
- tile_in: int32 [16, 8, 128], P('row', 'col'), may hold values from 0 to 31
- tile_vals: bfloat16 [16, 8, 128, 256, 256], P('row', 'col'), may hold values from -0.09375 to 0.09375
- tile_count: int32 [16, 8], P('row', 'col'), may hold values from 1 to 128, as said below
Outputs:
- hidden_out: bfloat16 [131072, 128], P(('col', 'row'))
- feature_grad: bfloat16 [131072, 128], P(('row', 'col'))
- weight_grad: float32 [128, 128], replicated
- bias_grad: float32 [128], replicated
Inputs may be any that keep to these rules, and one draw needn't show every extreme that they name: `tile_count`: live slots of each grid block; some grid block has exactly 128 in every draw.
All inputs are finite; a program needn't handle non-finite values.
Results may differ from a plain program's by a relative error of at most 0.025.
Values may be sent and summed in bfloat16 or wider, within the bound.
No kernel may reach another device: no remote copies, remote signals or barrier semaphores. Data moves between devices by JAX's collectives and lax.ppermute only.
A program may use at most 192 MiB of HBM per device.

v0:
```python
import math

import jax
import jax.numpy as jnp
from jax import lax
from jax.sharding import PartitionSpec as P

gelu_coef = 0.7978845608
cube_coef = 0.044715


def gelu_tanh(inputs):
    inner = jnp.tanh(gelu_coef * (inputs + cube_coef * inputs * inputs * inputs))
    return 0.5 * inputs * (1.0 + inner)


def gelu_slope(inputs):
    inner = jnp.tanh(gelu_coef * (inputs + cube_coef * inputs * inputs * inputs))
    return 0.5 * (1.0 + inner) + 0.5 * inputs * (1.0 - inner * inner) * gelu_coef * (
        1.0 + 3.0 * cube_coef * inputs * inputs
    )


def tile_sums(products, targets, live_mask, target_tiles):
    masked = products * live_mask[:, None, None]
    summed = (
        jnp.zeros((target_tiles, products.shape[1], products.shape[2]), jnp.float32)
        .at[targets]
        .add(masked)
    )
    return summed.reshape(target_tiles * products.shape[1], products.shape[2])


def local(features, weight, layer_bias, cotangent, tile_out, tile_in, tile_vals, tile_count):
    tile_size = tile_vals.shape[-1]
    slot_count = tile_vals.shape[2]
    node_rows = features.shape[0]
    feat_count = features.shape[1]
    rows_axis = lax.axis_size("row")
    cols_axis = lax.axis_size("col")
    target_tiles = rows_axis * node_rows // tile_size
    source_tiles = cols_axis * node_rows // tile_size
    out_index = tile_out[0, 0]
    in_index = tile_in[0, 0]
    values = tile_vals[0, 0]
    live_mask = (jnp.arange(slot_count, dtype=jnp.int32) < tile_count[0, 0]).astype(jnp.float32)
    source_rows = lax.all_gather(features, "col", axis=0, tiled=True)
    picked = jnp.take(source_rows.reshape(source_tiles, tile_size, feat_count), in_index, axis=0)
    products = jnp.einsum("tab,tbf->taf", values, picked, preferred_element_type=jnp.float32)
    partial_value = tile_sums(products, out_index, live_mask, target_tiles).astype(jnp.bfloat16)
    own_agg = (
        lax.psum_scatter(partial_value, "row", scatter_dimension=0, tiled=True)
        .astype(jnp.float32)
        .astype(jnp.bfloat16)
    )
    preact = jnp.dot(own_agg, weight, preferred_element_type=jnp.float32) + layer_bias
    hidden_out = gelu_tanh(preact).astype(jnp.bfloat16)
    own_grad = (cotangent.astype(jnp.float32) * gelu_slope(preact)).astype(jnp.bfloat16)
    grad_local = jnp.dot(own_grad, weight.T, preferred_element_type=jnp.float32).astype(
        jnp.bfloat16
    )
    target_grad = lax.all_gather(grad_local, "row", axis=0, tiled=True)
    weight_local = lax.dot_general(
        own_agg, own_grad, (((0,), (0,)), ((), ())), preferred_element_type=jnp.float32
    )
    bias_local = jnp.sum(own_grad.astype(jnp.float32), axis=0)
    weight_total, bias_total = lax.psum((weight_local, bias_local), ("row", "col"))
    norm_scale = 1.0 / math.sqrt(node_rows * rows_axis * cols_axis)
    weight_grad = weight_total * norm_scale
    bias_grad = bias_total * norm_scale
    picked_grad = jnp.take(
        target_grad.reshape(target_tiles, tile_size, feat_count), out_index, axis=0
    )
    back_products = jnp.einsum(
        "tab,taf->tbf", values, picked_grad, preferred_element_type=jnp.float32
    )
    back_partial = tile_sums(back_products, in_index, live_mask, source_tiles).astype(jnp.bfloat16)
    feature_grad = (
        lax.psum_scatter(back_partial, "col", scatter_dimension=0, tiled=True)
        .astype(jnp.float32)
        .astype(jnp.bfloat16)
    )
    return (hidden_out, feature_grad, weight_grad, bias_grad)


def solution(mesh):
    in_specs = (
        P(("row", "col"), None),
        P(),
        P(),
        P(("col", "row"), None),
        P("row", "col", None),
        P("row", "col", None),
        P("row", "col", None, None, None),
        P("row", "col"),
    )
    out_specs = (P(("col", "row"), None), P(("row", "col"), None), P(), P())
    return jax.shard_map(local, mesh=mesh, in_specs=in_specs, out_specs=out_specs, check_vma=False)
```

profile of v0, /device:TPU:0, one launch (start us, length us, event | category | flops | bytes accessed | tf_op | source)
XLA Modules:
  0.0 495.7 jit_solution(11982166304795398902)
XLA Ops:
  7.2 0.0 copy-start
  7.2 0.0 all-gather.3.cloned.1.call-start
  7.2 0.7 all-gather.3.cloned.1.call-update
  7.9 0.0 reduce-scatter.3.cloned.1.call-start
  8.6 0.7 fusion.22
  9.3 0.7 fusion.21
  9.9 0.7 compare_convert_fusion
  10.6 53.9 %all-gather.3.cloned.1.call-done = bf16[8192,128]{1,0:T(8,128)(2,1)} async-done(((bf16[1024,128]{1,0:T(8,128)(2,1)}), bf16[8192,128]{1,0:T(8,128)(2,1)}) %all-gather.3.cloned.1.call-update) | async-done | bytes 2097168 | tf_op jit(solution)/shard_map/all_gather | solution.py:47
  64.5 8.1 %gather_fusion = bf16[128,256,128]{2,1,0:T(8,128)(2,1)} fusion(bf16[32,256,128]{2,1,0:T(8,128)(2,1)} %bitcast.37, s32[1024]{0:T(1024)S(1)} %pad_clamp_fusion.1), kind=kCustom, calls=%fused_computation | custom fusion | bytes 16777728 | tf_op jit(solution)/shard_map/jit(_take)/gather | solution.py:48
  72.6 17.5 %multiply_bitcast_fusion.1 = f32[128,256,128]{1,2,0:T(8,128)} fusion(bf16[1,1,128,256,256]{4,3,2,1,0:T(8,128)(2,1)} %param.14, f32[128]{0:T(128)S(1)} %get-tuple-element.7, bf16[128,256,128]{2,1,0:T(8,128)(2,1)} %gather_fusion, pred[128]{0:T(512)(128)(4,1)S(1)} %get-tuple-element.8), kind=kOutput, calls=%fused_computation.9 | convolution fusion | flops 2155872256 | bytes 41943680 | tf_op jit(solution)/shard_map/tab,tbf->taf/dot_general | solution.py:49
  90.2 17.4 %copy.15 = f32[128,256,128]{2,1,0:T(8,128)} copy(f32[128,256,128]{1,2,0:T(8,128)} %multiply_bitcast_fusion.1) | data formatting | bytes 33554432 | tf_op jit(solution)/shard_map/mul | solution.py:25
  107.6 4.2 broadcast_in_dim.29
  111.8 38.5 %scatter_fusion = f32[64,256,128]{2,1,0:T(8,128)} fusion(f32[64,256,128]{2,1,0:T(8,128)} %broadcast_in_dim.29, s32[128]{0:T(128)S(1)} %fusion.21, f32[128,256,128]{2,1,0:T(8,128)} %copy.15), kind=kCustom, calls=%fused_computation.2 | custom fusion | flops 4194304 | bytes 50332160 | tf_op jit(solution)/shard_map/scatter-add | solution.py:29
  150.3 0.0 copy-start.2
  150.3 0.0 copy-start.3
  150.3 0.0 copy-start.4
  150.3 6.1 %convert_element_type.39 = bf16[64,256,128]{2,1,0:T(8,128)(2,1)} convert(f32[64,256,128]{2,1,0:T(8,128)} %scatter_fusion) | non-fusion elementwise | flops 2097152 | bytes 12582912 | tf_op jit(solution)/shard_map/convert_element_type | solution.py:50
  156.4 0.0 reduce-scatter.3.cloned.1.call-update
  156.4 0.0 all-gather.5.cloned.1.call-start
  156.5 79.5 %reduce-scatter.3.cloned.1.call-done = bf16[1024,128]{1,0:T(8,128)(2,1)} async-done(((bf16[16384,128]{1,0:T(8,128)(2,1)}), bf16[1024,128]{1,0:T(8,128)(2,1)}) %reduce-scatter.3.cloned.1.call-update) | async-done | bytes 262160 | tf_op jit(solution)/shard_map/reduce_scatter | solution.py:52
  236.0 0.0 copy-done
  236.0 0.0 copy-done.2
  236.0 0.0 copy-done.3
  236.0 2.2 convert_reduce_fusion
  238.3 0.9 convolution_convert_fusion
  239.2 0.0 all-gather.5.cloned.1.call-update
  239.2 0.0 all-reduce.2.cloned.1.call-start
  239.3 0.0 copy-done.4
  239.3 1.9 fusion.26
  241.2 0.0 all-reduce.2.cloned.1.call-update
  241.2 0.2 reduce-scatter.5.cloned.1.call-start
  241.4 52.8 %all-gather.5.cloned.1.call-done = bf16[16384,128]{1,0:T(8,128)(2,1)} async-done(((bf16[1024,128]{1,0:T(8,128)(2,1)}), bf16[16384,128]{1,0:T(8,128)(2,1)}) %all-gather.5.cloned.1.call-update) | async-done | bytes 4194320 | tf_op jit(solution)/shard_map/all_gather | solution.py:62
  294.2 8.7 %gather_fusion.1 = bf16[128,256,128]{2,1,0:T(8,128)(2,1)} fusion(bf16[64,256,128]{2,1,0:T(8,128)(2,1)} %bitcast.38, s32[1024]{0:T(1024)S(1)} %pad_clamp_fusion), kind=kCustom, calls=%fused_computation.1 | custom fusion | bytes 16777728 | tf_op jit(solution)/shard_map/jit(_take)/gather | solution.py:71
  302.9 14.0 %multiply_bitcast_fusion = f32[128,256,128]{1,2,0:T(8,128)} fusion(bf16[1,1,128,256,256]{4,3,2,1,0:T(8,128)(2,1)} %param.14, bf16[128,256,128]{2,1,0:T(8,128)(2,1)} %gather_fusion.1, f32[128]{0:T(128)S(1)} %get-tuple-element.7, pred[128]{0:T(512)(128)(4,1)S(1)} %compare_and_fusion), kind=kOutput, calls=%fused_computation.8 | convolution fusion | flops 2155872256 | bytes 41943680 | tf_op jit(solution)/shard_map/tab,taf->tbf/dot_general | solution.py:74
  316.9 17.4 %copy.17 = f32[128,256,128]{2,1,0:T(8,128)} copy(f32[128,256,128]{1,2,0:T(8,128)} %multiply_bitcast_fusion) | data formatting | bytes 33554432 | tf_op jit(solution)/shard_map/mul | solution.py:25
  334.4 2.4 broadcast_in_dim.32
  336.8 0.0 copy-start.1
  336.8 38.0 %scatter_fusion.1 = f32[32,256,128]{2,1,0:T(8,128)} fusion(f32[32,256,128]{2,1,0:T(8,128)} %broadcast_in_dim.32, s32[128]{0:T(128)S(1)} %fusion.22, f32[128,256,128]{2,1,0:T(8,128)} %copy.17), kind=kCustom, calls=%fused_computation.3 | custom fusion | flops 4194304 | bytes 50332160 | tf_op jit(solution)/shard_map/scatter-add | solution.py:29
  374.8 3.9 convert_element_type.45
  378.7 0.0 reduce-scatter.5.cloned.1.call-update
  378.7 64.9 %psum.15 = f32[128]{0:T(128)S(1)} all-reduce(f32[128]{0:T(128)S(1)} %get-tuple-element.4), channel_id=1, replica_groups=mesh['row'=16,'col'=8] {'row','col'}, use_global_device_ids=true, to_apply=%region_6.7 | all-reduce | flops 128 | bytes 1024 | tf_op jit(solution)/shard_map/psum | solution.py:67
  443.7 0.5 broadcast_multiply_fusion.1
  444.2 0.0 all-reduce.2.cloned.1.call-done
  444.2 1.5 broadcast_multiply_fusion
  445.7 43.5 %reduce-scatter.5.cloned.1.call-done = bf16[1024,128]{1,0:T(8,128)(2,1)} async-done(((bf16[8192,128]{1,0:T(8,128)(2,1)}), bf16[1024,128]{1,0:T(8,128)(2,1)}) %reduce-scatter.5.cloned.1.call-update) | async-done | bytes 262160 | tf_op jit(solution)/shard_map/reduce_scatter | solution.py:79
  489.1 0.0 copy-done.1
  (3 shorter events, 0.0 us)
Async XLA Ops:
  7.2 228.9 %copy-start = (bf16[128,128]{1,0:T(8,128)(2,1)S(1)}, bf16[128,128]{1,0:T(8,128)(2,1)}, u32[]{:S(2)}) copy-start(bf16[128,128]{1,0:T(8,128)(2,1)} %param.9) | copy-start | bytes 98308
  7.2 57.3 %all-gather.3.cloned.1.call-start = ((), (), s32[]{:S(2)}) async-start(), calls=%async_computation.2 | async-start | bytes 2359296 | tf_op jit(solution)/shard_map/all_gather | solution.py:47
  7.9 228.1 %reduce-scatter.3.cloned.1.call-start = ((), (), s32[]{:S(2)}) async-start(), calls=%async_computation.3 | async-start | bytes 4456448 | tf_op jit(solution)/shard_map/reduce_scatter | solution.py:52
  150.3 85.7 %copy-start.2 = (bf16[1024,128]{1,0:T(8,128)(2,1)S(1)}, bf16[1024,128]{1,0:T(8,128)(2,1)}, u32[]{:S(2)}) copy-start(bf16[1024,128]{1,0:T(8,128)(2,1)} %param.11) | copy-start | bytes 786436
  150.3 85.7 %copy-start.3 = (f32[128]{0:T(128)S(1)}, f32[128]{0:T(128)}, u32[]{:S(2)}) copy-start(f32[128]{0:T(128)} %param.10) | copy-start | bytes 1540
  150.3 89.0 %copy-start.4 = (s32[1,1,128]{2,1,0:T(1,128)S(1)}, s32[1,1,128]{2,1,0:T(1,128)}, u32[]{:S(2)}) copy-start(s32[1,1,128]{2,1,0:T(1,128)} %param.12) | copy-start | bytes 1540
  156.4 137.7 %all-gather.5.cloned.1.call-start = ((), (), s32[]{:S(2)}) async-start(), calls=%async_computation.4 | async-start | bytes 4456448 | tf_op jit(solution)/shard_map/all_gather | solution.py:62
  239.2 205.0 %all-reduce.2.cloned.1.call-start = ((), (), s32[]{:S(2)}) async-start(), calls=%async_computation.6 | async-start | bytes 131072 | tf_op jit(solution)/shard_map/psum | solution.py:67
  241.2 248.0 %reduce-scatter.5.cloned.1.call-start = ((), (), s32[]{:S(2)}) async-start(), calls=%async_computation.5 | async-start | bytes 2359296 | tf_op jit(solution)/shard_map/reduce_scatter | solution.py:79
  336.8 152.4 %copy-start.1 = (bf16[128,128]{1,0:T(8,128)(2,1)S(1)}, bf16[128,128]{1,0:T(8,128)(2,1)}, u32[]{:S(2)}) copy-start(bf16[128,128]{1,0:T(8,128)(2,1)} %param.9) | copy-start | bytes 98308
Sparse Core Ops, SparseCore 0:
  9.7 54.7 all-gather.2
  156.5 79.4 reduce-scatter.2
  239.3 54.7 all-gather.4
  300.1 134.3 all-reduce.1
  437.2 51.8 reduce-scatter.4
where the time goes:
time: 497 us; the launch traced here: 496 us
  waiting for transfers between devices  230 us (46%)
  other arithmetic  90.5 us (18%)
  blocking collectives  64.9 us (13%)
  local copies, waits for them, and re-layouts  58.4 us (12%)
  matrix products  36.6 us (7%)
  between operations  14.5 us (3%)
    reduce_scatter x1, waiting for transfers between devices, local(): lax.psum_scatter(partial_value, 'row', scatter_dimension=0, tiled=True)  79.5 us
    scatter-add x2, other arithmetic, tile_sums(): summed = jnp.zeros((target_tiles, products.shape[1], products.shape[2]),...  76.5 us
    psum x1, blocking collectives, local(): lax.psum((weight_local, bias_local), ('row', 'col'))  64.9 us
    all_gather x1, waiting for transfers between devices, local(): source_rows = lax.all_gather(features, 'col', axis=0, tiled=True)  53.9 us
    all_gather x1, waiting for transfers between devices, local(): target_grad = lax.all_gather(grad_local, 'row', axis=0, tiled=True)  52.8 us
    reduce_scatter x1, waiting for transfers between devices, local(): lax.psum_scatter(back_partial, 'col', scatter_dimension=0, tiled=True)  43.5 us
    mul x2, local copies, waits for them, and re-layouts, tile_sums(): masked = products * live_mask[:, None, None]  34.8 us
    dot_general x1, matrix products, local(): jnp.einsum('tab,tbf->taf', values, picked, preferred_element_type=jnp.flo...  17.5 us
  transfers between devices with their start and end apart: 5, of which 4 were waited for; matrix products, arithmetic and copies ran while one was open for 18% of the time, Pallas kernels for 0%

commit v1 on v0

v1 whole, which is shorter than its diff:
```python
import functools
import math

import jax
import jax.numpy as jnp
from jax import lax
from jax.experimental import pallas as pl
from jax.experimental.pallas import tpu as pltpu
from jax.sharding import PartitionSpec as P

gelu_coef = 0.7978845608
cube_coef = 0.044715
TILE = 256
FEAT = 128
SLOTS = 128
NPEER = 8
LIST = 160
UNROLL = 4
DEPTH = 16
EXTRA = 32
FWD_DUMMY = 32
BWD_DUMMY = 16
f32, bf16 = jnp.float32, jnp.bfloat16
VMEM_LIMIT = 48 * 2**20


def params():
    return pltpu.CompilerParams(vmem_limit_bytes=VMEM_LIMIT)


def vmem():
    return pl.BlockSpec(memory_space=pltpu.VMEM)


def smem():
    return pl.BlockSpec(memory_space=pltpu.SMEM)


def hbm():
    return pl.BlockSpec(memory_space=pl.ANY)


def prep_kernel(where_ref, out_ref, in_ref, count_ref, lists_ref, sizes_ref):
    core, z, y = where_ref[0], where_ref[1], where_ref[2]

    def clear(i, carry):
        lists_ref[i] = FWD_DUMMY << 16
        lists_ref[LIST + i] = FWD_DUMMY << 16
        lists_ref[2 * LIST + i] = BWD_DUMMY << 16
        lists_ref[3 * LIST + i] = BWD_DUMMY << 16
        return carry

    lax.fori_loop(0, LIST, clear, 0)

    def place(k, carry):
        f0, f1, b0, b1 = carry
        t = out_ref[k]
        s = in_ref[k]
        dev_t = t >> 2
        rel = jnp.bitwise_xor(dev_t & 1, core)
        j_t = dev_t >> 1
        half_t, sub_t = (t >> 1) & 1, t & 1
        dev_s = s >> 2
        half_s, sub_s = (s >> 1) & 1, s & 1
        dz = (z - (dev_s >> 1)) & 3
        dy = (y - (dev_s & 1)) & 1
        src_f = (dz * 2 + dy) * 4 + (s & 3)
        dst_f = rel * 16 + j_t * 2 + sub_t
        src_b = ((half_t * 2 + rel) * NPEER + j_t) * 2 + sub_t
        dst_b = dev_s * 2 + sub_s
        at_f = jnp.where(half_t == 0, f0, LIST + f1)
        at_b = jnp.where(half_s == 0, 2 * LIST + b0, 3 * LIST + b1)
        lists_ref[at_f] = k | (src_f << 8) | (dst_f << 16)
        lists_ref[at_b] = k | (src_b << 8) | (dst_b << 16)
        return (
            f0 + 1 - half_t,
            f1 + half_t,
            b0 + 1 - half_s,
            b1 + half_s,
        )

    zero = jnp.int32(0)
    sizes = lax.fori_loop(0, count_ref[0], place, (zero, zero, zero, zero))
    for i in range(4):
        sizes_ref[i] = sizes[i]


def prep(where, out_index, in_index, count):
    return pl.pallas_call(
        prep_kernel,
        out_shape=(
            jax.ShapeDtypeStruct((4 * LIST,), jnp.int32),
            jax.ShapeDtypeStruct((4,), jnp.int32),
        ),
        in_specs=[smem()] * 4,
        out_specs=(smem(), smem()),
        name="slot_lists",
    )(where, out_index, in_index, count)


def tile_loop(which, lists_ref, sizes_ref, vals, buf, sems, ready, step):
    base = which * LIST
    groups = (sizes_ref[which] + (UNROLL - 1)) // UNROLL
    ahead = DEPTH // UNROLL

    def copy(g, u):
        slot = lists_ref[base + g * UNROLL + u] & 255
        at = lax.rem(g, ahead) * UNROLL + u
        return pltpu.make_async_copy(vals.at[slot], buf.at[at], sems.at[at])

    for g in range(ahead):

        @pl.when(g < groups)
        def _():
            for u in range(UNROLL):
                copy(g, u).start()

    ready()

    def body(g, carry):
        for u in range(UNROLL):
            copy(g, u).wait()
        todo = []
        for u in range(UNROLL):
            entry = lists_ref[base + g * UNROLL + u]
            at = lax.rem(g, ahead) * UNROLL + u
            todo.append(((entry >> 16), step((entry >> 8) & 255, at)))
        yield_to(todo)

        @pl.when(g + ahead < groups)
        def _():
            for u in range(UNROLL):
                copy(g + ahead, u).start()

        return carry

    acc = step.acc

    def yield_to(todo):
        for to, product in todo:
            acc[to] += product

    lax.fori_loop(0, groups, body, 0)


class Step:
    def __init__(self, acc, product):
        self.acc = acc
        self.product = product

    def __call__(self, source, at):
        return self.product(source, at)


def forward_kernel(half, lists_ref, sizes_ref, vals, *rest):
    blocks = rest[:NPEER]
    mine_ref, other_ref, x, buf, acc, sems, xsems = rest[NPEER:]

    def block_copy(k):
        return pltpu.make_async_copy(blocks[k], x.at[pl.ds(k * 4 * TILE, 4 * TILE)], xsems.at[k])

    def ready():
        for k in range(NPEER):
            block_copy(k).start()

        def clear(i, carry):
            acc[i] = jnp.zeros((TILE, FEAT), f32)
            return carry

        lax.fori_loop(0, FWD_DUMMY + 1, clear, 0)
        for k in range(NPEER):
            block_copy(k).wait()

    def product(source, at):
        rows = x[pl.ds(pl.multiple_of(source * TILE, TILE), TILE), :]
        return jnp.dot(buf[at], rows, preferred_element_type=f32)

    tile_loop(half, lists_ref, sizes_ref, vals, buf, sems, ready, Step(acc, product))

    def put(i, carry):
        peer, sub = i // 2, i % 2
        rows = pl.ds(pl.multiple_of(sub * TILE, TILE), TILE)
        mine_ref[peer, rows, :] = acc[i].astype(bf16)
        other_ref[peer, rows, :] = acc[16 + i].astype(bf16)
        return carry

    lax.fori_loop(0, 16, put, 0)


def forward(half, lists, sizes, values, blocks):
    shape = jax.ShapeDtypeStruct((NPEER, 2 * TILE, FEAT), bf16)
    return pl.pallas_call(
        functools.partial(forward_kernel, half),
        out_shape=(shape, shape),
        in_specs=[smem(), smem()] + [hbm()] * (1 + NPEER),
        out_specs=(vmem(), vmem()),
        scratch_shapes=[
            pltpu.VMEM((NPEER * 4 * TILE, FEAT), bf16),
            pltpu.VMEM((DEPTH, TILE, TILE), bf16),
            pltpu.VMEM((FWD_DUMMY + 1, TILE, FEAT), f32),
            pltpu.SemaphoreType.DMA((DEPTH,)),
            pltpu.SemaphoreType.DMA((NPEER,)),
        ],
        compiler_params=params(),
        cost_estimate=pl.CostEstimate(
            flops=2 * 64 * TILE * TILE * FEAT, bytes_accessed=14 * 2**20, transcendentals=0
        ),
        name="forward_tiles",
    )(lists, sizes, values, *blocks)


def split_lanes(value):
    high = value.astype(bf16)
    low = (value - high.astype(f32)).astype(bf16)
    return jnp.concatenate([high, low], axis=1)


def backward_kernel(half, lists_ref, sizes_ref, vals, *rest):
    parts = rest[:4]
    out_ref, g, buf, acc, sems, gsems = rest[4:10]
    per = 2 * NPEER

    def part_copy(p, peer):
        return pltpu.make_async_copy(
            parts[p].at[peer, pl.ds(0, 2 * FEAT)],
            g.at[pl.ds((p * per + peer * 2) * FEAT, 2 * FEAT)],
            gsems.at[p],
        )

    if half == 0:
        extra, esem = rest[10:12]

        def extra_copy(p):
            return pltpu.make_async_copy(
                parts[2 + p].at[:, pl.ds(2 * FEAT, EXTRA)], extra.at[p], esem.at[p]
            )

    def ready():
        for p in range(4):
            for peer in range(NPEER):
                part_copy(p, peer).start()
        if half == 0:
            extra_copy(0).start()
            extra_copy(1).start()

        def clear(i, carry):
            acc[i] = jnp.zeros((FEAT, TILE), f32)
            return carry

        lax.fori_loop(0, BWD_DUMMY + 1, clear, 0)
        for p in range(4):
            pltpu.make_async_copy(
                g.at[pl.ds(p * per * FEAT, per * FEAT)],
                g.at[pl.ds(p * per * FEAT, per * FEAT)],
                gsems.at[p],
            ).wait()

    def product(source, at):
        rows = g[pl.ds(pl.multiple_of(source * FEAT, FEAT), FEAT), :]
        return jnp.dot(rows, buf[at], preferred_element_type=f32)

    tile_loop(2 + half, lists_ref, sizes_ref, vals, buf, sems, ready, Step(acc, product))

    def put(i, carry):
        peer, sub = i // 2, i % 2
        rows = pl.ds(pl.multiple_of(sub * FEAT, FEAT), FEAT)
        out_ref[peer, rows, :] = acc[i].astype(bf16)
        return carry

    lax.fori_loop(0, 16, put, 0)
    if half == 0:
        extra_copy(0).wait()
        extra_copy(1).wait()
        sums = []
        for p in range(2):
            total = jnp.zeros((EXTRA, FEAT), f32)
            for peer in range(NPEER):
                pair = extra[p, peer].astype(f32)
                total += pair[:, :FEAT] + pair[:, FEAT:]
            sums.append(total)
        packed = split_lanes(sums[0] + sums[1])
        for peer in range(NPEER):
            out_ref[peer, pl.ds(2 * FEAT, EXTRA), :] = packed


def backward(half, lists, sizes, values, parts):
    rows = 2 * FEAT + (EXTRA if half == 0 else 0)
    scratch = [
        pltpu.VMEM((4 * 2 * NPEER * FEAT, TILE), bf16),
        pltpu.VMEM((DEPTH, TILE, TILE), bf16),
        pltpu.VMEM((BWD_DUMMY + 1, FEAT, TILE), f32),
        pltpu.SemaphoreType.DMA((DEPTH,)),
        pltpu.SemaphoreType.DMA((4,)),
    ]
    if half == 0:
        scratch += [
            pltpu.VMEM((2, NPEER, EXTRA, TILE), bf16),
            pltpu.SemaphoreType.DMA((2,)),
        ]
    return pl.pallas_call(
        functools.partial(backward_kernel, half),
        out_shape=jax.ShapeDtypeStruct((NPEER, rows, TILE), bf16),
        in_specs=[smem(), smem()] + [hbm()] * 5,
        out_specs=vmem(),
        scratch_shapes=scratch,
        compiler_params=params(),
        cost_estimate=pl.CostEstimate(
            flops=2 * 64 * TILE * TILE * FEAT, bytes_accessed=14 * 2**20, transcendentals=0
        ),
        name="backward_tiles",
    )(lists, sizes, values, *parts)


def dense_kernel(half, recv_ref, weight_ref, bias_ref, cot_ref, *rest):
    if half == 0:
        hidden_ref, grad_ref, wsum_ref = rest
    else:
        before_ref, unused, hidden_ref, grad_ref = rest
    total = recv_ref[0].astype(f32)
    for peer in range(1, NPEER):
        total += recv_ref[peer].astype(f32)
    agg = total.astype(bf16)
    weight = weight_ref[...]
    v = jnp.dot(agg, weight, preferred_element_type=f32) + bias_ref[...]
    s = jnp.tanh(gelu_coef * (v + cube_coef * v * v * v))
    hidden_ref[...] = (0.5 * v * (1.0 + s)).astype(bf16)
    slope = 0.5 * (1.0 + s) + 0.5 * v * (1.0 - s * s) * gelu_coef * (1.0 + 3.0 * cube_coef * v * v)
    grad = (cot_ref[...].astype(f32) * slope).astype(bf16)
    wsum = lax.dot_general(agg, grad, (((0,), (0,)), ((), ())), preferred_element_type=f32)
    bsum = jnp.dot(jnp.ones((16, 2 * TILE), bf16), grad, preferred_element_type=f32)
    back = lax.dot_general(weight, grad, (((1,), (1,)), ((), ())), preferred_element_type=f32)
    back = back.astype(bf16)
    for peer in range(NPEER):
        for sub in range(2):
            grad_ref[peer, pl.ds(sub * FEAT, FEAT), :] = back[:, sub * TILE : (sub + 1) * TILE]
    if half == 0:
        wsum_ref[pl.ds(0, FEAT), :] = wsum
        wsum_ref[pl.ds(FEAT, 16), :] = bsum
    else:
        wpack = split_lanes(wsum + before_ref[pl.ds(0, FEAT), :])
        bpack = split_lanes(bsum + before_ref[pl.ds(FEAT, 16), :])
        for peer in range(NPEER):
            grad_ref[peer, pl.ds(2 * FEAT, 16), :] = wpack[peer * 16 : peer * 16 + 16]
            grad_ref[peer, pl.ds(2 * FEAT + 16, 16), :] = bpack


def dense(half, recv, weight, bias, cotangent, before=None, hidden=None):
    rows = 2 * FEAT + (EXTRA if half == 1 else 0)
    hidden_shape = jax.ShapeDtypeStruct((4 * TILE, FEAT), bf16)
    half_rows = pl.BlockSpec((2 * TILE, FEAT), lambda i: (half, 0))
    grad_shape = jax.ShapeDtypeStruct((NPEER, rows, TILE), bf16)
    whole3 = pl.BlockSpec((NPEER, rows, TILE), lambda i: (0, 0, 0))
    wsum_shape = jax.ShapeDtypeStruct((FEAT + 16, FEAT), f32)

    def whole(*shape):
        return pl.BlockSpec(shape, lambda i: (0,) * len(shape))

    in_specs = [whole(NPEER, 2 * TILE, FEAT), whole(FEAT, FEAT), whole(1, FEAT), half_rows]
    operands = [recv, weight, bias, cotangent]
    aliases = {}
    if half == 0:
        out_shape = (hidden_shape, grad_shape, wsum_shape)
        out_specs = (half_rows, whole3, whole(FEAT + 16, FEAT))
    else:
        out_shape = (hidden_shape, grad_shape)
        out_specs = (half_rows, whole3)
        in_specs += [whole(FEAT + 16, FEAT), hbm()]
        operands += [before, hidden]
        aliases = {5: 0}
    return pl.pallas_call(
        functools.partial(dense_kernel, half),
        grid=(1,),
        out_shape=out_shape,
        in_specs=in_specs,
        out_specs=out_specs,
        input_output_aliases=aliases,
        compiler_params=params(),
        cost_estimate=pl.CostEstimate(
            flops=6 * 512 * FEAT * FEAT, bytes_accessed=3 * 2**20, transcendentals=512 * FEAT
        ),
        name="dense_layer",
    )(*operands)


def last_kernel(half, scale, recv_ref, *rest):
    if half == 0:
        grad_ref, slice_ref = rest
    else:
        unused, grad_ref = rest
    for sub in range(2):
        rows = pl.ds(sub * FEAT, FEAT)
        total = recv_ref[0, rows, :].astype(f32)
        for peer in range(1, NPEER):
            total += recv_ref[peer, rows, :].astype(f32)
        grad_ref[pl.ds(sub * TILE, TILE), :] = total.T.astype(bf16)
    if half == 0:
        total = jnp.zeros((EXTRA, FEAT), f32)
        for peer in range(NPEER):
            pair = recv_ref[peer, pl.ds(2 * FEAT, EXTRA), :].astype(f32)
            total += pair[:, :FEAT] + pair[:, FEAT:]
        total = total * scale
        for peer in range(NPEER):
            slice_ref[peer] = total


def last(half, scale, recv, grad=None):
    rows = recv.shape[1]
    half_rows = pl.BlockSpec((2 * TILE, FEAT), lambda i: (half, 0))
    grad_shape = jax.ShapeDtypeStruct((4 * TILE, FEAT), bf16)
    in_specs = [pl.BlockSpec((NPEER, rows, TILE), lambda i: (0, 0, 0))]
    operands = [recv]
    aliases = {}
    if half == 0:
        out_shape = (grad_shape, jax.ShapeDtypeStruct((NPEER, EXTRA, FEAT), f32))
        out_specs = (half_rows, pl.BlockSpec((NPEER, EXTRA, FEAT), lambda i: (0, 0, 0)))
    else:
        out_shape = grad_shape
        out_specs = half_rows
        in_specs += [hbm()]
        operands += [grad]
        aliases = {1: 0}
    return pl.pallas_call(
        functools.partial(last_kernel, half, scale),
        grid=(1,),
        out_shape=out_shape,
        in_specs=in_specs,
        out_specs=out_specs,
        input_output_aliases=aliases,
        compiler_params=params(),
        cost_estimate=pl.CostEstimate(flops=2**20, bytes_accessed=2 * 2**20, transcendentals=0),
        name="last_sum",
    )(*operands)


SAME_CORE = [[2 * j + core for j in range(NPEER)] for core in range(2)]
OTHER_CORE = [(r, r ^ 1) for r in range(16)]


def to_other_core(value):
    return lax.ppermute(value, "row", OTHER_CORE)


def row_exchange(value):
    return lax.all_to_all(value, "row", 0, 0, axis_index_groups=SAME_CORE)


def col_exchange(value):
    return lax.all_to_all(value, "col", 0, 0)


def col_shift(value, dz, dy):
    pairs = []
    for c in range(8):
        z, y = c // 2, c % 2
        pairs.append((c, ((z + dz) % 4) * 2 + (y + dy) % 2))
    return lax.ppermute(value, "col", pairs)


def local(features, weight, layer_bias, cotangent, tile_out, tile_in, tile_vals, tile_count):
    values = tile_vals[0, 0]
    row, col = lax.axis_index("row"), lax.axis_index("col")
    where = jnp.stack([row % 2, col // 2, col % 2]).astype(jnp.int32)
    lists, sizes = prep(where, tile_out[0, 0], tile_in[0, 0], tile_count[0])
    bias = layer_bias.reshape(1, FEAT)

    blocks = [features]
    for k in range(1, NPEER):
        blocks.append(col_shift(features, k // 2, k % 2))

    received = []
    for half in range(2):
        mine, other = forward(half, lists, sizes, values, blocks)
        both = mine + to_other_core(other)
        received.append(row_exchange(both))

    hidden, grad0, wsum = dense(0, received[0], weight, bias, cotangent)
    grads0 = row_exchange(grad0)
    hidden, grad1 = dense(1, received[1], weight, bias, cotangent, wsum, hidden)
    grads1 = row_exchange(grad1)
    parts = [grads0, to_other_core(grads0), grads1, to_other_core(grads1)]

    back0 = col_exchange(backward(0, lists, sizes, values, parts))
    back1 = col_exchange(backward(1, lists, sizes, values, parts))
    scale = 1.0 / math.sqrt(4 * TILE * 128)
    feature_grad, wslice = last(0, scale, back0)
    slices = row_exchange(wslice)
    feature_grad = last(1, scale, back1, feature_grad)
    weight_grad = slices[:, :16].reshape(FEAT, FEAT)
    bias_grad = slices[0, 16]
    return (hidden, feature_grad, weight_grad, bias_grad)


def solution(mesh):
    in_specs = (
        P(("row", "col"), None),
        P(),
        P(),
        P(("col", "row"), None),
        P("row", "col", None),
        P("row", "col", None),
        P("row", "col", None, None, None),
        P("row", "col"),
    )
    out_specs = (P(("col", "row"), None), P(("row", "col"), None), P(), P())
    return jax.shard_map(local, mesh=mesh, in_specs=in_specs, out_specs=out_specs, check_vma=False)
```

time: 497 us -> 209 us (0.42)
  waiting for transfers between devices: 230 us -> 93 us
  other arithmetic: 90.5 us -> 4.34 us
  local copies, waits for them, and re-layouts: 58.4 us -> 8.95 us
  starting transfers between devices: 0.38 us -> 46.4 us
  blocking collectives: 64.9 us -> 21.9 us
  matrix products: 36.6 us -> 0 us
  Pallas kernels: 0 us -> 31.7 us
  between operations: 14.5 us -> 1.49 us
    reduce_scatter x2 -> x0, waiting for transfers between devices: 123 us -> none  [the longest x1 79.5 us: local(): lax.psum_scatter(partial_value, 'row', scatter_dimension=0, tiled=True)]
    all_gather x2 -> x0, waiting for transfers between devices: 107 us -> none  [the longest x1 53.9 us: local(): source_rows = lax.all_gather(features, 'col', axis=0, tiled=True)]
    scatter-add x2 -> x0, other arithmetic: 76.5 us -> none  [tile_sums(): summed = jnp.zeros((target_tiles, products.shape[1], products.shape[2]),...]
    all_to_all x0 -> x6, waiting for transfers between devices: none -> 71.3 us  [the longest x4 50 us: row_exchange(): return lax.all_to_all(value, 'row', 0, 0, axis_index_groups=SAME_CORE)]
    psum x1 -> x0, blocking collectives: 64.9 us -> none  [local(): lax.psum((weight_local, bias_local), ('row', 'col'))]
    dot_general x5 -> x0, matrix products: 36.6 us -> none  [the longest x1 17.5 us: local(): jnp.einsum('tab,tbf->taf', values, picked, preferred_element_type=jnp.flo...]
    mul x2 -> x0, local copies, waits for them, and re-layouts: 34.8 us -> none  [tile_sums(): masked = products * live_mask[:, None, None]]
    all_to_all x0 -> x6, starting transfers between devices: none -> 33.3 us  [the longest x4 20.3 us: row_exchange(): return lax.all_to_all(value, 'row', 0, 0, axis_index_groups=SAME_CORE)]
  transfers between devices with their start and end apart: 5 -> 17, of which waited for: 4 -> 10; matrix products, arithmetic and copies ran while one was open for 18% -> 2% of each run, Pallas kernels for 0% -> 9%
where the time goes in v1:
time: 209 us; the launch traced here: 208 us
  waiting for transfers between devices  93 us (44%)
  starting transfers between devices  46.4 us (22%)
  Pallas kernels  31.7 us (15%)
  blocking collectives  21.9 us (10%)
  local copies, waits for them, and re-layouts  8.95 us (4%)
  other arithmetic  4.34 us (2%)
    all_to_all x4, waiting for transfers between devices, row_exchange(): return lax.all_to_all(value, 'row', 0, 0, axis_index_groups=SAME_CORE)  50 us
    all_to_all x1, blocking collectives, row_exchange(): return lax.all_to_all(value, 'row', 0, 0, axis_index_groups=SAME_CORE)  21.9 us
    all_to_all x2, waiting for transfers between devices, col_exchange(): return lax.all_to_all(value, 'col', 0, 0)  21.3 us
    all_to_all x4, starting transfers between devices, row_exchange(): return lax.all_to_all(value, 'row', 0, 0, axis_index_groups=SAME_CORE)  20.3 us
    ppermute x7, waiting for transfers between devices, col_shift(): return lax.ppermute(value, 'col', pairs)  19.1 us
    pallas_call x2, Pallas kernels, backward(): pl.pallas_call(functools.partial(backward_kernel, half), out_shape=jax.Sh...  15.7 us
    all_to_all x2, starting transfers between devices, col_exchange(): return lax.all_to_all(value, 'col', 0, 0)  13 us
    ppermute x7, starting transfers between devices, col_shift(): return lax.ppermute(value, 'col', pairs)  12.4 us
  transfers between devices with their start and end apart: 17, of which 10 were waited for; matrix products, arithmetic and copies ran while one was open for 2% of the time, Pallas kernels for 9%

profile of v1, /device:TPU:0, one launch (start us, length us, event | category | flops | bytes accessed | tf_op | source)
XLA Modules:
  0.0 207.8 jit_solution(4460814067160588172)
XLA Ops:
  0.6 5.2 %collective-permute-start.6 = (bf16[1024,128]{1,0:T(8,128)(2,1)}, bf16[1024,128]{1,0:T(8,128)(2,1)S(1)}, u32[]{:S(2)}, u32[]{:S(2)}) collective-permute-start(bf16[1024,128]{1,0:T(8,128)(2,1)} %rest_0_.3), channel_id=1, source_target_pairs={{0,7},{1,6},{2,1},{3,0},{4,3},{5,2},{6,5},{7,4},{8,15},{9,14},{10,... | collective-permute-start | bytes 786440 | tf_op jit(solution)/shard_map/ppermute | solution.py:456
  5.8 0.4 collective-permute-start.5
  6.2 0.0 collective-permute-start.4
  6.2 3.4 %collective-permute-start.3 = (bf16[1024,128]{1,0:T(8,128)(2,1)}, bf16[1024,128]{1,0:T(8,128)(2,1)S(1)}, u32[]{:S(2)}, u32[]{:S(2)}) collective-permute-start(bf16[1024,128]{1,0:T(8,128)(2,1)} %rest_0_.3), channel_id=1, source_target_pairs={{0,4},{1,5},{2,6},{3,7},{4,0},{5,1},{6,2},{7,3},{8,12},{9,13},{10,... | collective-permute-start | bytes 786440 | tf_op jit(solution)/shard_map/ppermute | solution.py:456
  9.7 2.6 %collective-permute-start.2 = (bf16[1024,128]{1,0:T(8,128)(2,1)}, bf16[1024,128]{1,0:T(8,128)(2,1)S(1)}, u32[]{:S(2)}, u32[]{:S(2)}) collective-permute-start(bf16[1024,128]{1,0:T(8,128)(2,1)} %rest_0_.3), channel_id=1, source_target_pairs={{0,3},{1,2},{2,5},{3,4},{4,7},{5,6},{6,1},{7,0},{8,11},{9,10},{10,... | collective-permute-start | bytes 786440 | tf_op jit(solution)/shard_map/ppermute | solution.py:456
  12.3 1.8 collective-permute-done.6.rest_7_
  14.1 0.0 collective-permute-start.1
  14.1 14.4 %collective-permute-done.5.rest_6_ = bf16[1024,128]{1,0:T(8,128)(2,1)S(1)} collective-permute-done((bf16[1024,128]{1,0:T(8,128)(2,1)}, bf16[1024,128]{1,0:T(8,128)(2,1)S(1)}, u32[]{:S(2)}, u32[]{:S(2)}) %collective-permute-start.5) | collective-permute-done | bytes 262176 | tf_op jit(solution)/shard_map/ppermute | solution.py:456
  28.5 0.8 collective-permute-start
  29.9 0.6 pad_add_fusion.where_ref
  30.5 3.5 %slot_lists.1 = (s32[640]{0:T(1024)}, s32[4]{0:T(128)}) custom-call(s32[3]{0:T(128)} %pad_add_fusion.where_ref, s32[128]{0:T(128)} %bitcast.19, s32[128]{0:T(128)} %bitcast.20, s32[1]{0:T(128)} %bitcast.11.count_ref), custom_call_target="tpu_custom_call" | custom-call | tf_op jit(solution)/shard_map/slot_lists/pallas_call | solution.py:89
  33.9 0.0 collective-permute-done.4.rest_5_
  33.9 0.0 collective-permute-done.3.rest_4_
  33.9 0.0 collective-permute-done.2.rest_3_
  34.0 0.0 collective-permute-done.1.rest_2_
  34.0 2.9 %collective-permute-done.rest_1_ = bf16[1024,128]{1,0:T(8,128)(2,1)S(1)} collective-permute-done((bf16[1024,128]{1,0:T(8,128)(2,1)}, bf16[1024,128]{1,0:T(8,128)(2,1)S(1)}, u32[]{:S(2)}, u32[]{:S(2)}) %collective-permute-start) | collective-permute-done | bytes 262176 | tf_op jit(solution)/shard_map/ppermute | solution.py:456
  36.9 0.9 copy-done.6
  37.8 0.7 copy-done.9
  38.5 0.7 copy-done.11
  39.2 3.8 %forward_tiles.3 = (bf16[8,512,128]{2,1,0:T(8,128)(2,1)S(1)}, bf16[8,512,128]{2,1,0:T(8,128)(2,1)S(1)}) custom-call(s32[640]{0:T(1024)S(1)} %copy-done.9, s32[4]{0:T(128)S(1)} %copy-done.11, bf16[128,256,256]{2,1,0:T(8,128)(2,1)} %bitcast.14, bf16[1024,128]{1,0:T(8,128)(2,1)S(1)} %copy-done.6, bf16[1024,128]{1,0:T(8,128)(2,1)S(1)} %collective-permute-done.rest_1_, ...), custom_call_target="tpu_custom_call" | custom-call | flops 1073741824 | bytes 14680064 | tf_op jit(solution)/shard_map/forward_tiles/pallas_call | solution.py:192
  43.0 0.1 collective-permute-start.8
  43.1 4.4 %forward_tiles.2 = (bf16[8,512,128]{2,1,0:T(8,128)(2,1)S(1)}, bf16[8,512,128]{2,1,0:T(8,128)(2,1)}) custom-call(s32[640]{0:T(1024)S(1)} %copy-done.9, s32[4]{0:T(128)S(1)} %copy-done.11, bf16[128,256,256]{2,1,0:T(8,128)(2,1)} %bitcast.15, bf16[1024,128]{1,0:T(8,128)(2,1)S(1)} %copy-done.6, bf16[1024,128]{1,0:T(8,128)(2,1)S(1)} %collective-permute-done.rest_1_, ...), custom_call_target="tpu_custom_call" | custom-call | flops 1073741824 | bytes 14680064 | tf_op jit(solution)/shard_map/forward_tiles/pallas_call | solution.py:192
  47.5 0.6 collective-permute-start.7
  48.1 0.0 collective-permute-done.8
  48.1 1.3 add.17
  49.4 9.4 %all-to-all-start.1 = ((bf16[8,512,128]{2,1,0:T(8,128)(2,1)}), bf16[8,512,128]{2,1,0:T(8,128)(2,1)S(1)}, u32[]{:S(2)}, u32[]{:S(2)}) async-start(bf16[8,512,128]{2,1,0:T(8,128)(2,1)} %add.17), calls=%async_computation.1 | async-start | bytes 2097152 | tf_op jit(solution)/shard_map/all_to_all | solution.py:444
  58.8 0.0 collective-permute-done.7
  58.8 2.5 %add.16 = bf16[8,512,128]{2,1,0:T(8,128)(2,1)} add(bf16[8,512,128]{2,1,0:T(8,128)(2,1)S(1)} %get-tuple-element.19, bf16[8,512,128]{2,1,0:T(8,128)(2,1)} %collective-permute-done.7) | non-fusion elementwise | flops 524288 | bytes 3145728 | tf_op jit(solution)/shard_map/add | solution.py:473
  61.2 14.9 %all-to-all-done.1.recv_ref = bf16[8,512,128]{2,1,0:T(8,128)(2,1)S(1)} async-done(((bf16[8,512,128]{2,1,0:T(8,128)(2,1)}), bf16[8,512,128]{2,1,0:T(8,128)(2,1)S(1)}, u32[]{:S(2)}, u32[]{:S(2)}) %all-to-all-start.1) | async-done | bytes 1048608 | tf_op jit(solution)/shard_map/all_to_all | solution.py:444
  76.1 3.6 %all-to-all-start = ((bf16[8,512,128]{2,1,0:T(8,128)(2,1)}), bf16[8,512,128]{2,1,0:T(8,128)(2,1)S(1)}, u32[]{:S(2)}, u32[]{:S(2)}) async-start(bf16[8,512,128]{2,1,0:T(8,128)(2,1)} %add.16), calls=%async_computation | async-start | bytes 2097152 | tf_op jit(solution)/shard_map/all_to_all | solution.py:444
  79.7 0.0 copy-done.7
  79.7 0.0 copy-done.8
  79.7 0.0 copy-done.13
  79.7 1.6 dense_layer.2
  81.3 14.0 %all-to-all-done.recv_ref = bf16[8,512,128]{2,1,0:T(8,128)(2,1)S(1)} async-done(((bf16[8,512,128]{2,1,0:T(8,128)(2,1)}), bf16[8,512,128]{2,1,0:T(8,128)(2,1)S(1)}, u32[]{:S(2)}, u32[]{:S(2)}) %all-to-all-start) | async-done | bytes 1048608 | tf_op jit(solution)/shard_map/all_to_all | solution.py:444
  95.3 1.0 dense_layer.3
  96.3 21.9 %all_to_all.35.rest_2_ = bf16[8,288,256]{2,1,0:T(8,128)(2,1)S(1)} all-to-all(bf16[8,288,256]{2,1,0:T(8,128)(2,1)S(1)} %get-tuple-element.27), channel_id=1, replica_groups={{0,16,32,48,64,80,96,112},{8,24,40,56,72,88,104,120},{1,17,33,49,65,81,..., dimensions={0} | all-to-all | bytes 2359296 | tf_op jit(solution)/shard_map/all_to_all | solution.py:444
  118.2 3.7 %all-to-all-start.2 = ((bf16[8,256,256]{2,1,0:T(8,128)(2,1)}), bf16[8,256,256]{2,1,0:T(8,128)(2,1)S(1)}, u32[]{:S(2)}, u32[]{:S(2)}) async-start(bf16[8,256,256]{2,1,0:T(8,128)(2,1)} %get-tuple-element.26), calls=%async_computation.2 | async-start | bytes 2097152 | tf_op jit(solution)/shard_map/all_to_all | solution.py:444
  121.9 0.1 collective-permute-start.10
  122.0 14.1 %all-to-all-done.2.rest_0_ = bf16[8,256,256]{2,1,0:T(8,128)(2,1)S(1)} async-done(((bf16[8,256,256]{2,1,0:T(8,128)(2,1)}), bf16[8,256,256]{2,1,0:T(8,128)(2,1)S(1)}, u32[]{:S(2)}, u32[]{:S(2)}) %all-to-all-start.2) | async-done | bytes 1048608 | tf_op jit(solution)/shard_map/all_to_all | solution.py:444
  136.0 0.0 collective-permute-start.9
  136.0 2.7 %collective-permute-done.9.rest_1_ = bf16[8,256,256]{2,1,0:T(8,128)(2,1)S(1)} collective-permute-done((bf16[8,256,256]{2,1,0:T(8,128)(2,1)S(1)}, bf16[8,256,256]{2,1,0:T(8,128)(2,1)S(1)}, u32[]{:S(2)}, u32[]{:S(2)}) %collective-permute-start.9) | collective-permute-done | bytes 1048608 | tf_op jit(solution)/shard_map/ppermute | solution.py:440
  138.7 0.0 collective-permute-done.10.rest_3_
  138.7 0.0 copy-done.12
  138.7 0.0 copy-start.1
  138.7 7.7 %backward_tiles.3 = bf16[8,288,256]{2,1,0:T(8,128)(2,1)S(1)} custom-call(s32[640]{0:T(1024)S(1)} %copy-done.10, s32[4]{0:T(128)S(1)} %copy-done.12, bf16[128,256,256]{2,1,0:T(8,128)(2,1)} %bitcast.16, bf16[8,256,256]{2,1,0:T(8,128)(2,1)S(1)} %all-to-all-done.2.rest_0_, bf16[8,256,256]{2,1,0:T(8,128)(2,1)S(1)} %collective-permute-done.9.rest_1_, ...), custom_call_target="tpu_custom_call" | custom-call | flops 1073741824 | bytes 14680064 | tf_op jit(solution)/shard_map/backward_tiles/pallas_call | solution.py:300
  146.4 0.0 copy-done.1
  146.4 0.0 copy-start
  146.5 1.0 copy-done
  147.5 1.0 copy-done.4
  148.5 8.6 %all-to-all-start.5 = ((bf16[8,288,256]{2,1,0:T(8,128)(2,1)}), bf16[8,288,256]{2,1,0:T(8,128)(2,1)S(1)}, u32[]{:S(2)}, u32[]{:S(2)}) async-start(bf16[8,288,256]{2,1,0:T(8,128)(2,1)} %copy-done), calls=%async_computation.5 | async-start | bytes 2359296 | tf_op jit(solution)/shard_map/all_to_all | solution.py:448
  157.1 1.3 copy-done.2
  158.4 1.2 copy-done.5
  159.6 8.0 %backward_tiles.2 = bf16[8,256,256]{2,1,0:T(8,128)(2,1)S(1)} custom-call(s32[640]{0:T(1024)S(1)} %copy-done.10, s32[4]{0:T(128)S(1)} %copy-done.12, bf16[128,256,256]{2,1,0:T(8,128)(2,1)} %bitcast.17, bf16[8,256,256]{2,1,0:T(8,128)(2,1)S(1)} %all-to-all-done.2.rest_0_, bf16[8,256,256]{2,1,0:T(8,128)(2,1)S(1)} %copy-done.5, ...), custom_call_target="tpu_custom_call" | custom-call | flops 1073741824 | bytes 14680064 | tf_op jit(solution)/shard_map/backward_tiles/pallas_call | solution.py:300
  167.6 1.0 copy-done.3
  168.6 5.3 %all-to-all-done.5.recv_ref = bf16[8,288,256]{2,1,0:T(8,128)(2,1)S(1)} async-done(((bf16[8,288,256]{2,1,0:T(8,128)(2,1)}), bf16[8,288,256]{2,1,0:T(8,128)(2,1)S(1)}, u32[]{:S(2)}, u32[]{:S(2)}) %all-to-all-start.5) | async-done | bytes 1179680 | tf_op jit(solution)/shard_map/all_to_all | solution.py:448
  173.9 4.4 %all-to-all-start.4 = ((bf16[8,256,256]{2,1,0:T(8,128)(2,1)}), bf16[8,256,256]{2,1,0:T(8,128)(2,1)S(1)}, u32[]{:S(2)}, u32[]{:S(2)}) async-start(bf16[8,256,256]{2,1,0:T(8,128)(2,1)} %copy-done.3), calls=%async_computation.4 | async-start | bytes 2097152 | tf_op jit(solution)/shard_map/all_to_all | solution.py:448
  178.2 0.9 last_sum.2
  179.1 16.0 %all-to-all-done.4.recv_ref = bf16[8,256,256]{2,1,0:T(8,128)(2,1)S(1)} async-done(((bf16[8,256,256]{2,1,0:T(8,128)(2,1)}), bf16[8,256,256]{2,1,0:T(8,128)(2,1)S(1)}, u32[]{:S(2)}, u32[]{:S(2)}) %all-to-all-start.4) | async-done | bytes 1048608 | tf_op jit(solution)/shard_map/all_to_all | solution.py:448
  195.1 3.6 %all-to-all-start.6 = ((f32[8,32,128]{2,1,0:T(8,128)}), f32[8,32,128]{2,1,0:T(8,128)S(1)}, u32[]{:S(2)}, u32[]{:S(2)}) async-start(f32[8,32,128]{2,1,0:T(8,128)} %get-tuple-element.29), calls=%async_computation.6 | async-start | bytes 262144 | tf_op jit(solution)/shard_map/all_to_all | solution.py:444
  198.7 0.9 last_sum.3
  199.6 7.0 %all-to-all-done.6 = f32[8,32,128]{2,1,0:T(8,128)S(1)} async-done(((f32[8,32,128]{2,1,0:T(8,128)}), f32[8,32,128]{2,1,0:T(8,128)S(1)}, u32[]{:S(2)}, u32[]{:S(2)}) %all-to-all-start.6) | async-done | bytes 131104 | tf_op jit(solution)/shard_map/all_to_all | solution.py:444
  206.7 0.5 slice_bitcast_fusion
  207.2 0.6 slice.8
  (13 shorter events, 0.0 us)
Async XLA Ops:
  0.6 13.4 %collective-permute-start.6 = (bf16[1024,128]{1,0:T(8,128)(2,1)}, bf16[1024,128]{1,0:T(8,128)(2,1)S(1)}, u32[]{:S(2)}, u32[]{:S(2)}) collective-permute-start(bf16[1024,128]{1,0:T(8,128)(2,1)} %rest_0_.3), channel_id=1, source_target_pairs={{0,7},{1,6},{2,1},{3,0},{4,3},{5,2},{6,5},{7,4},{8,15},{9,14},{10,... | collective-permute-start | bytes 786440 | tf_op jit(solution)/shard_map/ppermute | solution.py:456
  5.8 22.6 %collective-permute-start.5 = (bf16[1024,128]{1,0:T(8,128)(2,1)}, bf16[1024,128]{1,0:T(8,128)(2,1)S(1)}, u32[]{:S(2)}, u32[]{:S(2)}) collective-permute-start(bf16[1024,128]{1,0:T(8,128)(2,1)} %rest_0_.3), channel_id=1, source_target_pairs={{0,6},{1,7},{2,0},{3,1},{4,2},{5,3},{6,4},{7,5},{8,14},{9,15},{10,... | collective-permute-start | bytes 786440 | tf_op jit(solution)/shard_map/ppermute | solution.py:456
  6.2 27.7 %collective-permute-start.4 = (bf16[1024,128]{1,0:T(8,128)(2,1)}, bf16[1024,128]{1,0:T(8,128)(2,1)S(1)}, u32[]{:S(2)}, u32[]{:S(2)}) collective-permute-start(bf16[1024,128]{1,0:T(8,128)(2,1)} %rest_0_.3), channel_id=1, source_target_pairs={{0,5},{1,4},{2,7},{3,6},{4,1},{5,0},{6,3},{7,2},{8,13},{9,12},{10,... | collective-permute-start | bytes 786440 | tf_op jit(solution)/shard_map/ppermute | solution.py:456
  6.2 27.7 %collective-permute-start.3 = (bf16[1024,128]{1,0:T(8,128)(2,1)}, bf16[1024,128]{1,0:T(8,128)(2,1)S(1)}, u32[]{:S(2)}, u32[]{:S(2)}) collective-permute-start(bf16[1024,128]{1,0:T(8,128)(2,1)} %rest_0_.3), channel_id=1, source_target_pairs={{0,4},{1,5},{2,6},{3,7},{4,0},{5,1},{6,2},{7,3},{8,12},{9,13},{10,... | collective-permute-start | bytes 786440 | tf_op jit(solution)/shard_map/ppermute | solution.py:456
  9.7 24.3 %collective-permute-start.2 = (bf16[1024,128]{1,0:T(8,128)(2,1)}, bf16[1024,128]{1,0:T(8,128)(2,1)S(1)}, u32[]{:S(2)}, u32[]{:S(2)}) collective-permute-start(bf16[1024,128]{1,0:T(8,128)(2,1)} %rest_0_.3), channel_id=1, source_target_pairs={{0,3},{1,2},{2,5},{3,4},{4,7},{5,6},{6,1},{7,0},{8,11},{9,10},{10,... | collective-permute-start | bytes 786440 | tf_op jit(solution)/shard_map/ppermute | solution.py:456
  14.1 19.9 %collective-permute-start.1 = (bf16[1024,128]{1,0:T(8,128)(2,1)}, bf16[1024,128]{1,0:T(8,128)(2,1)S(1)}, u32[]{:S(2)}, u32[]{:S(2)}) collective-permute-start(bf16[1024,128]{1,0:T(8,128)(2,1)} %rest_0_.3), channel_id=1, source_target_pairs={{0,2},{1,3},{2,4},{3,5},{4,6},{5,7},{6,0},{7,1},{8,10},{9,11},{10,... | collective-permute-start | bytes 786440 | tf_op jit(solution)/shard_map/ppermute | solution.py:456
  28.5 8.4 %collective-permute-start = (bf16[1024,128]{1,0:T(8,128)(2,1)}, bf16[1024,128]{1,0:T(8,128)(2,1)S(1)}, u32[]{:S(2)}, u32[]{:S(2)}) collective-permute-start(bf16[1024,128]{1,0:T(8,128)(2,1)} %rest_0_.3), channel_id=1, source_target_pairs={{0,1},{1,0},{2,3},{3,2},{4,5},{5,4},{6,7},{7,6},{8,9},{9,8},{10,11... | collective-permute-start | bytes 786440 | tf_op jit(solution)/shard_map/ppermute | solution.py:456
  36.9 1.0 copy-start.6
  37.8 0.7 copy-start.9
  38.5 0.7 copy-start.11
  43.0 5.1 %collective-permute-start.8 = (bf16[8,512,128]{2,1,0:T(8,128)(2,1)S(1)}, bf16[8,512,128]{2,1,0:T(8,128)(2,1)S(1)}, u32[]{:S(2)}, u32[]{:S(2)}) collective-permute-start(bf16[8,512,128]{2,1,0:T(8,128)(2,1)S(1)} %get-tuple-element.22), channel_id=1, source_target_pairs={{0,8},{8,0},{16,24},{24,16},{32,40},{40,32},{48,56},{56,48},{64,72... | collective-permute-start | bytes 3145736 | tf_op jit(solution)/shard_map/ppermute | solution.py:440
  47.5 11.2 %collective-permute-start.7 = (bf16[8,512,128]{2,1,0:T(8,128)(2,1)}, bf16[8,512,128]{2,1,0:T(8,128)(2,1)}, u32[]{:S(2)}, u32[]{:S(2)}) collective-permute-start(bf16[8,512,128]{2,1,0:T(8,128)(2,1)} %get-tuple-element.20), channel_id=1, source_target_pairs={{0,8},{8,0},{16,24},{24,16},{32,40},{40,32},{48,56},{56,48},{64,72... | collective-permute-start | bytes 3145736 | tf_op jit(solution)/shard_map/ppermute | solution.py:440
  49.4 26.8 %all-to-all-start.1 = ((bf16[8,512,128]{2,1,0:T(8,128)(2,1)}), bf16[8,512,128]{2,1,0:T(8,128)(2,1)S(1)}, u32[]{:S(2)}, u32[]{:S(2)}) async-start(bf16[8,512,128]{2,1,0:T(8,128)(2,1)} %add.17), calls=%async_computation.1 | async-start | bytes 2097152 | tf_op jit(solution)/shard_map/all_to_all | solution.py:444
  61.2 18.5 %copy-start.7 = (bf16[1024,128]{1,0:T(8,128)(2,1)S(1)}, bf16[1024,128]{1,0:T(8,128)(2,1)}, u32[]{:S(2)}) copy-start(bf16[1024,128]{1,0:T(8,128)(2,1)} %cot_ref.3) | copy-start | bytes 786436
  61.2 18.5 %copy-start.8 = (bf16[128,128]{1,0:T(8,128)(2,1)S(1)}, bf16[128,128]{1,0:T(8,128)(2,1)}, u32[]{:S(2)}) copy-start(bf16[128,128]{1,0:T(8,128)(2,1)} %weight_ref.3) | copy-start | bytes 98308
  61.2 18.5 %copy-start.13 = (f32[128]{0:T(128)S(1)}, f32[128]{0:T(128)}, u32[]{:S(2)}) copy-start(f32[128]{0:T(128)} %param.10) | copy-start | bytes 1540
  76.1 19.1 %all-to-all-start = ((bf16[8,512,128]{2,1,0:T(8,128)(2,1)}), bf16[8,512,128]{2,1,0:T(8,128)(2,1)S(1)}, u32[]{:S(2)}, u32[]{:S(2)}) async-start(bf16[8,512,128]{2,1,0:T(8,128)(2,1)} %add.16), calls=%async_computation | async-start | bytes 2097152 | tf_op jit(solution)/shard_map/all_to_all | solution.py:444
  118.2 20.5 %copy-start.10 = (s32[640]{0:T(1024)S(1)}, s32[640]{0:T(1024)}, u32[]{:S(2)}) copy-start(s32[640]{0:T(1024)} %get-tuple-element.17.lists_ref) | copy-start | bytes 7684
  118.2 20.5 %copy-start.12 = (s32[4]{0:T(128)S(1)}, s32[4]{0:T(128)}, u32[]{:S(2)}) copy-start(s32[4]{0:T(128)} %get-tuple-element.18.sizes_ref) | copy-start | bytes 52
  118.2 17.9 %all-to-all-start.2 = ((bf16[8,256,256]{2,1,0:T(8,128)(2,1)}), bf16[8,256,256]{2,1,0:T(8,128)(2,1)S(1)}, u32[]{:S(2)}, u32[]{:S(2)}) async-start(bf16[8,256,256]{2,1,0:T(8,128)(2,1)} %get-tuple-element.26), calls=%async_computation.2 | async-start | bytes 2097152 | tf_op jit(solution)/shard_map/all_to_all | solution.py:444
  121.9 16.8 %collective-permute-start.10 = (bf16[8,288,256]{2,1,0:T(8,128)(2,1)S(1)}, bf16[8,288,256]{2,1,0:T(8,128)(2,1)S(1)}, u32[]{:S(2)}, u32[]{:S(2)}) collective-permute-start(bf16[8,288,256]{2,1,0:T(8,128)(2,1)S(1)} %all_to_all.35.rest_2_), channel_id=1, source_target_pairs={{0,8},{8,0},{16,24},{24,16},{32,40},{40,32},{48,56},{56,48},{64,72... | collective-permute-start | bytes 3538952 | tf_op jit(solution)/shard_map/ppermute | solution.py:440
  136.0 2.7 %collective-permute-start.9 = (bf16[8,256,256]{2,1,0:T(8,128)(2,1)S(1)}, bf16[8,256,256]{2,1,0:T(8,128)(2,1)S(1)}, u32[]{:S(2)}, u32[]{:S(2)}) collective-permute-start(bf16[8,256,256]{2,1,0:T(8,128)(2,1)S(1)} %all-to-all-done.2.rest_0_), channel_id=1, source_target_pairs={{0,8},{8,0},{16,24},{24,16},{32,40},{40,32},{48,56},{56,48},{64,72... | collective-permute-start | bytes 3145736 | tf_op jit(solution)/shard_map/ppermute | solution.py:440
  138.7 7.7 %copy-start.1 = (bf16[8,288,256]{2,1,0:T(8,128)(2,1)}, bf16[8,288,256]{2,1,0:T(8,128)(2,1)S(1)}, u32[]{:S(2)}) copy-start(bf16[8,288,256]{2,1,0:T(8,128)(2,1)S(1)} %collective-permute-done.10.rest_3_) | copy-start | bytes 3538948
  146.4 1.0 copy-start
  147.5 1.0 copy-start.4
  148.5 25.4 %all-to-all-start.5 = ((bf16[8,288,256]{2,1,0:T(8,128)(2,1)}), bf16[8,288,256]{2,1,0:T(8,128)(2,1)S(1)}, u32[]{:S(2)}, u32[]{:S(2)}) async-start(bf16[8,288,256]{2,1,0:T(8,128)(2,1)} %copy-done), calls=%async_computation.5 | async-start | bytes 2359296 | tf_op jit(solution)/shard_map/all_to_all | solution.py:448
  157.1 1.3 copy-start.2
  158.4 1.2 copy-start.5
  167.6 1.0 copy-start.3
  173.9 21.3 %all-to-all-start.4 = ((bf16[8,256,256]{2,1,0:T(8,128)(2,1)}), bf16[8,256,256]{2,1,0:T(8,128)(2,1)S(1)}, u32[]{:S(2)}, u32[]{:S(2)}) async-start(bf16[8,256,256]{2,1,0:T(8,128)(2,1)} %copy-done.3), calls=%async_computation.4 | async-start | bytes 2097152 | tf_op jit(solution)/shard_map/all_to_all | solution.py:448
  195.1 11.5 %all-to-all-start.6 = ((f32[8,32,128]{2,1,0:T(8,128)}), f32[8,32,128]{2,1,0:T(8,128)S(1)}, u32[]{:S(2)}, u32[]{:S(2)}) async-start(f32[8,32,128]{2,1,0:T(8,128)} %get-tuple-element.29), calls=%async_computation.6 | async-start | bytes 262144 | tf_op jit(solution)/shard_map/all_to_all | solution.py:444

commit v2 on v1

v2 whole, which is shorter than its diff:
```python
import functools
import math

import jax
import jax.numpy as jnp
from jax import lax
from jax.experimental import pallas as pl
from jax.experimental.pallas import tpu as pltpu
from jax.sharding import PartitionSpec as P

gelu_coef = 0.7978845608
cube_coef = 0.044715
TILE = 256
FEAT = 128
SLOTS = 128
NPEER = 8
LIST = 160
UNROLL = 8
DEPTH = 32
EXTRA = 32
FWD_DUMMY = 32
BWD_DUMMY = 16
f32, bf16 = jnp.float32, jnp.bfloat16
VMEM_LIMIT = 28 * 2**20


def params():
    return pltpu.CompilerParams(vmem_limit_bytes=VMEM_LIMIT)


def vmem():
    return pl.BlockSpec(memory_space=pltpu.VMEM)


def smem():
    return pl.BlockSpec(memory_space=pltpu.SMEM)


def hbm():
    return pl.BlockSpec(memory_space=pl.ANY)


def prep_kernel(where_ref, out_ref, in_ref, count_ref, lists_ref, sizes_ref):
    x, yh, core, z, y = (where_ref[i] for i in range(5))

    def clear(i, carry):
        lists_ref[i] = FWD_DUMMY << 16
        lists_ref[LIST + i] = FWD_DUMMY << 16
        lists_ref[2 * LIST + i] = BWD_DUMMY << 16
        lists_ref[3 * LIST + i] = BWD_DUMMY << 16
        return carry

    lax.fori_loop(0, LIST, clear, 0)

    def place(k, carry):
        f0, f1, b0, b1 = carry
        t = out_ref[k]
        s = in_ref[k]
        rel = jnp.bitwise_xor((t >> 2) & 1, core)
        yh_t, x_t = (t >> 3) & 1, t >> 4
        half_t, sub_t = (t >> 1) & 1, t & 1
        y_s, z_s = (s >> 2) & 1, s >> 3
        half_s, sub_s = (s >> 1) & 1, s & 1
        dy_row = (yh_t + yh) & 1
        dy_col = (y_s + y) & 1
        j_t = t >> 3
        src_f = ((((z - z_s) & 3) * 2 + dy_col) << 2) + (s & 3)
        to_t = jnp.where(half_t == 0, j_t, ((x_t - x) & 3) * 2 + dy_row)
        from_t = jnp.where(half_t == 0, ((x - x_t) & 3) * 2 + dy_row, j_t)
        dst_f = rel * 16 + to_t * 2 + sub_t
        src_b = ((half_t * 2 + rel) * NPEER + from_t) * 2 + sub_t
        to_s = jnp.where(half_s == 0, s >> 2, ((z_s - z) & 3) * 2 + dy_col)
        dst_b = to_s * 2 + sub_s
        at_f = jnp.where(half_t == 0, f0, LIST + f1)
        at_b = jnp.where(half_s == 0, 2 * LIST + b0, 3 * LIST + b1)
        lists_ref[at_f] = k | (src_f << 8) | (dst_f << 16)
        lists_ref[at_b] = k | (src_b << 8) | (dst_b << 16)
        return (
            f0 + 1 - half_t,
            f1 + half_t,
            b0 + 1 - half_s,
            b1 + half_s,
        )

    zero = jnp.int32(0)
    sizes = lax.fori_loop(0, count_ref[0], place, (zero, zero, zero, zero))
    for i in range(4):
        sizes_ref[i] = sizes[i]


def prep(where, out_index, in_index, count):
    return pl.pallas_call(
        prep_kernel,
        out_shape=(
            jax.ShapeDtypeStruct((4 * LIST,), jnp.int32),
            jax.ShapeDtypeStruct((4,), jnp.int32),
        ),
        in_specs=[smem()] * 4,
        out_specs=(smem(), smem()),
        name="slot_lists",
    )(where, out_index, in_index, count)


def tile_loop(which, lists_ref, sizes_ref, vals, buf, sems, acc, ready, product):
    base = which * LIST
    groups = (sizes_ref[which] + (UNROLL - 1)) // UNROLL
    ahead = DEPTH // UNROLL

    def copy(g, u):
        slot = lists_ref[base + g * UNROLL + u] & 255
        at = lax.rem(g, ahead) * UNROLL + u
        return pltpu.make_async_copy(vals.at[slot], buf.at[at], sems.at[at])

    for g in range(ahead):

        @pl.when(g < groups)
        def _():
            for u in range(UNROLL):
                copy(g, u).start()

    ready()

    def body(g, carry):
        for u in range(UNROLL):
            copy(g, u).wait()
        todo = []
        for u in range(UNROLL):
            entry = lists_ref[base + g * UNROLL + u]
            at = lax.rem(g, ahead) * UNROLL + u
            todo.append((entry >> 16, product(buf[at], (entry >> 8) & 255)))
        for to, value in todo:
            acc[to] += value

        @pl.when(g + ahead < groups)
        def _():
            for u in range(UNROLL):
                copy(g + ahead, u).start()

        return carry

    lax.fori_loop(0, groups, body, 0)


def in_hbm(array):
    return pltpu.with_memory_space_constraint(array, pltpu.HBM)


TILES_COST = pl.CostEstimate(
    flops=2 * 64 * TILE * TILE * FEAT, bytes_accessed=20 * 2**20, transcendentals=0
)


def forward_kernel(half, lists_ref, sizes_ref, vals, *rest):
    blocks = rest[:NPEER]
    mine_ref, *others = rest[NPEER : NPEER + 3]
    x, buf, acc, sems = rest[NPEER + 3 :]

    def ready():
        def clear(i, carry):
            acc[i] = jnp.zeros((TILE, FEAT), f32)
            return carry

        lax.fori_loop(0, FWD_DUMMY, clear, 0)
        for k in range(NPEER):
            x[pl.ds(k * 4 * TILE, 4 * TILE), :] = blocks[k][...]

    def product(tile, source):
        rows = x[pl.ds(pl.multiple_of(source * TILE, TILE), TILE), :]
        return jnp.dot(tile, rows, preferred_element_type=f32)

    tile_loop(half, lists_ref, sizes_ref, vals, buf, sems, acc, ready, product)

    for i in range(2 * NPEER):
        peer, rows = i // 2, pl.ds((i % 2) * TILE, TILE)
        mine_ref[peer, rows, :] = acc[i].astype(bf16)
        others[peer // 4][peer % 4, rows, :] = acc[16 + i].astype(bf16)


def forward(half, lists, sizes, values, blocks):
    shape = jax.ShapeDtypeStruct((NPEER, 2 * TILE, FEAT), bf16)
    piece = jax.ShapeDtypeStruct((NPEER // 2, 2 * TILE, FEAT), bf16)
    return pl.pallas_call(
        functools.partial(forward_kernel, half),
        out_shape=(shape, piece, piece),
        in_specs=[smem(), smem(), hbm()] + [vmem()] * NPEER,
        out_specs=(vmem(), vmem(), vmem()),
        scratch_shapes=[
            pltpu.VMEM((NPEER * 4 * TILE, FEAT), bf16),
            pltpu.VMEM((DEPTH, TILE, TILE), bf16),
            pltpu.VMEM((FWD_DUMMY + 1, TILE, FEAT), f32),
            pltpu.SemaphoreType.DMA((DEPTH,)),
        ],
        compiler_params=params(),
        cost_estimate=TILES_COST,
        name="forward_tiles",
    )(lists, sizes, in_hbm(values), *blocks)


def pair_sum_kernel(half, mine_ref, low_ref, high_ref, *outs):
    others = [low_ref, high_ref]
    for k in range(NPEER):
        other = others[k // 4][k % 4].astype(f32)
        both = (mine_ref[k].astype(f32) + other).astype(bf16)
        if half == 0:
            outs[0][k] = both
        else:
            outs[k][...] = both


def pair_sum(half, mine, low, high):
    if half == 0:
        out_shape, out_specs = jax.ShapeDtypeStruct(mine.shape, bf16), vmem()
    else:
        out_shape = (jax.ShapeDtypeStruct(mine.shape[1:], bf16),) * NPEER
        out_specs = (vmem(),) * NPEER
    return pl.pallas_call(
        functools.partial(pair_sum_kernel, half),
        out_shape=out_shape,
        in_specs=[vmem()] * 3,
        out_specs=out_specs,
        compiler_params=params(),
        cost_estimate=pl.CostEstimate(flops=2**20, bytes_accessed=3 * 2**20, transcendentals=0),
        name="pair_sum",
    )(mine, low, high)


def split_lanes(value):
    high = value.astype(bf16)
    low = (value - high.astype(f32)).astype(bf16)
    return jnp.concatenate([high, low], axis=1)


def backward_kernel(half, lists_ref, sizes_ref, vals, *rest):
    rows2 = 2 * FEAT
    if half == 0:
        shifted, swapped = rest[: 2 * NPEER], rest[2 * NPEER : 2 * NPEER + 2]
        out_ref, g, buf, acc, sems = rest[2 * NPEER + 2 :]
    else:
        g, *outs = rest[: 1 + NPEER]
        buf, acc, sems = rest[1 + NPEER :]

    def ready():
        def clear(i, carry):
            acc[i] = jnp.zeros((FEAT, TILE), f32)
            return carry

        lax.fori_loop(0, BWD_DUMMY, clear, 0)
        if half == 0:
            for i in range(2 * NPEER):
                g[pl.ds(i * rows2, rows2), :] = shifted[i][...]
            for p in range(2):
                for peer in range(NPEER):
                    i = (2 + p) * NPEER + peer
                    g[pl.ds(i * rows2, rows2), :] = swapped[p][peer, pl.ds(0, rows2), :]

    def product(tile, source):
        rows = g[pl.ds(pl.multiple_of(source * FEAT, FEAT), FEAT), :]
        return jnp.dot(rows, tile, preferred_element_type=f32)

    tile_loop(2 + half, lists_ref, sizes_ref, vals, buf, sems, acc, ready, product)

    for i in range(2 * NPEER):
        rows = pl.ds((i % 2) * FEAT, FEAT)
        if half == 0:
            out_ref[i // 2, rows, :] = acc[i].astype(bf16)
        else:
            outs[i // 2][rows, :] = acc[i].astype(bf16)
    if half == 0:
        sums = []
        for p in range(2):
            total = jnp.zeros((EXTRA, FEAT), f32)
            for peer in range(NPEER):
                pair = swapped[p][peer, pl.ds(rows2, EXTRA), :].astype(f32)
                total += pair[:, :FEAT] + pair[:, FEAT:]
            sums.append(total)
        packed = split_lanes(sums[0] + sums[1])
        for peer in range(NPEER):
            out_ref[peer, pl.ds(rows2, EXTRA), :] = packed


def backward(half, lists, sizes, values, grads):
    if half == 0:
        out_shape = (
            jax.ShapeDtypeStruct((NPEER, 2 * FEAT + EXTRA, TILE), bf16),
            jax.ShapeDtypeStruct((4 * 2 * NPEER * FEAT, TILE), bf16),
        )
    else:
        out_shape = (jax.ShapeDtypeStruct((2 * FEAT, TILE), bf16),) * NPEER
    return pl.pallas_call(
        functools.partial(backward_kernel, half),
        out_shape=out_shape,
        in_specs=[smem(), smem(), hbm()] + [vmem()] * len(grads),
        out_specs=(vmem(),) * len(out_shape),
        scratch_shapes=[
            pltpu.VMEM((DEPTH, TILE, TILE), bf16),
            pltpu.VMEM((BWD_DUMMY + 1, FEAT, TILE), f32),
            pltpu.SemaphoreType.DMA((DEPTH,)),
        ],
        compiler_params=params(),
        cost_estimate=TILES_COST,
        name="backward_tiles",
    )(lists, sizes, in_hbm(values), *grads)


def dense_kernel(half, weight_ref, bias_ref, cot_ref, *rest):
    if half == 0:
        recv_ref, hidden_ref, grad_ref, wsum_ref = rest
        parts = [recv_ref.at[peer] for peer in range(NPEER)]
    else:
        before_ref, unused = rest[:2]
        parts = rest[2 : 2 + NPEER]
        hidden_ref, grad_ref = rest[2 + NPEER :]
    total = parts[0][...].astype(f32)
    for peer in range(1, NPEER):
        total += parts[peer][...].astype(f32)
    agg = total.astype(bf16)
    weight = weight_ref[...]
    v = jnp.dot(agg, weight, preferred_element_type=f32) + bias_ref[...]
    s = jnp.tanh(gelu_coef * (v + cube_coef * v * v * v))
    hidden_ref[...] = (0.5 * v * (1.0 + s)).astype(bf16)
    slope = 0.5 * (1.0 + s) + 0.5 * v * (1.0 - s * s) * gelu_coef * (1.0 + 3.0 * cube_coef * v * v)
    grad = (cot_ref[...].astype(f32) * slope).astype(bf16)
    wsum = lax.dot_general(agg, grad, (((0,), (0,)), ((), ())), preferred_element_type=f32)
    bsum = jnp.dot(jnp.ones((16, 2 * TILE), bf16), grad, preferred_element_type=f32)
    back = lax.dot_general(weight, grad, (((1,), (1,)), ((), ())), preferred_element_type=f32)
    back = back.astype(bf16)
    for sub in range(2):
        rows = pl.ds(sub * FEAT, FEAT)
        if half == 0:
            grad_ref[rows, :] = back[:, sub * TILE : (sub + 1) * TILE]
        else:
            for peer in range(NPEER):
                grad_ref[peer, rows, :] = back[:, sub * TILE : (sub + 1) * TILE]
    if half == 0:
        wsum_ref[pl.ds(0, FEAT), :] = wsum
        wsum_ref[pl.ds(FEAT, 16), :] = bsum
    else:
        wpack = split_lanes(wsum + before_ref[pl.ds(0, FEAT), :])
        bpack = split_lanes(bsum + before_ref[pl.ds(FEAT, 16), :])
        for peer in range(NPEER):
            grad_ref[peer, pl.ds(2 * FEAT, 16), :] = wpack[peer * 16 : peer * 16 + 16]
            grad_ref[peer, pl.ds(2 * FEAT + 16, 16), :] = bpack


def dense(half, recv, weight, bias, cotangent, before=None, hidden=None):
    hidden_shape = jax.ShapeDtypeStruct((4 * TILE, FEAT), bf16)
    half_rows = pl.BlockSpec((2 * TILE, FEAT), lambda i: (half, 0))
    wsum_shape = jax.ShapeDtypeStruct((FEAT + 16, FEAT), f32)

    def whole(*shape):
        return pl.BlockSpec(shape, lambda i: (0,) * len(shape))

    in_specs = [whole(FEAT, FEAT), whole(1, FEAT), half_rows]
    operands = [weight, bias, cotangent]
    aliases = {}
    if half == 0:
        grad = (2 * FEAT, TILE)
        in_specs += [whole(NPEER, 2 * TILE, FEAT)]
        operands += [recv]
        out_shape = (hidden_shape, jax.ShapeDtypeStruct(grad, bf16), wsum_shape)
        out_specs = (half_rows, whole(*grad), whole(FEAT + 16, FEAT))
    else:
        grad = (NPEER, 2 * FEAT + EXTRA, TILE)
        in_specs += [whole(FEAT + 16, FEAT), hbm()] + [whole(2 * TILE, FEAT)] * NPEER
        operands += [before, hidden, *recv]
        out_shape = (hidden_shape, jax.ShapeDtypeStruct(grad, bf16))
        out_specs = (half_rows, whole(*grad))
        aliases = {4: 0}
    return pl.pallas_call(
        functools.partial(dense_kernel, half),
        grid=(1,),
        out_shape=out_shape,
        in_specs=in_specs,
        out_specs=out_specs,
        input_output_aliases=aliases,
        compiler_params=params(),
        cost_estimate=pl.CostEstimate(
            flops=6 * 512 * FEAT * FEAT, bytes_accessed=3 * 2**20, transcendentals=512 * FEAT
        ),
        name="dense_layer",
    )(*operands)


def last_kernel(half, scale, *rest):
    if half == 0:
        recv_ref, grad_ref, slice_ref = rest
        parts = [recv_ref.at[peer] for peer in range(NPEER)]
    else:
        parts = rest[1 : 1 + NPEER]
        grad_ref = rest[1 + NPEER]
    for sub in range(2):
        rows = pl.ds(sub * FEAT, FEAT)
        total = parts[0][rows, :].astype(f32)
        for peer in range(1, NPEER):
            total += parts[peer][rows, :].astype(f32)
        grad_ref[pl.ds(sub * TILE, TILE), :] = total.T.astype(bf16)
    if half == 0:
        total = jnp.zeros((EXTRA, FEAT), f32)
        for peer in range(NPEER):
            pair = recv_ref[peer, pl.ds(2 * FEAT, EXTRA), :].astype(f32)
            total += pair[:, :FEAT] + pair[:, FEAT:]
        total = total * scale
        for peer in range(NPEER):
            slice_ref[peer] = total


def last(half, scale, recv, grad=None):
    half_rows = pl.BlockSpec((2 * TILE, FEAT), lambda i: (half, 0))
    grad_shape = jax.ShapeDtypeStruct((4 * TILE, FEAT), bf16)
    aliases = {}
    if half == 0:
        in_specs = [pl.BlockSpec(recv.shape, lambda i: (0, 0, 0))]
        operands = [recv]
        out_shape = (grad_shape, jax.ShapeDtypeStruct((NPEER, EXTRA, FEAT), f32))
        out_specs = (half_rows, pl.BlockSpec((NPEER, EXTRA, FEAT), lambda i: (0, 0, 0)))
    else:
        in_specs = [hbm()] + [pl.BlockSpec((2 * FEAT, TILE), lambda i: (0, 0))] * NPEER
        operands = [grad, *recv]
        out_shape = grad_shape
        out_specs = half_rows
        aliases = {0: 0}
    return pl.pallas_call(
        functools.partial(last_kernel, half, scale),
        grid=(1,),
        out_shape=out_shape,
        in_specs=in_specs,
        out_specs=out_specs,
        input_output_aliases=aliases,
        compiler_params=params(),
        cost_estimate=pl.CostEstimate(flops=2**20, bytes_accessed=2 * 2**20, transcendentals=0),
        name="last_sum",
    )(*operands)


SAME_CORE = [[2 * j + core for j in range(NPEER)] for core in range(2)]
OTHER_CORE = [(r, r ^ 1) for r in range(16)]


def to_other_core(value):
    return lax.ppermute(value, "row", OTHER_CORE)


def row_exchange(value):
    return lax.all_to_all(value, "row", 0, 0, axis_index_groups=SAME_CORE)


def col_exchange(value):
    return lax.all_to_all(value, "col", 0, 0)


def col_shift(value, k):
    pairs = []
    for c in range(8):
        z, y = c // 2, c % 2
        pairs.append((c, ((z + k // 2) % 4) * 2 + (y + k) % 2))
    return lax.ppermute(value, "col", pairs)


def row_shift(value, k):
    pairs = []
    for r in range(16):
        x, y, core = r // 4, (r // 2) % 2, r % 2
        pairs.append((r, ((x + k // 2) % 4) * 4 + ((y + k) % 2) * 2 + core))
    return lax.ppermute(value, "row", pairs)


def local(features, weight, layer_bias, cotangent, tile_out, tile_in, tile_vals, tile_count):
    values = tile_vals[0, 0]
    row, col = lax.axis_index("row"), lax.axis_index("col")
    where = jnp.stack([row >> 2, (row >> 1) & 1, row & 1, col >> 1, col & 1]).astype(jnp.int32)
    lists, sizes = prep(where, tile_out[0, 0], tile_in[0, 0], tile_count[0])
    bias = layer_bias.reshape(1, FEAT)
    order = lax.optimization_barrier

    blocks = [features] + [col_shift(features, k) for k in range(1, NPEER)]

    mine, low, high = forward(0, lists, sizes, values, blocks)
    both = pair_sum(0, mine, to_other_core(low), to_other_core(high))
    both, lists = order((both, lists))
    swapped = row_exchange(both)
    mine, low, high = forward(1, lists, sizes, values, blocks)
    chunks = pair_sum(1, mine, to_other_core(low), to_other_core(high))
    shifted = [chunks[0]] + [row_shift(chunks[k], k) for k in range(1, NPEER)]

    swapped = order((swapped, *chunks))[0]
    hidden, grad, wsum = dense(0, swapped, weight, bias, cotangent)
    grads = [grad] + [row_shift(grad, k) for k in range(1, NPEER)]
    hidden, grad = dense(1, shifted, weight, bias, cotangent, wsum, hidden)
    grad, *grads = order((grad, *grads))
    swapped = row_exchange(grad)
    grads += [to_other_core(g) for g in grads]
    swapped, *grads = order((swapped, *grads))
    grads += [swapped, to_other_core(swapped)]

    back, grads = backward(0, lists, sizes, values, grads)
    back0 = col_exchange(back)
    chunks = backward(1, lists, sizes, values, [grads])
    back1 = [chunks[0]] + [col_shift(chunks[k], k) for k in range(1, NPEER)]
    scale = 1.0 / math.sqrt(4 * TILE * 128)
    feature_grad, wslice = last(0, scale, back0)
    slices = row_exchange(wslice)
    feature_grad = last(1, scale, back1, feature_grad)
    weight_grad = slices[:, :16].reshape(FEAT, FEAT)
    bias_grad = slices[0, 16]
    return (hidden, feature_grad, weight_grad, bias_grad)


def solution(mesh):
    in_specs = (
        P(("row", "col"), None),
        P(),
        P(),
        P(("col", "row"), None),
        P("row", "col", None),
        P("row", "col", None),
        P("row", "col", None, None, None),
        P("row", "col"),
    )
    out_specs = (P(("col", "row"), None), P(("row", "col"), None), P(), P())
    return jax.shard_map(local, mesh=mesh, in_specs=in_specs, out_specs=out_specs, check_vma=False)
```

time: 209 us -> 181 us (0.87)
  starting transfers between devices: 46.4 us -> 92.2 us
  waiting for transfers between devices: 93 us -> 57.9 us
  blocking collectives: 21.9 us -> 0 us
  Pallas kernels: 31.7 us -> 21.6 us
  other arithmetic: 4.34 us -> 0 us
    ppermute x0 -> x14, starting transfers between devices: none -> 32.6 us  [row_shift(): return lax.ppermute(value, 'row', pairs)]
    all_to_all x4 -> x3, waiting for transfers between devices: 50 us -> 17.4 us  [row_exchange(): return lax.all_to_all(value, 'row', 0, 0, axis_index_groups=SAME_CORE)]
    all_to_all x1 -> x0, blocking collectives: 21.9 us -> none  [row_exchange(): return lax.all_to_all(value, 'row', 0, 0, axis_index_groups=SAME_CORE)]
    all_to_all x2 -> x1, waiting for transfers between devices: 21.3 us -> 0.01 us  [col_exchange(): return lax.all_to_all(value, 'col', 0, 0)]
    ppermute x7 -> x14, starting transfers between devices: 12.4 us -> 26.8 us  [col_shift(): return lax.ppermute(value, 'col', pairs)]
    ppermute x7 -> x14, waiting for transfers between devices: 19.1 us -> 27.6 us  [col_shift(): return lax.ppermute(value, 'col', pairs)]
    pallas_call x2 -> x4, Pallas kernels: 15.7 us -> 8.08 us  [the longest x2 6.59 us: backward(): pl.pallas_call(functools.partial(backward_kernel, half), out_shape=out_sh...]
    ppermute x4 -> x13, waiting for transfers between devices: 2.67 us -> 8.59 us  [to_other_core(): return lax.ppermute(value, 'row', OTHER_CORE)]
  transfers between devices with their start and end apart: 17 -> 45, of which waited for: 10 -> 21; matrix products, arithmetic and copies ran while one was open for 2% -> 0% of each run, Pallas kernels for 9% -> 7%
where the time goes in v2:
time: 181 us; the launch traced here: 182 us
  starting transfers between devices  92.2 us (51%)
  waiting for transfers between devices  57.9 us (32%)
  Pallas kernels  21.6 us (12%)
  local copies, waits for them, and re-layouts  8.29 us (5%)
    ppermute x14, starting transfers between devices, row_shift(): return lax.ppermute(value, 'row', pairs)  32.6 us
    ppermute x14, waiting for transfers between devices, col_shift(): return lax.ppermute(value, 'col', pairs)  27.6 us
    ppermute x14, starting transfers between devices, col_shift(): return lax.ppermute(value, 'col', pairs)  26.8 us
    all_to_all x3, starting transfers between devices, row_exchange(): return lax.all_to_all(value, 'row', 0, 0, axis_index_groups=SAME_CORE)  20.3 us
    all_to_all x3, waiting for transfers between devices, row_exchange(): return lax.all_to_all(value, 'row', 0, 0, axis_index_groups=SAME_CORE)  17.4 us
    all_to_all x1, starting transfers between devices, col_exchange(): return lax.all_to_all(value, 'col', 0, 0)  8.79 us
    ppermute x13, waiting for transfers between devices, to_other_core(): return lax.ppermute(value, 'row', OTHER_CORE)  8.59 us
    pallas_call x2, Pallas kernels, backward(): pl.pallas_call(functools.partial(backward_kernel, half), out_shape=out_sh...  6.59 us
  transfers between devices with their start and end apart: 45, of which 21 were waited for; matrix products, arithmetic and copies ran while one was open for 0% of the time, Pallas kernels for 7%

profile of v2, /device:TPU:0, one launch (start us, length us, event | category | flops | bytes accessed | tf_op | source)
XLA Modules:
  0.0 181.7 jit_solution(4142958550685031832)
XLA Ops:
  0.6 5.2 %collective-permute-start.6 = (bf16[1024,128]{1,0:T(8,128)(2,1)}, bf16[1024,128]{1,0:T(8,128)(2,1)S(1)}, u32[]{:S(2)}, u32[]{:S(2)}) collective-permute-start(bf16[1024,128]{1,0:T(8,128)(2,1)} %rest_0_.3), channel_id=1, source_target_pairs={{0,7},{1,6},{2,1},{3,0},{4,3},{5,2},{6,5},{7,4},{8,15},{9,14},{10,... | collective-permute-start | bytes 786440 | tf_op jit(solution)/shard_map/ppermute | solution.py:456
  5.8 0.4 collective-permute-start.5
  6.2 3.4 %collective-permute-start.3 = (bf16[1024,128]{1,0:T(8,128)(2,1)}, bf16[1024,128]{1,0:T(8,128)(2,1)S(1)}, u32[]{:S(2)}, u32[]{:S(2)}) collective-permute-start(bf16[1024,128]{1,0:T(8,128)(2,1)} %rest_0_.3), channel_id=1, source_target_pairs={{0,4},{1,5},{2,6},{3,7},{4,0},{5,1},{6,2},{7,3},{8,12},{9,13},{10,... | collective-permute-start | bytes 786440 | tf_op jit(solution)/shard_map/ppermute | solution.py:456
  9.7 2.6 %collective-permute-start.2 = (bf16[1024,128]{1,0:T(8,128)(2,1)}, bf16[1024,128]{1,0:T(8,128)(2,1)S(1)}, u32[]{:S(2)}, u32[]{:S(2)}) collective-permute-start(bf16[1024,128]{1,0:T(8,128)(2,1)} %rest_0_.3), channel_id=1, source_target_pairs={{0,3},{1,2},{2,5},{3,4},{4,7},{5,6},{6,1},{7,0},{8,11},{9,10},{10,... | collective-permute-start | bytes 786440 | tf_op jit(solution)/shard_map/ppermute | solution.py:456
  12.3 1.8 collective-permute-done.6.rest_7_
  14.1 14.4 %collective-permute-done.5.rest_6_ = bf16[1024,128]{1,0:T(8,128)(2,1)S(1)} collective-permute-done((bf16[1024,128]{1,0:T(8,128)(2,1)}, bf16[1024,128]{1,0:T(8,128)(2,1)S(1)}, u32[]{:S(2)}, u32[]{:S(2)}) %collective-permute-start.5) | collective-permute-done | bytes 262176 | tf_op jit(solution)/shard_map/ppermute | solution.py:456
  28.5 0.8 collective-permute-start
  29.9 0.7 stack.23.where_ref
  30.5 3.2 %slot_lists.1 = (s32[640]{0:T(1024)}, s32[4]{0:T(128)}) custom-call(s32[5]{0:T(128)} %stack.23.where_ref, s32[128]{0:T(128)} %bitcast.21, s32[128]{0:T(128)} %bitcast.22, s32[1]{0:T(128)} %bitcast.13.count_ref), custom_call_target="tpu_custom_call" | custom-call | tf_op jit(solution)/shard_map/slot_lists/pallas_call | solution.py:92
  33.7 3.2 %collective-permute-done.rest_1_ = bf16[1024,128]{1,0:T(8,128)(2,1)S(1)} collective-permute-done((bf16[1024,128]{1,0:T(8,128)(2,1)}, bf16[1024,128]{1,0:T(8,128)(2,1)S(1)}, u32[]{:S(2)}, u32[]{:S(2)}) %collective-permute-start) | collective-permute-done | bytes 262176 | tf_op jit(solution)/shard_map/ppermute | solution.py:456
  36.9 0.9 copy-done.2
  37.8 0.7 copy-done.6
  38.5 0.7 copy-done.8
  39.2 3.3 %forward_tiles.2 = (bf16[8,512,128]{2,1,0:T(8,128)(2,1)S(1)}, bf16[4,512,128]{2,1,0:T(8,128)(2,1)S(1)}, bf16[4,512,128]{2,1,0:T(8,128)(2,1)S(1)}) custom-call(s32[640]{0:T(1024)S(1)} %copy-done.6, s32[4]{0:T(128)S(1)} %copy-done.8, bf16[128,256,256]{2,1,0:T(8,128)(2,1)} %bitcast.16, bf16[1024,128]{1,0:T(8,128)(2,1)S(1)} %copy-done.2, ...), custom_call_target="tpu_custom_call" | custom-call | flops 1073741824 | bytes 20971520 | tf_op jit(solution)/shard_map/forward_tiles/pallas_call | solution.py:182
  42.5 0.5 collective-permute-start.8
  43.0 1.4 collective-permute-done.7.low_ref
  44.4 0.7 collective-permute-done.8.high_ref
  45.2 1.3 pair_sum.2
  46.5 7.4 %all-to-all-start = ((bf16[8,512,128]{2,1,0:T(8,128)(2,1)}), bf16[8,512,128]{2,1,0:T(8,128)(2,1)S(1)}, u32[]{:S(2)}, u32[]{:S(2)}) async-start(bf16[8,512,128]{2,1,0:T(8,128)(2,1)} %pair_sum.2), calls=%async_computation | async-start | bytes 2097152 | tf_op jit(solution)/shard_map/all_to_all | solution.py:444
  53.9 2.8 %forward_tiles.3 = (bf16[8,512,128]{2,1,0:T(8,128)(2,1)S(1)}, bf16[4,512,128]{2,1,0:T(8,128)(2,1)S(1)}, bf16[4,512,128]{2,1,0:T(8,128)(2,1)S(1)}) custom-call(s32[640]{0:T(1024)S(1)} %copy-done.7, s32[4]{0:T(128)S(1)} %copy-done.9, bf16[128,256,256]{2,1,0:T(8,128)(2,1)} %bitcast.17, bf16[1024,128]{1,0:T(8,128)(2,1)S(1)} %copy-done.3, ...), custom_call_target="tpu_custom_call" | custom-call | flops 1073741824 | bytes 20971520 | tf_op jit(solution)/shard_map/forward_tiles/pallas_call | solution.py:182
  56.7 1.3 collective-permute-start.9
  58.1 1.4 collective-permute-done.9.low_ref
  59.5 0.7 collective-permute-done.10.high_ref
  60.5 3.8 %collective-permute-start.11 = (bf16[512,128]{1,0:T(8,128)(2,1)S(1)}, bf16[512,128]{1,0:T(8,128)(2,1)S(1)}, u32[]{:S(2)}, u32[]{:S(2)}) collective-permute-start(bf16[512,128]{1,0:T(8,128)(2,1)S(1)} %get-tuple-element.77), channel_id=1, source_target_pairs={{0,16},{8,24},{16,0},{24,8},{32,48},{40,56},{48,32},{56,40},{64,80... | collective-permute-start | bytes 393224 | tf_op jit(solution)/shard_map/ppermute | solution.py:464
  64.3 0.9 collective-permute-start.12
  65.2 3.3 %collective-permute-start.13 = (bf16[512,128]{1,0:T(8,128)(2,1)S(1)}, bf16[512,128]{1,0:T(8,128)(2,1)S(1)}, u32[]{:S(2)}, u32[]{:S(2)}) collective-permute-start(bf16[512,128]{1,0:T(8,128)(2,1)S(1)} %get-tuple-element.79), channel_id=1, source_target_pairs={{0,48},{8,56},{16,32},{24,40},{32,80},{40,88},{48,64},{56,72},{64,... | collective-permute-start | bytes 393224 | tf_op jit(solution)/shard_map/ppermute | solution.py:464
  68.5 4.5 %collective-permute-start.15 = (bf16[512,128]{1,0:T(8,128)(2,1)S(1)}, bf16[512,128]{1,0:T(8,128)(2,1)S(1)}, u32[]{:S(2)}, u32[]{:S(2)}) collective-permute-start(bf16[512,128]{1,0:T(8,128)(2,1)S(1)} %get-tuple-element.81), channel_id=1, source_target_pairs={{0,80},{8,88},{16,64},{24,72},{32,112},{40,120},{48,96},{56,104},{... | collective-permute-start | bytes 393224 | tf_op jit(solution)/shard_map/ppermute | solution.py:464
  73.1 1.0 dense_layer.2
  74.1 1.4 collective-permute-start.16
  75.4 0.7 collective-permute-start.17
  76.1 1.5 collective-permute-done.13.rest_5_
  77.7 2.8 %collective-permute-start.24 = (bf16[256,256]{1,0:T(8,128)(2,1)S(1)}, bf16[256,256]{1,0:T(8,128)(2,1)S(1)}, u32[]{:S(2)}, u32[]{:S(2)}) collective-permute-start(bf16[256,256]{1,0:T(8,128)(2,1)S(1)} %get-tuple-element.99.rest_0_), channel_id=1, source_target_pairs={{0,112},{8,120},{16,96},{24,104},{32,16},{40,24},{48,0},{56,8},{64... | collective-permute-start | bytes 393224 | tf_op jit(solution)/shard_map/ppermute | solution.py:464
  80.5 4.1 %collective-permute-start.23 = (bf16[256,256]{1,0:T(8,128)(2,1)S(1)}, bf16[256,256]{1,0:T(8,128)(2,1)S(1)}, u32[]{:S(2)}, u32[]{:S(2)}) collective-permute-start(bf16[256,256]{1,0:T(8,128)(2,1)S(1)} %get-tuple-element.99.rest_0_), channel_id=1, source_target_pairs={{0,96},{8,104},{16,112},{24,120},{32,0},{40,8},{48,16},{56,24},{64... | collective-permute-start | bytes 393224 | tf_op jit(solution)/shard_map/ppermute | solution.py:464
  84.6 6.1 %collective-permute-start.21 = (bf16[256,256]{1,0:T(8,128)(2,1)S(1)}, bf16[256,256]{1,0:T(8,128)(2,1)S(1)}, u32[]{:S(2)}, u32[]{:S(2)}) collective-permute-start(bf16[256,256]{1,0:T(8,128)(2,1)S(1)} %get-tuple-element.99.rest_0_), channel_id=1, source_target_pairs={{0,64},{8,72},{16,80},{24,88},{32,96},{40,104},{48,112},{56,120},{... | collective-permute-start | bytes 393224 | tf_op jit(solution)/shard_map/ppermute | solution.py:464
  90.7 5.0 %collective-permute-start.18 = (bf16[256,256]{1,0:T(8,128)(2,1)S(1)}, bf16[256,256]{1,0:T(8,128)(2,1)S(1)}, u32[]{:S(2)}, u32[]{:S(2)}) collective-permute-start(bf16[256,256]{1,0:T(8,128)(2,1)S(1)} %get-tuple-element.99.rest_0_), channel_id=1, source_target_pairs={{0,16},{8,24},{16,0},{24,8},{32,48},{40,56},{48,32},{56,40},{64,80... | collective-permute-start | bytes 393224 | tf_op jit(solution)/shard_map/ppermute | solution.py:464
  95.7 1.6 dense_layer.3
  97.3 2.0 %collective-permute-done.20.rest_3_ = bf16[256,256]{1,0:T(8,128)(2,1)S(1)} collective-permute-done((bf16[256,256]{1,0:T(8,128)(2,1)S(1)}, bf16[256,256]{1,0:T(8,128)(2,1)S(1)}, u32[]{:S(2)}, u32[]{:S(2)}) %collective-permute-start.20) | collective-permute-done | bytes 131104 | tf_op jit(solution)/shard_map/ppermute | solution.py:464
  99.6 0.5 collective-permute-done.18.rest_1_
  100.1 6.5 %all-to-all-start.1 = ((bf16[8,288,256]{2,1,0:T(8,128)(2,1)}), bf16[8,288,256]{2,1,0:T(8,128)(2,1)S(1)}, u32[]{:S(2)}, u32[]{:S(2)}) async-start(bf16[8,288,256]{2,1,0:T(8,128)(2,1)} %get-tuple-element.90), calls=%async_computation.1 | async-start | bytes 2359296 | tf_op jit(solution)/shard_map/all_to_all | solution.py:444
  106.6 0.5 collective-permute-start.26
  107.2 0.4 collective-permute-start.28
  108.9 0.3 collective-permute-done.30.rest_13_
  109.4 0.3 collective-permute-done.32.rest_15_
  109.8 10.4 %all-to-all-done.1.rest_16_ = bf16[8,288,256]{2,1,0:T(8,128)(2,1)S(1)} async-done(((bf16[8,288,256]{2,1,0:T(8,128)(2,1)}), bf16[8,288,256]{2,1,0:T(8,128)(2,1)S(1)}, u32[]{:S(2)}, u32[]{:S(2)}) %all-to-all-start.1) | async-done | bytes 1179680 | tf_op jit(solution)/shard_map/all_to_all | solution.py:444
  120.2 2.8 %collective-permute-done.33.rest_17_ = bf16[8,288,256]{2,1,0:T(8,128)(2,1)S(1)} collective-permute-done((bf16[8,288,256]{2,1,0:T(8,128)(2,1)S(1)}, bf16[8,288,256]{2,1,0:T(8,128)(2,1)S(1)}, u32[]{:S(2)}, u32[]{:S(2)}) %collective-permute-start.33) | collective-permute-done | bytes 1179680 | tf_op jit(solution)/shard_map/ppermute | solution.py:440
  123.1 3.7 %backward_tiles.2 = (bf16[8,288,256]{2,1,0:T(8,128)(2,1)}, bf16[8192,256]{1,0:T(8,128)(2,1)S(1)}) custom-call(s32[640]{0:T(1024)S(1)} %copy-done.7, s32[4]{0:T(128)S(1)} %copy-done.9, bf16[128,256,256]{2,1,0:T(8,128)(2,1)} %bitcast.18, bf16[256,256]{1,0:T(8,128)(2,1)S(1)} %get-tuple-element.99.rest_0_, bf16[256,256]{1,0:T(8,128)(2,1)S(1)} %collective-permute-done.18.rest_1_, ...), custom_call_target="tpu_custom_call" | custom-call | flops 1073741824 | bytes 20971520 | tf_op jit(solution)/shard_map/backward_tiles/pallas_call | solution.py:289
  126.8 2.0 %copy-done = bf16[8192,256]{1,0:T(8,128)(2,1)} copy-done((bf16[8192,256]{1,0:T(8,128)(2,1)}, bf16[8192,256]{1,0:T(8,128)(2,1)S(1)}, u32[]{:S(2)}) %copy-start) | copy-done | bytes 4194328
  128.7 8.8 %all-to-all-start.2 = ((bf16[8,288,256]{2,1,0:T(8,128)(2,1)}), bf16[8,288,256]{2,1,0:T(8,128)(2,1)S(1)}, u32[]{:S(2)}, u32[]{:S(2)}) async-start(bf16[8,288,256]{2,1,0:T(8,128)(2,1)} %get-tuple-element.116), calls=%async_computation.2 | async-start | bytes 2359296 | tf_op jit(solution)/shard_map/all_to_all | solution.py:448
  137.5 2.2 %copy-done.1 = bf16[8192,256]{1,0:T(8,128)(2,1)S(1)} copy-done((bf16[8192,256]{1,0:T(8,128)(2,1)S(1)}, bf16[8192,256]{1,0:T(8,128)(2,1)}, u32[]{:S(2)}) %copy-start.1) | copy-done | bytes 4194328
  139.7 2.9 %backward_tiles.3 = (bf16[256,256]{1,0:T(8,128)(2,1)S(1)}, bf16[256,256]{1,0:T(8,128)(2,1)S(1)}, bf16[256,256]{1,0:T(8,128)(2,1)S(1)}, bf16[256,256]{1,0:T(8,128...) custom-call(s32[640]{0:T(1024)S(1)} %copy-done.7, ...), custom_call_target="tpu_custom_call" | custom-call | flops 1073741824 | bytes 20971520 | tf_op jit(solution)/shard_map/backward_tiles/pallas_call | solution.py:289
  142.6 1.8 collective-permute-start.34
  144.4 3.7 %collective-permute-start.35 = (bf16[256,256]{1,0:T(8,128)(2,1)S(1)}, bf16[256,256]{1,0:T(8,128)(2,1)S(1)}, u32[]{:S(2)}, u32[]{:S(2)}) collective-permute-start(bf16[256,256]{1,0:T(8,128)(2,1)S(1)} %get-tuple-element.121), channel_id=1, source_target_pairs={{0,2},{1,3},{2,4},{3,5},{4,6},{5,7},{6,0},{7,1},{8,10},{9,11},{10,... | collective-permute-start | bytes 393224 | tf_op jit(solution)/shard_map/ppermute | solution.py:456
  148.3 3.4 %collective-permute-start.37 = (bf16[256,256]{1,0:T(8,128)(2,1)S(1)}, bf16[256,256]{1,0:T(8,128)(2,1)S(1)}, u32[]{:S(2)}, u32[]{:S(2)}) collective-permute-start(bf16[256,256]{1,0:T(8,128)(2,1)S(1)} %get-tuple-element.123), channel_id=1, source_target_pairs={{0,4},{1,5},{2,6},{3,7},{4,0},{5,1},{6,2},{7,3},{8,12},{9,13},{10,... | collective-permute-start | bytes 393224 | tf_op jit(solution)/shard_map/ppermute | solution.py:456
  151.7 0.9 collective-permute-start.38
  152.6 5.1 %collective-permute-done.34.rest_2_ = bf16[256,256]{1,0:T(8,128)(2,1)S(1)} collective-permute-done((bf16[256,256]{1,0:T(8,128)(2,1)S(1)}, bf16[256,256]{1,0:T(8,128)(2,1)S(1)}, u32[]{:S(2)}, u32[]{:S(2)}) %collective-permute-start.34) | collective-permute-done | bytes 131104 | tf_op jit(solution)/shard_map/ppermute | solution.py:456
  157.7 1.7 collective-permute-start.39
  159.4 3.2 %collective-permute-done.35.rest_3_ = bf16[256,256]{1,0:T(8,128)(2,1)S(1)} collective-permute-done((bf16[256,256]{1,0:T(8,128)(2,1)S(1)}, bf16[256,256]{1,0:T(8,128)(2,1)S(1)}, u32[]{:S(2)}, u32[]{:S(2)}) %collective-permute-start.35) | collective-permute-done | bytes 131104 | tf_op jit(solution)/shard_map/ppermute | solution.py:456
  162.6 2.7 %collective-permute-start.40 = (bf16[256,256]{1,0:T(8,128)(2,1)S(1)}, bf16[256,256]{1,0:T(8,128)(2,1)S(1)}, u32[]{:S(2)}, u32[]{:S(2)}) collective-permute-start(bf16[256,256]{1,0:T(8,128)(2,1)S(1)} %get-tuple-element.126), channel_id=1, source_target_pairs={{0,7},{1,6},{2,1},{3,0},{4,3},{5,2},{6,5},{7,4},{8,15},{9,14},{10,... | collective-permute-start | bytes 393224 | tf_op jit(solution)/shard_map/ppermute | solution.py:456
  165.3 0.9 last_sum.2
  166.2 6.4 %all-to-all-start.3 = ((f32[8,32,128]{2,1,0:T(8,128)}), f32[8,32,128]{2,1,0:T(8,128)S(1)}, u32[]{:S(2)}, u32[]{:S(2)}) async-start(f32[8,32,128]{2,1,0:T(8,128)} %get-tuple-element.127), calls=%async_computation.3 | async-start | bytes 262144 | tf_op jit(solution)/shard_map/all_to_all | solution.py:444
  172.6 0.9 last_sum.3
  173.5 7.0 %all-to-all-done.3 = f32[8,32,128]{2,1,0:T(8,128)S(1)} async-done(((f32[8,32,128]{2,1,0:T(8,128)}), f32[8,32,128]{2,1,0:T(8,128)S(1)}, u32[]{:S(2)}, u32[]{:S(2)}) %all-to-all-start.3) | async-done | bytes 131104 | tf_op jit(solution)/shard_map/all_to_all | solution.py:444
  180.5 0.5 slice_bitcast_fusion
  181.0 0.6 slice.8
  (62 shorter events, 2.8 us)
Async XLA Ops:
  0.6 13.4 %collective-permute-start.6 = (bf16[1024,128]{1,0:T(8,128)(2,1)}, bf16[1024,128]{1,0:T(8,128)(2,1)S(1)}, u32[]{:S(2)}, u32[]{:S(2)}) collective-permute-start(bf16[1024,128]{1,0:T(8,128)(2,1)} %rest_0_.3), channel_id=1, source_target_pairs={{0,7},{1,6},{2,1},{3,0},{4,3},{5,2},{6,5},{7,4},{8,15},{9,14},{10,... | collective-permute-start | bytes 786440 | tf_op jit(solution)/shard_map/ppermute | solution.py:456
  5.8 22.6 %collective-permute-start.5 = (bf16[1024,128]{1,0:T(8,128)(2,1)}, bf16[1024,128]{1,0:T(8,128)(2,1)S(1)}, u32[]{:S(2)}, u32[]{:S(2)}) collective-permute-start(bf16[1024,128]{1,0:T(8,128)(2,1)} %rest_0_.3), channel_id=1, source_target_pairs={{0,6},{1,7},{2,0},{3,1},{4,2},{5,3},{6,4},{7,5},{8,14},{9,15},{10,... | collective-permute-start | bytes 786440 | tf_op jit(solution)/shard_map/ppermute | solution.py:456
  6.2 27.5 %collective-permute-start.4 = (bf16[1024,128]{1,0:T(8,128)(2,1)}, bf16[1024,128]{1,0:T(8,128)(2,1)S(1)}, u32[]{:S(2)}, u32[]{:S(2)}) collective-permute-start(bf16[1024,128]{1,0:T(8,128)(2,1)} %rest_0_.3), channel_id=1, source_target_pairs={{0,5},{1,4},{2,7},{3,6},{4,1},{5,0},{6,3},{7,2},{8,13},{9,12},{10,... | collective-permute-start | bytes 786440 | tf_op jit(solution)/shard_map/ppermute | solution.py:456
  6.2 27.5 %collective-permute-start.3 = (bf16[1024,128]{1,0:T(8,128)(2,1)}, bf16[1024,128]{1,0:T(8,128)(2,1)S(1)}, u32[]{:S(2)}, u32[]{:S(2)}) collective-permute-start(bf16[1024,128]{1,0:T(8,128)(2,1)} %rest_0_.3), channel_id=1, source_target_pairs={{0,4},{1,5},{2,6},{3,7},{4,0},{5,1},{6,2},{7,3},{8,12},{9,13},{10,... | collective-permute-start | bytes 786440 | tf_op jit(solution)/shard_map/ppermute | solution.py:456
  9.7 24.1 %collective-permute-start.2 = (bf16[1024,128]{1,0:T(8,128)(2,1)}, bf16[1024,128]{1,0:T(8,128)(2,1)S(1)}, u32[]{:S(2)}, u32[]{:S(2)}) collective-permute-start(bf16[1024,128]{1,0:T(8,128)(2,1)} %rest_0_.3), channel_id=1, source_target_pairs={{0,3},{1,2},{2,5},{3,4},{4,7},{5,6},{6,1},{7,0},{8,11},{9,10},{10,... | collective-permute-start | bytes 786440 | tf_op jit(solution)/shard_map/ppermute | solution.py:456
  14.1 19.6 %collective-permute-start.1 = (bf16[1024,128]{1,0:T(8,128)(2,1)}, bf16[1024,128]{1,0:T(8,128)(2,1)S(1)}, u32[]{:S(2)}, u32[]{:S(2)}) collective-permute-start(bf16[1024,128]{1,0:T(8,128)(2,1)} %rest_0_.3), channel_id=1, source_target_pairs={{0,2},{1,3},{2,4},{3,5},{4,6},{5,7},{6,0},{7,1},{8,10},{9,11},{10,... | collective-permute-start | bytes 786440 | tf_op jit(solution)/shard_map/ppermute | solution.py:456
  28.5 8.4 %collective-permute-start = (bf16[1024,128]{1,0:T(8,128)(2,1)}, bf16[1024,128]{1,0:T(8,128)(2,1)S(1)}, u32[]{:S(2)}, u32[]{:S(2)}) collective-permute-start(bf16[1024,128]{1,0:T(8,128)(2,1)} %rest_0_.3), channel_id=1, source_target_pairs={{0,1},{1,0},{2,3},{3,2},{4,5},{5,4},{6,7},{7,6},{8,9},{9,8},{10,11... | collective-permute-start | bytes 786440 | tf_op jit(solution)/shard_map/ppermute | solution.py:456
  36.9 1.0 copy-start.2
  37.8 0.7 copy-start.6
  38.5 0.7 copy-start.8
  42.5 2.0 %collective-permute-start.7 = (bf16[4,512,128]{2,1,0:T(8,128)(2,1)S(1)}, bf16[4,512,128]{2,1,0:T(8,128)(2,1)S(1)}, u32[]{:S(2)}, u32[]{:S(2)}) collective-permute-start(bf16[4,512,128]{2,1,0:T(8,128)(2,1)S(1)} %get-tuple-element.69), channel_id=1, source_target_pairs={{0,8},{8,0},{16,24},{24,16},{32,40},{40,32},{48,56},{56,48},{64,72... | collective-permute-start | bytes 1572872 | tf_op jit(solution)/shard_map/ppermute | solution.py:440
  42.5 2.6 %collective-permute-start.8 = (bf16[4,512,128]{2,1,0:T(8,128)(2,1)S(1)}, bf16[4,512,128]{2,1,0:T(8,128)(2,1)S(1)}, u32[]{:S(2)}, u32[]{:S(2)}) collective-permute-start(bf16[4,512,128]{2,1,0:T(8,128)(2,1)S(1)} %get-tuple-element.70), channel_id=1, source_target_pairs={{0,8},{8,0},{16,24},{24,16},{32,40},{40,32},{48,56},{56,48},{64,72... | collective-permute-start | bytes 1572872 | tf_op jit(solution)/shard_map/ppermute | solution.py:440
  46.4 7.4 %copy-start.3 = (bf16[1024,128]{1,0:T(8,128)(2,1)S(1)}, bf16[1024,128]{1,0:T(8,128)(2,1)}, u32[]{:S(2)}) copy-start(bf16[1024,128]{1,0:T(8,128)(2,1)} %rest_0_.3) | copy-start | bytes 786436
  46.4 7.4 %copy-start.7 = (s32[640]{0:T(1024)S(1)}, s32[640]{0:T(1024)}, u32[]{:S(2)}) copy-start(s32[640]{0:T(1024)} %get-tuple-element.72.lists_ref) | copy-start | bytes 7684
  46.5 7.4 %copy-start.9 = (s32[4]{0:T(128)S(1)}, s32[4]{0:T(128)}, u32[]{:S(2)}) copy-start(s32[4]{0:T(128)} %get-tuple-element.67.sizes_ref) | copy-start | bytes 52
  46.5 26.6 %all-to-all-start = ((bf16[8,512,128]{2,1,0:T(8,128)(2,1)}), bf16[8,512,128]{2,1,0:T(8,128)(2,1)S(1)}, u32[]{:S(2)}, u32[]{:S(2)}) async-start(bf16[8,512,128]{2,1,0:T(8,128)(2,1)} %pair_sum.2), calls=%async_computation | async-start | bytes 2097152 | tf_op jit(solution)/shard_map/all_to_all | solution.py:444
  56.7 16.4 %copy-start.4 = (bf16[1024,128]{1,0:T(8,128)(2,1)S(1)}, bf16[1024,128]{1,0:T(8,128)(2,1)}, u32[]{:S(2)}) copy-start(bf16[1024,128]{1,0:T(8,128)(2,1)} %cot_ref.3) | copy-start | bytes 786436
  56.7 16.4 %copy-start.5 = (bf16[128,128]{1,0:T(8,128)(2,1)S(1)}, bf16[128,128]{1,0:T(8,128)(2,1)}, u32[]{:S(2)}) copy-start(bf16[128,128]{1,0:T(8,128)(2,1)} %weight_ref.3) | copy-start | bytes 98308
  56.7 16.4 %copy-start.10 = (f32[128]{0:T(128)S(1)}, f32[128]{0:T(128)}, u32[]{:S(2)}) copy-start(f32[128]{0:T(128)} %param.10) | copy-start | bytes 1540
  56.7 2.8 %collective-permute-start.9 = (bf16[4,512,128]{2,1,0:T(8,128)(2,1)S(1)}, bf16[4,512,128]{2,1,0:T(8,128)(2,1)S(1)}, u32[]{:S(2)}, u32[]{:S(2)}) collective-permute-start(bf16[4,512,128]{2,1,0:T(8,128)(2,1)S(1)} %get-tuple-element.74), channel_id=1, source_target_pairs={{0,8},{8,0},{16,24},{24,16},{32,40},{40,32},{48,56},{56,48},{64,72... | collective-permute-start | bytes 1572872 | tf_op jit(solution)/shard_map/ppermute | solution.py:440
  58.0 2.3 %collective-permute-start.10 = (bf16[4,512,128]{2,1,0:T(8,128)(2,1)S(1)}, bf16[4,512,128]{2,1,0:T(8,128)(2,1)S(1)}, u32[]{:S(2)}, u32[]{:S(2)}) collective-permute-start(bf16[4,512,128]{2,1,0:T(8,128)(2,1)S(1)} %get-tuple-element.75), channel_id=1, source_target_pairs={{0,8},{8,0},{16,24},{24,16},{32,40},{40,32},{48,56},{56,48},{64,72... | collective-permute-start | bytes 1572872 | tf_op jit(solution)/shard_map/ppermute | solution.py:440
  60.5 13.5 %collective-permute-start.11 = (bf16[512,128]{1,0:T(8,128)(2,1)S(1)}, bf16[512,128]{1,0:T(8,128)(2,1)S(1)}, u32[]{:S(2)}, u32[]{:S(2)}) collective-permute-start(bf16[512,128]{1,0:T(8,128)(2,1)S(1)} %get-tuple-element.77), channel_id=1, source_target_pairs={{0,16},{8,24},{16,0},{24,8},{32,48},{40,56},{48,32},{56,40},{64,80... | collective-permute-start | bytes 393224 | tf_op jit(solution)/shard_map/ppermute | solution.py:464
  64.3 11.1 %collective-permute-start.12 = (bf16[512,128]{1,0:T(8,128)(2,1)S(1)}, bf16[512,128]{1,0:T(8,128)(2,1)S(1)}, u32[]{:S(2)}, u32[]{:S(2)}) collective-permute-start(bf16[512,128]{1,0:T(8,128)(2,1)S(1)} %get-tuple-element.78), channel_id=1, source_target_pairs={{0,32},{8,40},{16,48},{24,56},{32,64},{40,72},{48,80},{56,88},{64,... | collective-permute-start | bytes 393224 | tf_op jit(solution)/shard_map/ppermute | solution.py:464
  65.2 12.5 %collective-permute-start.13 = (bf16[512,128]{1,0:T(8,128)(2,1)S(1)}, bf16[512,128]{1,0:T(8,128)(2,1)S(1)}, u32[]{:S(2)}, u32[]{:S(2)}) collective-permute-start(bf16[512,128]{1,0:T(8,128)(2,1)S(1)} %get-tuple-element.79), channel_id=1, source_target_pairs={{0,48},{8,56},{16,32},{24,40},{32,80},{40,88},{48,64},{56,72},{64,... | collective-permute-start | bytes 393224 | tf_op jit(solution)/shard_map/ppermute | solution.py:464
  68.5 12.0 %collective-permute-start.14 = (bf16[512,128]{1,0:T(8,128)(2,1)S(1)}, bf16[512,128]{1,0:T(8,128)(2,1)S(1)}, u32[]{:S(2)}, u32[]{:S(2)}) collective-permute-start(bf16[512,128]{1,0:T(8,128)(2,1)S(1)} %get-tuple-element.80), channel_id=1, source_target_pairs={{0,64},{8,72},{16,80},{24,88},{32,96},{40,104},{48,112},{56,120},{... | collective-permute-start | bytes 393224 | tf_op jit(solution)/shard_map/ppermute | solution.py:464
  68.5 16.0 %collective-permute-start.15 = (bf16[512,128]{1,0:T(8,128)(2,1)S(1)}, bf16[512,128]{1,0:T(8,128)(2,1)S(1)}, u32[]{:S(2)}, u32[]{:S(2)}) collective-permute-start(bf16[512,128]{1,0:T(8,128)(2,1)S(1)} %get-tuple-element.81), channel_id=1, source_target_pairs={{0,80},{8,88},{16,64},{24,72},{32,112},{40,120},{48,96},{56,104},{... | collective-permute-start | bytes 393224 | tf_op jit(solution)/shard_map/ppermute | solution.py:464
  74.1 10.5 %collective-permute-start.16 = (bf16[512,128]{1,0:T(8,128)(2,1)S(1)}, bf16[512,128]{1,0:T(8,128)(2,1)S(1)}, u32[]{:S(2)}, u32[]{:S(2)}) collective-permute-start(bf16[512,128]{1,0:T(8,128)(2,1)S(1)} %get-tuple-element.82), channel_id=1, source_target_pairs={{0,96},{8,104},{16,112},{24,120},{32,0},{40,8},{48,16},{56,24},{64... | collective-permute-start | bytes 393224 | tf_op jit(solution)/shard_map/ppermute | solution.py:464
  75.4 15.2 %collective-permute-start.17 = (bf16[512,128]{1,0:T(8,128)(2,1)S(1)}, bf16[512,128]{1,0:T(8,128)(2,1)S(1)}, u32[]{:S(2)}, u32[]{:S(2)}) collective-permute-start(bf16[512,128]{1,0:T(8,128)(2,1)S(1)} %get-tuple-element.83), channel_id=1, source_target_pairs={{0,112},{8,120},{16,96},{24,104},{32,16},{40,24},{48,0},{56,8},{64... | collective-permute-start | bytes 393224 | tf_op jit(solution)/shard_map/ppermute | solution.py:464
  77.7 13.0 %collective-permute-start.24 = (bf16[256,256]{1,0:T(8,128)(2,1)S(1)}, bf16[256,256]{1,0:T(8,128)(2,1)S(1)}, u32[]{:S(2)}, u32[]{:S(2)}) collective-permute-start(bf16[256,256]{1,0:T(8,128)(2,1)S(1)} %get-tuple-element.99.rest_0_), channel_id=1, source_target_pairs={{0,112},{8,120},{16,96},{24,104},{32,16},{40,24},{48,0},{56,8},{64... | collective-permute-start | bytes 393224 | tf_op jit(solution)/shard_map/ppermute | solution.py:464
  80.5 10.2 %collective-permute-start.23 = (bf16[256,256]{1,0:T(8,128)(2,1)S(1)}, bf16[256,256]{1,0:T(8,128)(2,1)S(1)}, u32[]{:S(2)}, u32[]{:S(2)}) collective-permute-start(bf16[256,256]{1,0:T(8,128)(2,1)S(1)} %get-tuple-element.99.rest_0_), channel_id=1, source_target_pairs={{0,96},{8,104},{16,112},{24,120},{32,0},{40,8},{48,16},{56,24},{64... | collective-permute-start | bytes 393224 | tf_op jit(solution)/shard_map/ppermute | solution.py:464
  84.6 12.8 %collective-permute-start.22 = (bf16[256,256]{1,0:T(8,128)(2,1)S(1)}, bf16[256,256]{1,0:T(8,128)(2,1)S(1)}, u32[]{:S(2)}, u32[]{:S(2)}) collective-permute-start(bf16[256,256]{1,0:T(8,128)(2,1)S(1)} %get-tuple-element.99.rest_0_), channel_id=1, source_target_pairs={{0,80},{8,88},{16,64},{24,72},{32,112},{40,120},{48,96},{56,104},{... | collective-permute-start | bytes 393224 | tf_op jit(solution)/shard_map/ppermute | solution.py:464
  84.6 12.8 %collective-permute-start.21 = (bf16[256,256]{1,0:T(8,128)(2,1)S(1)}, bf16[256,256]{1,0:T(8,128)(2,1)S(1)}, u32[]{:S(2)}, u32[]{:S(2)}) collective-permute-start(bf16[256,256]{1,0:T(8,128)(2,1)S(1)} %get-tuple-element.99.rest_0_), channel_id=1, source_target_pairs={{0,64},{8,72},{16,80},{24,88},{32,96},{40,104},{48,112},{56,120},{... | collective-permute-start | bytes 393224 | tf_op jit(solution)/shard_map/ppermute | solution.py:464
  90.6 8.7 %collective-permute-start.20 = (bf16[256,256]{1,0:T(8,128)(2,1)S(1)}, bf16[256,256]{1,0:T(8,128)(2,1)S(1)}, u32[]{:S(2)}, u32[]{:S(2)}) collective-permute-start(bf16[256,256]{1,0:T(8,128)(2,1)S(1)} %get-tuple-element.99.rest_0_), channel_id=1, source_target_pairs={{0,48},{8,56},{16,32},{24,40},{32,80},{40,88},{48,64},{56,72},{64,... | collective-permute-start | bytes 393224 | tf_op jit(solution)/shard_map/ppermute | solution.py:464
  90.7 8.9 %collective-permute-start.19 = (bf16[256,256]{1,0:T(8,128)(2,1)S(1)}, bf16[256,256]{1,0:T(8,128)(2,1)S(1)}, u32[]{:S(2)}, u32[]{:S(2)}) collective-permute-start(bf16[256,256]{1,0:T(8,128)(2,1)S(1)} %get-tuple-element.99.rest_0_), channel_id=1, source_target_pairs={{0,32},{8,40},{16,48},{24,56},{32,64},{40,72},{48,80},{56,88},{64,... | collective-permute-start | bytes 393224 | tf_op jit(solution)/shard_map/ppermute | solution.py:464
  90.7 9.3 %collective-permute-start.18 = (bf16[256,256]{1,0:T(8,128)(2,1)S(1)}, bf16[256,256]{1,0:T(8,128)(2,1)S(1)}, u32[]{:S(2)}, u32[]{:S(2)}) collective-permute-start(bf16[256,256]{1,0:T(8,128)(2,1)S(1)} %get-tuple-element.99.rest_0_), channel_id=1, source_target_pairs={{0,16},{8,24},{16,0},{24,8},{32,48},{40,56},{48,32},{56,40},{64,80... | collective-permute-start | bytes 393224 | tf_op jit(solution)/shard_map/ppermute | solution.py:464
  100.1 20.2 %all-to-all-start.1 = ((bf16[8,288,256]{2,1,0:T(8,128)(2,1)}), bf16[8,288,256]{2,1,0:T(8,128)(2,1)S(1)}, u32[]{:S(2)}, u32[]{:S(2)}) async-start(bf16[8,288,256]{2,1,0:T(8,128)(2,1)} %get-tuple-element.90), calls=%async_computation.1 | async-start | bytes 2359296 | tf_op jit(solution)/shard_map/all_to_all | solution.py:444
  106.6 1.3 collective-permute-start.25
  106.6 1.5 collective-permute-start.26
  107.1 1.4 collective-permute-start.27
  107.2 1.5 collective-permute-start.28
  107.6 1.3 collective-permute-start.29
  107.9 1.3 collective-permute-start.30
  108.1 1.3 collective-permute-start.31
  108.4 1.3 collective-permute-start.32
  120.2 2.8 %collective-permute-start.33 = (bf16[8,288,256]{2,1,0:T(8,128)(2,1)S(1)}, bf16[8,288,256]{2,1,0:T(8,128)(2,1)S(1)}, u32[]{:S(2)}, u32[]{:S(2)}) collective-permute-start(bf16[8,288,256]{2,1,0:T(8,128)(2,1)S(1)} %all-to-all-done.1.rest_16_), channel_id=1, source_target_pairs={{0,8},{8,0},{16,24},{24,16},{32,40},{40,32},{48,56},{56,48},{64,72... | collective-permute-start | bytes 3538952 | tf_op jit(solution)/shard_map/ppermute | solution.py:440
  126.7 2.0 %copy-start = (bf16[8192,256]{1,0:T(8,128)(2,1)}, bf16[8192,256]{1,0:T(8,128)(2,1)S(1)}, u32[]{:S(2)}) copy-start(bf16[8192,256]{1,0:T(8,128)(2,1)S(1)} %get-tuple-element.118.rest_0_) | copy-start | bytes 12582916
  128.7 36.6 %all-to-all-start.2 = ((bf16[8,288,256]{2,1,0:T(8,128)(2,1)}), bf16[8,288,256]{2,1,0:T(8,128)(2,1)S(1)}, u32[]{:S(2)}, u32[]{:S(2)}) async-start(bf16[8,288,256]{2,1,0:T(8,128)(2,1)} %get-tuple-element.116), calls=%async_computation.2 | async-start | bytes 2359296 | tf_op jit(solution)/shard_map/all_to_all | solution.py:448
  137.5 2.2 %copy-start.1 = (bf16[8192,256]{1,0:T(8,128)(2,1)S(1)}, bf16[8192,256]{1,0:T(8,128)(2,1)}, u32[]{:S(2)}) copy-start(bf16[8192,256]{1,0:T(8,128)(2,1)} %copy-done) | copy-start | bytes 12582916
  142.6 15.0 %collective-permute-start.34 = (bf16[256,256]{1,0:T(8,128)(2,1)S(1)}, bf16[256,256]{1,0:T(8,128)(2,1)S(1)}, u32[]{:S(2)}, u32[]{:S(2)}) collective-permute-start(bf16[256,256]{1,0:T(8,128)(2,1)S(1)} %get-tuple-element.120), channel_id=1, source_target_pairs={{0,1},{1,0},{2,3},{3,2},{4,5},{5,4},{6,7},{7,6},{8,9},{9,8},{10,11... | collective-permute-start | bytes 393224 | tf_op jit(solution)/shard_map/ppermute | solution.py:456
  144.4 18.2 %collective-permute-start.35 = (bf16[256,256]{1,0:T(8,128)(2,1)S(1)}, bf16[256,256]{1,0:T(8,128)(2,1)S(1)}, u32[]{:S(2)}, u32[]{:S(2)}) collective-permute-start(bf16[256,256]{1,0:T(8,128)(2,1)S(1)} %get-tuple-element.121), channel_id=1, source_target_pairs={{0,2},{1,3},{2,4},{3,5},{4,6},{5,7},{6,0},{7,1},{8,10},{9,11},{10,... | collective-permute-start | bytes 393224 | tf_op jit(solution)/shard_map/ppermute | solution.py:456
  148.1 24.5 %collective-permute-start.36 = (bf16[256,256]{1,0:T(8,128)(2,1)S(1)}, bf16[256,256]{1,0:T(8,128)(2,1)S(1)}, u32[]{:S(2)}, u32[]{:S(2)}) collective-permute-start(bf16[256,256]{1,0:T(8,128)(2,1)S(1)} %get-tuple-element.122), channel_id=1, source_target_pairs={{0,3},{1,2},{2,5},{3,4},{4,7},{5,6},{6,1},{7,0},{8,11},{9,10},{10,... | collective-permute-start | bytes 393224 | tf_op jit(solution)/shard_map/ppermute | solution.py:456
  148.3 24.3 %collective-permute-start.37 = (bf16[256,256]{1,0:T(8,128)(2,1)S(1)}, bf16[256,256]{1,0:T(8,128)(2,1)S(1)}, u32[]{:S(2)}, u32[]{:S(2)}) collective-permute-start(bf16[256,256]{1,0:T(8,128)(2,1)S(1)} %get-tuple-element.123), channel_id=1, source_target_pairs={{0,4},{1,5},{2,6},{3,7},{4,0},{5,1},{6,2},{7,3},{8,12},{9,13},{10,... | collective-permute-start | bytes 393224 | tf_op jit(solution)/shard_map/ppermute | solution.py:456
  151.7 20.9 %collective-permute-start.38 = (bf16[256,256]{1,0:T(8,128)(2,1)S(1)}, bf16[256,256]{1,0:T(8,128)(2,1)S(1)}, u32[]{:S(2)}, u32[]{:S(2)}) collective-permute-start(bf16[256,256]{1,0:T(8,128)(2,1)S(1)} %get-tuple-element.124), channel_id=1, source_target_pairs={{0,5},{1,4},{2,7},{3,6},{4,1},{5,0},{6,3},{7,2},{8,13},{9,12},{10,... | collective-permute-start | bytes 393224 | tf_op jit(solution)/shard_map/ppermute | solution.py:456
  157.7 14.9 %collective-permute-start.39 = (bf16[256,256]{1,0:T(8,128)(2,1)S(1)}, bf16[256,256]{1,0:T(8,128)(2,1)S(1)}, u32[]{:S(2)}, u32[]{:S(2)}) collective-permute-start(bf16[256,256]{1,0:T(8,128)(2,1)S(1)} %get-tuple-element.125), channel_id=1, source_target_pairs={{0,6},{1,7},{2,0},{3,1},{4,2},{5,3},{6,4},{7,5},{8,14},{9,15},{10,... | collective-permute-start | bytes 393224 | tf_op jit(solution)/shard_map/ppermute | solution.py:456
  162.6 10.0 %collective-permute-start.40 = (bf16[256,256]{1,0:T(8,128)(2,1)S(1)}, bf16[256,256]{1,0:T(8,128)(2,1)S(1)}, u32[]{:S(2)}, u32[]{:S(2)}) collective-permute-start(bf16[256,256]{1,0:T(8,128)(2,1)S(1)} %get-tuple-element.126), channel_id=1, source_target_pairs={{0,7},{1,6},{2,1},{3,0},{4,3},{5,2},{6,5},{7,4},{8,15},{9,14},{10,... | collective-permute-start | bytes 393224 | tf_op jit(solution)/shard_map/ppermute | solution.py:456
  166.2 14.4 %all-to-all-start.3 = ((f32[8,32,128]{2,1,0:T(8,128)}), f32[8,32,128]{2,1,0:T(8,128)S(1)}, u32[]{:S(2)}, u32[]{:S(2)}) async-start(f32[8,32,128]{2,1,0:T(8,128)} %get-tuple-element.127), calls=%async_computation.3 | async-start | bytes 262144 | tf_op jit(solution)/shard_map/all_to_all | solution.py:444

commit v3 on v2

--- a/solution.py
+++ b/solution.py
@@ -17,7 +17,7 @@
 LIST = 160
 UNROLL = 8
 DEPTH = 32
-EXTRA = 32
+EXTRA = 144
 FWD_DUMMY = 32
 BWD_DUMMY = 16
 f32, bf16 = jnp.float32, jnp.bfloat16
@@ -40,7 +40,7 @@
     return pl.BlockSpec(memory_space=pl.ANY)
 
 
-def prep_kernel(where_ref, out_ref, in_ref, count_ref, lists_ref, sizes_ref):
+def prep_kernel(where_ref, out_ref, in_ref, count_ref, lists_ref):
     x, yh, core, z, y = (where_ref[i] for i in range(5))
 
     def clear(i, carry):
@@ -66,7 +66,7 @@
         j_t = t >> 3
         src_f = ((((z - z_s) & 3) * 2 + dy_col) << 2) + (s & 3)
         to_t = jnp.where(half_t == 0, j_t, ((x_t - x) & 3) * 2 + dy_row)
-        from_t = jnp.where(half_t == 0, ((x - x_t) & 3) * 2 + dy_row, j_t)
+        from_t = jnp.where(half_t == 0, j_t, ((x - x_t) & 3) * 2 + dy_row)
         dst_f = rel * 16 + to_t * 2 + sub_t
         src_b = ((half_t * 2 + rel) * NPEER + from_t) * 2 + sub_t
         to_s = jnp.where(half_s == 0, s >> 2, ((z_s - z) & 3) * 2 + dy_col)
@@ -85,25 +85,22 @@
     zero = jnp.int32(0)
     sizes = lax.fori_loop(0, count_ref[0], place, (zero, zero, zero, zero))
     for i in range(4):
-        sizes_ref[i] = sizes[i]
+        lists_ref[4 * LIST + i] = sizes[i]
 
 
 def prep(where, out_index, in_index, count):
     return pl.pallas_call(
         prep_kernel,
-        out_shape=(
-            jax.ShapeDtypeStruct((4 * LIST,), jnp.int32),
-            jax.ShapeDtypeStruct((4,), jnp.int32),
-        ),
+        out_shape=jax.ShapeDtypeStruct((1024,), jnp.int32),
         in_specs=[smem()] * 4,
-        out_specs=(smem(), smem()),
+        out_specs=smem(),
         name="slot_lists",
     )(where, out_index, in_index, count)
 
 
-def tile_loop(which, lists_ref, sizes_ref, vals, buf, sems, acc, ready, product):
+def tile_loop(which, lists_ref, vals, buf, sems, acc, ready, product):
     base = which * LIST
-    groups = (sizes_ref[which] + (UNROLL - 1)) // UNROLL
+    groups = (lists_ref[4 * LIST + which] + (UNROLL - 1)) // UNROLL
     ahead = DEPTH // UNROLL
 
     def copy(g, u):
@@ -150,10 +147,12 @@
 )
 
 
-def forward_kernel(half, lists_ref, sizes_ref, vals, *rest):
+def forward_kernel(half, lists_ref, vals, *rest):
     blocks = rest[:NPEER]
     mine_ref, *others = rest[NPEER : NPEER + 3]
-    x, buf, acc, sems = rest[NPEER + 3 :]
+    x, buf, acc, sems, own_sem = rest[NPEER + 3 :]
+    own = pltpu.make_async_copy(blocks[0], x.at[pl.ds(0, 4 * TILE)], own_sem)
+    own.start()
 
     def ready():
         def clear(i, carry):
@@ -161,14 +160,15 @@
             return carry
 
         lax.fori_loop(0, FWD_DUMMY, clear, 0)
-        for k in range(NPEER):
+        for k in range(1, NPEER):
             x[pl.ds(k * 4 * TILE, 4 * TILE), :] = blocks[k][...]
+        own.wait()
 
     def product(tile, source):
         rows = x[pl.ds(pl.multiple_of(source * TILE, TILE), TILE), :]
         return jnp.dot(tile, rows, preferred_element_type=f32)
 
-    tile_loop(half, lists_ref, sizes_ref, vals, buf, sems, acc, ready, product)
+    tile_loop(half, lists_ref, vals, buf, sems, acc, ready, product)
 
     for i in range(2 * NPEER):
         peer, rows = i // 2, pl.ds((i % 2) * TILE, TILE)
@@ -176,24 +176,25 @@
         others[peer // 4][peer % 4, rows, :] = acc[16 + i].astype(bf16)
 
 
-def forward(half, lists, sizes, values, blocks):
+def forward(half, lists, values, blocks):
     shape = jax.ShapeDtypeStruct((NPEER, 2 * TILE, FEAT), bf16)
     piece = jax.ShapeDtypeStruct((NPEER // 2, 2 * TILE, FEAT), bf16)
     return pl.pallas_call(
         functools.partial(forward_kernel, half),
         out_shape=(shape, piece, piece),
-        in_specs=[smem(), smem(), hbm()] + [vmem()] * NPEER,
+        in_specs=[smem(), hbm(), hbm()] + [vmem()] * (NPEER - 1),
         out_specs=(vmem(), vmem(), vmem()),
         scratch_shapes=[
             pltpu.VMEM((NPEER * 4 * TILE, FEAT), bf16),
             pltpu.VMEM((DEPTH, TILE, TILE), bf16),
             pltpu.VMEM((FWD_DUMMY + 1, TILE, FEAT), f32),
             pltpu.SemaphoreType.DMA((DEPTH,)),
+            pltpu.SemaphoreType.DMA,
         ],
         compiler_params=params(),
         cost_estimate=TILES_COST,
         name="forward_tiles",
-    )(lists, sizes, in_hbm(values), *blocks)
+    )(in_hbm(lists), in_hbm(values), in_hbm(blocks[0]), *blocks[1:])
 
 
 def pair_sum_kernel(half, mine_ref, low_ref, high_ref, *outs):
@@ -230,14 +231,17 @@
     return jnp.concatenate([high, low], axis=1)
 
 
-def backward_kernel(half, lists_ref, sizes_ref, vals, *rest):
+def backward_kernel(half, lists_ref, vals, *rest):
     rows2 = 2 * FEAT
     if half == 0:
-        shifted, swapped = rest[: 2 * NPEER], rest[2 * NPEER : 2 * NPEER + 2]
-        out_ref, g, buf, acc, sems = rest[2 * NPEER + 2 :]
-    else:
-        g, *outs = rest[: 1 + NPEER]
-        buf, acc, sems = rest[1 + NPEER :]
+        swapped, shifted = rest[:2], rest[2 : 2 + 2 * NPEER]
+        out_ref, kept, g, buf, acc, sems, g_sem = rest[2 + 2 * NPEER :]
+        keep = pltpu.make_async_copy(g, kept, g_sem)
+    else:
+        kept, *outs = rest[: 1 + NPEER]
+        g, buf, acc, sems, g_sem = rest[1 + NPEER :]
+        keep = pltpu.make_async_copy(kept, g, g_sem)
+        keep.start()
 
     def ready():
         def clear(i, carry):
@@ -246,18 +250,21 @@
 
         lax.fori_loop(0, BWD_DUMMY, clear, 0)
         if half == 0:
-            for i in range(2 * NPEER):
-                g[pl.ds(i * rows2, rows2), :] = shifted[i][...]
             for p in range(2):
                 for peer in range(NPEER):
-                    i = (2 + p) * NPEER + peer
-                    g[pl.ds(i * rows2, rows2), :] = swapped[p][peer, pl.ds(0, rows2), :]
+                    i = p * NPEER + peer
+                    g[pl.ds(i * rows2, rows2), :] = swapped[p][peer]
+            for i in range(2 * NPEER):
+                g[pl.ds((2 * NPEER + i) * rows2, rows2), :] = shifted[i][pl.ds(0, rows2), :]
+            keep.start()
+        else:
+            keep.wait()
 
     def product(tile, source):
         rows = g[pl.ds(pl.multiple_of(source * FEAT, FEAT), FEAT), :]
         return jnp.dot(rows, tile, preferred_element_type=f32)
 
-    tile_loop(2 + half, lists_ref, sizes_ref, vals, buf, sems, acc, ready, product)
+    tile_loop(2 + half, lists_ref, vals, buf, sems, acc, ready, product)
 
     for i in range(2 * NPEER):
         rows = pl.ds((i % 2) * FEAT, FEAT)
@@ -266,40 +273,49 @@
         else:
             outs[i // 2][rows, :] = acc[i].astype(bf16)
     if half == 0:
-        sums = []
-        for p in range(2):
-            total = jnp.zeros((EXTRA, FEAT), f32)
-            for peer in range(NPEER):
-                pair = swapped[p][peer, pl.ds(rows2, EXTRA), :].astype(f32)
-                total += pair[:, :FEAT] + pair[:, FEAT:]
-            sums.append(total)
-        packed = split_lanes(sums[0] + sums[1])
+        total = None
+        for k in range(NPEER):
+            pair = [
+                shifted[i][pl.ds(rows2, EXTRA), :].astype(f32) for i in (k, NPEER + k)
+            ]
+            pair = [v[:, :FEAT] + v[:, FEAT:] for v in pair]
+            total = pair[0] + pair[1] if total is None else total + (pair[0] + pair[1])
+        packed = split_lanes(total)
         for peer in range(NPEER):
             out_ref[peer, pl.ds(rows2, EXTRA), :] = packed
-
-
-def backward(half, lists, sizes, values, grads):
+        keep.wait()
+
+
+def backward(half, lists, values, grads):
+    blocks = pltpu.HBM((4 * 2 * NPEER * FEAT, TILE), bf16)
     if half == 0:
         out_shape = (
             jax.ShapeDtypeStruct((NPEER, 2 * FEAT + EXTRA, TILE), bf16),
-            jax.ShapeDtypeStruct((4 * 2 * NPEER * FEAT, TILE), bf16),
+            blocks,
         )
+        out_specs = (vmem(), pl.BlockSpec(memory_space=pltpu.HBM))
+        in_specs = [vmem()] * len(grads)
     else:
         out_shape = (jax.ShapeDtypeStruct((2 * FEAT, TILE), bf16),) * NPEER
+        out_specs = (vmem(),) * NPEER
+        in_specs = [hbm()]
+        grads = [in_hbm(g) for g in grads]
     return pl.pallas_call(
         functools.partial(backward_kernel, half),
         out_shape=out_shape,
-        in_specs=[smem(), smem(), hbm()] + [vmem()] * len(grads),
-        out_specs=(vmem(),) * len(out_shape),
+        in_specs=[smem(), hbm()] + in_specs,
+        out_specs=out_specs,
         scratch_shapes=[
+            pltpu.VMEM(blocks.shape, bf16),
             pltpu.VMEM((DEPTH, TILE, TILE), bf16),
             pltpu.VMEM((BWD_DUMMY + 1, FEAT, TILE), f32),
             pltpu.SemaphoreType.DMA((DEPTH,)),
+            pltpu.SemaphoreType.DMA,
         ],
         compiler_params=params(),
         cost_estimate=TILES_COST,
         name="backward_tiles",
-    )(lists, sizes, in_hbm(values), *grads)
+    )(in_hbm(lists), in_hbm(values), *grads)
 
 
 def dense_kernel(half, weight_ref, bias_ref, cot_ref, *rest):
@@ -327,19 +343,16 @@
     for sub in range(2):
         rows = pl.ds(sub * FEAT, FEAT)
         if half == 0:
-            grad_ref[rows, :] = back[:, sub * TILE : (sub + 1) * TILE]
-        else:
             for peer in range(NPEER):
                 grad_ref[peer, rows, :] = back[:, sub * TILE : (sub + 1) * TILE]
+        else:
+            grad_ref[rows, :] = back[:, sub * TILE : (sub + 1) * TILE]
     if half == 0:
         wsum_ref[pl.ds(0, FEAT), :] = wsum
         wsum_ref[pl.ds(FEAT, 16), :] = bsum
     else:
-        wpack = split_lanes(wsum + before_ref[pl.ds(0, FEAT), :])
-        bpack = split_lanes(bsum + before_ref[pl.ds(FEAT, 16), :])
-        for peer in range(NPEER):
-            grad_ref[peer, pl.ds(2 * FEAT, 16), :] = wpack[peer * 16 : peer * 16 + 16]
-            grad_ref[peer, pl.ds(2 * FEAT + 16, 16), :] = bpack
+        grad_ref[pl.ds(2 * FEAT, FEAT), :] = split_lanes(wsum + before_ref[pl.ds(0, FEAT), :])
+        grad_ref[pl.ds(3 * FEAT, 16), :] = split_lanes(bsum + before_ref[pl.ds(FEAT, 16), :])
 
 
 def dense(half, recv, weight, bias, cotangent, before=None, hidden=None):
@@ -354,13 +367,13 @@
     operands = [weight, bias, cotangent]
     aliases = {}
     if half == 0:
-        grad = (2 * FEAT, TILE)
+        grad = (NPEER, 2 * FEAT, TILE)
         in_specs += [whole(NPEER, 2 * TILE, FEAT)]
         operands += [recv]
         out_shape = (hidden_shape, jax.ShapeDtypeStruct(grad, bf16), wsum_shape)
         out_specs = (half_rows, whole(*grad), whole(FEAT + 16, FEAT))
     else:
-        grad = (NPEER, 2 * FEAT + EXTRA, TILE)
+        grad = (2 * FEAT + EXTRA, TILE)
         in_specs += [whole(FEAT + 16, FEAT), hbm()] + [whole(2 * TILE, FEAT)] * NPEER
         operands += [before, hidden, *recv]
         out_shape = (hidden_shape, jax.ShapeDtypeStruct(grad, bf16))
@@ -383,7 +396,7 @@
 
 def last_kernel(half, scale, *rest):
     if half == 0:
-        recv_ref, grad_ref, slice_ref = rest
+        recv_ref, grad_ref, weight_ref, bias_ref = rest
         parts = [recv_ref.at[peer] for peer in range(NPEER)]
     else:
         parts = rest[1 : 1 + NPEER]
@@ -400,8 +413,8 @@
             pair = recv_ref[peer, pl.ds(2 * FEAT, EXTRA), :].astype(f32)
             total += pair[:, :FEAT] + pair[:, FEAT:]
         total = total * scale
-        for peer in range(NPEER):
-            slice_ref[peer] = total
+        weight_ref[...] = total[:FEAT]
+        bias_ref[...] = total[FEAT : FEAT + 1]
 
 
 def last(half, scale, recv, grad=None):
@@ -411,8 +424,9 @@
     if half == 0:
         in_specs = [pl.BlockSpec(recv.shape, lambda i: (0, 0, 0))]
         operands = [recv]
-        out_shape = (grad_shape, jax.ShapeDtypeStruct((NPEER, EXTRA, FEAT), f32))
-        out_specs = (half_rows, pl.BlockSpec((NPEER, EXTRA, FEAT), lambda i: (0, 0, 0)))
+        sums = [(FEAT, FEAT), (1, FEAT)]
+        out_shape = (grad_shape, *[jax.ShapeDtypeStruct(s, f32) for s in sums])
+        out_specs = (half_rows, *[pl.BlockSpec(s, lambda i: (0, 0)) for s in sums])
     else:
         in_specs = [hbm()] + [pl.BlockSpec((2 * FEAT, TILE), lambda i: (0, 0))] * NPEER
         operands = [grad, *recv]
@@ -468,40 +482,36 @@
     values = tile_vals[0, 0]
     row, col = lax.axis_index("row"), lax.axis_index("col")
     where = jnp.stack([row >> 2, (row >> 1) & 1, row & 1, col >> 1, col & 1]).astype(jnp.int32)
-    lists, sizes = prep(where, tile_out[0, 0], tile_in[0, 0], tile_count[0])
+    lists = prep(where, tile_out[0, 0], tile_in[0, 0], tile_count[0])
     bias = layer_bias.reshape(1, FEAT)
     order = lax.optimization_barrier
 
     blocks = [features] + [col_shift(features, k) for k in range(1, NPEER)]
 
-    mine, low, high = forward(0, lists, sizes, values, blocks)
+    mine, low, high = forward(0, lists, values, blocks)
     both = pair_sum(0, mine, to_other_core(low), to_other_core(high))
     both, lists = order((both, lists))
     swapped = row_exchange(both)
-    mine, low, high = forward(1, lists, sizes, values, blocks)
+    mine, low, high = forward(1, lists, values, blocks)
     chunks = pair_sum(1, mine, to_other_core(low), to_other_core(high))
     shifted = [chunks[0]] + [row_shift(chunks[k], k) for k in range(1, NPEER)]
 
-    swapped = order((swapped, *chunks))[0]
+    swapped, *shifted[1:4] = order((swapped, *shifted[1:4]))
     hidden, grad, wsum = dense(0, swapped, weight, bias, cotangent)
+    swapped = row_exchange(grad)
+    hidden, grad = dense(1, shifted, weight, bias, cotangent, wsum, hidden)
     grads = [grad] + [row_shift(grad, k) for k in range(1, NPEER)]
-    hidden, grad = dense(1, shifted, weight, bias, cotangent, wsum, hidden)
-    grad, *grads = order((grad, *grads))
-    swapped = row_exchange(grad)
-    grads += [to_other_core(g) for g in grads]
-    swapped, *grads = order((swapped, *grads))
-    grads += [swapped, to_other_core(swapped)]
-
-    back, grads = backward(0, lists, sizes, values, grads)
+    swapped, *grads[1:6] = order((swapped, *grads[1:6]))
+    grads = [swapped, to_other_core(swapped)] + grads + [to_other_core(g) for g in grads]
+
+    back, grads = backward(0, lists, values, grads)
     back0 = col_exchange(back)
-    chunks = backward(1, lists, sizes, values, [grads])
+    chunks = backward(1, lists, values, [grads])
     back1 = [chunks[0]] + [col_shift(chunks[k], k) for k in range(1, NPEER)]
     scale = 1.0 / math.sqrt(4 * TILE * 128)
-    feature_grad, wslice = last(0, scale, back0)
-    slices = row_exchange(wslice)
+    feature_grad, weight_grad, bias_grad = last(0, scale, back0)
     feature_grad = last(1, scale, back1, feature_grad)
-    weight_grad = slices[:, :16].reshape(FEAT, FEAT)
-    bias_grad = slices[0, 16]
+    bias_grad = bias_grad.reshape(FEAT)
     return (hidden, feature_grad, weight_grad, bias_grad)
 
 

time: 181 us -> 200 us (1.10)
  waiting for transfers between devices: 57.9 us -> 83.4 us
  Pallas kernels: 21.6 us -> 41.2 us
  starting transfers between devices: 92.2 us -> 73.1 us
  local copies, waits for them, and re-layouts: 8.29 us -> 0.64 us
    ppermute x14, waiting for transfers between devices: 4.3 us -> 44.8 us  [row_shift(): return lax.ppermute(value, 'row', pairs)]
    all_to_all x3 -> x2, waiting for transfers between devices: 17.4 us -> 0.01 us  [row_exchange(): return lax.all_to_all(value, 'row', 0, 0, axis_index_groups=SAME_CORE)]
    all_to_all x3 -> x2, starting transfers between devices: 20.3 us -> 9.57 us  [row_exchange(): return lax.all_to_all(value, 'row', 0, 0, axis_index_groups=SAME_CORE)]
    pallas_call x2, Pallas kernels: 6.59 us -> 14.9 us  [backward(): pl.pallas_call(functools.partial(backward_kernel, half), out_shape=out_sh...]
    pallas_call x2, Pallas kernels: 6.06 us -> 14.3 us  [forward(): pl.pallas_call(functools.partial(forward_kernel, half), out_shape=(shape,...]
    unnamed x22 -> x6, local copies, waits for them, and re-layouts: 6.48 us -> 0.02 us
    ppermute x14, waiting for transfers between devices: 27.6 us -> 32.4 us  [col_shift(): return lax.ppermute(value, 'col', pairs)]
    ppermute x14, starting transfers between devices: 32.6 us -> 29.2 us  [row_shift(): return lax.ppermute(value, 'row', pairs)]
  transfers between devices with their start and end apart: 45 -> 44, of which waited for: 21 -> 28; matrix products, arithmetic and copies ran while one was open for 0% -> 0% of each run, Pallas kernels for 7% -> 12%
where the time goes in v3:
time: 200 us
  waiting for transfers between devices  83.4 us (42%)
  starting transfers between devices  73.1 us (37%)
  Pallas kernels  41.2 us (21%)
    ppermute x14, waiting for transfers between devices, row_shift(): return lax.ppermute(value, 'row', pairs)  44.8 us
    ppermute x14, waiting for transfers between devices, col_shift(): return lax.ppermute(value, 'col', pairs)  32.4 us
    ppermute x14, starting transfers between devices, row_shift(): return lax.ppermute(value, 'row', pairs)  29.2 us
    ppermute x14, starting transfers between devices, col_shift(): return lax.ppermute(value, 'col', pairs)  23.8 us
    pallas_call x2, Pallas kernels, backward(): pl.pallas_call(functools.partial(backward_kernel, half), out_shape=out_sh...  14.9 us
    pallas_call x2, Pallas kernels, forward(): pl.pallas_call(functools.partial(forward_kernel, half), out_shape=(shape,...  14.3 us
    all_to_all x2, starting transfers between devices, row_exchange(): return lax.all_to_all(value, 'row', 0, 0, axis_index_groups=SAME_CORE)  9.57 us
    all_to_all x1, starting transfers between devices, col_exchange(): return lax.all_to_all(value, 'col', 0, 0)  7.95 us
  transfers between devices with their start and end apart: 44, of which 28 were waited for; matrix products, arithmetic and copies ran while one was open for 0% of the time, Pallas kernels for 12%

profile of v3, /device:TPU:0, one launch (start us, length us, event | category | flops | bytes accessed | tf_op | source)
XLA Modules:
  0.0 199.8 jit_solution(4007668428378536733)
XLA Ops:
  0.6 5.2 %collective-permute-start.6 = (bf16[1024,128]{1,0:T(8,128)(2,1)}, bf16[1024,128]{1,0:T(8,128)(2,1)S(1)}, u32[]{:S(2)}, u32[]{:S(2)}) collective-permute-start(bf16[1024,128]{1,0:T(8,128)(2,1)} %rest_0_.3), channel_id=1, source_target_pairs={{0,7},{1,6},{2,1},{3,0},{4,3},{5,2},{6,5},{7,4},{8,15},{9,14},{10,... | collective-permute-start | bytes 786440 | tf_op jit(solution)/shard_map/ppermute | solution.py:470
  6.2 3.4 %collective-permute-start.3 = (bf16[1024,128]{1,0:T(8,128)(2,1)}, bf16[1024,128]{1,0:T(8,128)(2,1)S(1)}, u32[]{:S(2)}, u32[]{:S(2)}) collective-permute-start(bf16[1024,128]{1,0:T(8,128)(2,1)} %rest_0_.3), channel_id=1, source_target_pairs={{0,4},{1,5},{2,6},{3,7},{4,0},{5,1},{6,2},{7,3},{8,12},{9,13},{10,... | collective-permute-start | bytes 786440 | tf_op jit(solution)/shard_map/ppermute | solution.py:470
  9.7 2.6 %collective-permute-start.2 = (bf16[1024,128]{1,0:T(8,128)(2,1)}, bf16[1024,128]{1,0:T(8,128)(2,1)S(1)}, u32[]{:S(2)}, u32[]{:S(2)}) collective-permute-start(bf16[1024,128]{1,0:T(8,128)(2,1)} %rest_0_.3), channel_id=1, source_target_pairs={{0,3},{1,2},{2,5},{3,4},{4,7},{5,6},{6,1},{7,0},{8,11},{9,10},{10,... | collective-permute-start | bytes 786440 | tf_op jit(solution)/shard_map/ppermute | solution.py:470
  12.3 1.8 collective-permute-done.6.rest_7_
  14.1 14.4 %collective-permute-done.5.rest_6_ = bf16[1024,128]{1,0:T(8,128)(2,1)S(1)} collective-permute-done((bf16[1024,128]{1,0:T(8,128)(2,1)}, bf16[1024,128]{1,0:T(8,128)(2,1)S(1)}, u32[]{:S(2)}, u32[]{:S(2)}) %collective-permute-start.5) | collective-permute-done | bytes 262176 | tf_op jit(solution)/shard_map/ppermute | solution.py:470
  28.5 0.8 collective-permute-start
  29.9 0.6 stack.23.where_ref
  30.5 6.2 %slot_lists.1.lists_ref = s32[1024]{0:T(1024)} custom-call(s32[5]{0:T(128)} %stack.23.where_ref, s32[128]{0:T(128)} %bitcast.18, s32[128]{0:T(128)} %bitcast.19, s32[1]{0:T(128)} %bitcast.11.count_ref), custom_call_target="tpu_custom_call" | custom-call | tf_op jit(solution)/shard_map/slot_lists/pallas_call | solution.py:92
  36.9 7.3 %forward_tiles.2 = (bf16[8,512,128]{2,1,0:T(8,128)(2,1)S(1)}, bf16[4,512,128]{2,1,0:T(8,128)(2,1)S(1)}, bf16[4,512,128]{2,1,0:T(8,128)(2,1)S(1)}) custom-call(s32[1024]{0:T(1024)} %slot_lists.1.lists_ref, bf16[128,256,256]{2,1,0:T(8,128)(2,1)} %bitcast.14, bf16[1024,128]{1,0:T(8,128)(2,1)} %rest_0_.3, bf16[1024,128]{1,0:T(8,128)(2,1)S(1)} %collective-permute-done.rest_1_, ...), custom_call_target="tpu_custom_call" | custom-call | flops 1073741824 | bytes 20971520 | tf_op jit(solution)/shard_map/forward_tiles/pallas_call | solution.py:182
  44.3 0.5 collective-permute-start.8
  44.7 1.4 collective-permute-done.7.low_ref
  46.1 0.7 collective-permute-done.8.high_ref
  46.9 1.3 pair_sum.2
  48.2 5.3 %all-to-all-start = ((bf16[8,512,128]{2,1,0:T(8,128)(2,1)}), bf16[8,512,128]{2,1,0:T(8,128)(2,1)S(1)}, u32[]{:S(2)}, u32[]{:S(2)}) async-start(bf16[8,512,128]{2,1,0:T(8,128)(2,1)} %pair_sum.2), calls=%async_computation | async-start | bytes 2097152 | tf_op jit(solution)/shard_map/all_to_all | solution.py:458
  53.5 7.0 %forward_tiles.3 = (bf16[8,512,128]{2,1,0:T(8,128)(2,1)S(1)}, bf16[4,512,128]{2,1,0:T(8,128)(2,1)S(1)}, bf16[4,512,128]{2,1,0:T(8,128)(2,1)S(1)}) custom-call(s32[1024]{0:T(1024)} %slot_lists.1.lists_ref, bf16[128,256,256]{2,1,0:T(8,128)(2,1)} %bitcast.15, bf16[1024,128]{1,0:T(8,128)(2,1)} %rest_0_.3, bf16[1024,128]{1,0:T(8,128)(2,1)S(1)} %collective-permute-done.rest_1_, ...), custom_call_target="tpu_custom_call" | custom-call | flops 1073741824 | bytes 20971520 | tf_op jit(solution)/shard_map/forward_tiles/pallas_call | solution.py:182
  60.6 0.5 collective-permute-start.10
  61.1 1.4 collective-permute-done.9.low_ref
  62.5 0.7 collective-permute-done.10.high_ref
  63.5 2.0 %collective-permute-start.11 = (bf16[512,128]{1,0:T(8,128)(2,1)S(1)}, bf16[512,128]{1,0:T(8,128)(2,1)S(1)}, u32[]{:S(2)}, u32[]{:S(2)}) collective-permute-start(bf16[512,128]{1,0:T(8,128)(2,1)S(1)} %get-tuple-element.56), channel_id=1, source_target_pairs={{0,16},{8,24},{16,0},{24,8},{32,48},{40,56},{48,32},{56,40},{64,80... | collective-permute-start | bytes 393224 | tf_op jit(solution)/shard_map/ppermute | solution.py:478
  65.5 1.8 collective-permute-start.12
  67.3 1.1 collective-permute-start.13
  68.4 4.0 %collective-permute-done.11.rest_3_ = bf16[512,128]{1,0:T(8,128)(2,1)S(1)} collective-permute-done((bf16[512,128]{1,0:T(8,128)(2,1)S(1)}, bf16[512,128]{1,0:T(8,128)(2,1)S(1)}, u32[]{:S(2)}, u32[]{:S(2)}) %collective-permute-start.11) | collective-permute-done | bytes 131104 | tf_op jit(solution)/shard_map/ppermute | solution.py:478
  72.4 1.1 collective-permute-done.12.rest_4_
  73.5 3.4 %collective-permute-done.13.rest_5_ = bf16[512,128]{1,0:T(8,128)(2,1)S(1)} collective-permute-done((bf16[512,128]{1,0:T(8,128)(2,1)S(1)}, bf16[512,128]{1,0:T(8,128)(2,1)S(1)}, u32[]{:S(2)}, u32[]{:S(2)}) %collective-permute-start.13) | collective-permute-done | bytes 131104 | tf_op jit(solution)/shard_map/ppermute | solution.py:478
  76.9 1.6 dense_layer.2
  78.5 4.3 %all-to-all-start.1 = ((bf16[8,256,256]{2,1,0:T(8,128)(2,1)}), bf16[8,256,256]{2,1,0:T(8,128)(2,1)S(1)}, u32[]{:S(2)}, u32[]{:S(2)}) async-start(bf16[8,256,256]{2,1,0:T(8,128)(2,1)} %get-tuple-element.71), calls=%async_computation.1 | async-start | bytes 2097152 | tf_op jit(solution)/shard_map/all_to_all | solution.py:458
  82.8 3.5 %collective-permute-start.14 = (bf16[512,128]{1,0:T(8,128)(2,1)S(1)}, bf16[512,128]{1,0:T(8,128)(2,1)S(1)}, u32[]{:S(2)}, u32[]{:S(2)}) collective-permute-start(bf16[512,128]{1,0:T(8,128)(2,1)S(1)} %get-tuple-element.66), channel_id=1, source_target_pairs={{0,64},{8,72},{16,80},{24,88},{32,96},{40,104},{48,112},{56,120},{... | collective-permute-start | bytes 393224 | tf_op jit(solution)/shard_map/ppermute | solution.py:478
  86.3 3.0 %collective-permute-start.15 = (bf16[512,128]{1,0:T(8,128)(2,1)S(1)}, bf16[512,128]{1,0:T(8,128)(2,1)S(1)}, u32[]{:S(2)}, u32[]{:S(2)}) collective-permute-start(bf16[512,128]{1,0:T(8,128)(2,1)S(1)} %get-tuple-element.67), channel_id=1, source_target_pairs={{0,80},{8,88},{16,64},{24,72},{32,112},{40,120},{48,96},{56,104},{... | collective-permute-start | bytes 393224 | tf_op jit(solution)/shard_map/ppermute | solution.py:478
  89.3 2.7 %collective-permute-start.16 = (bf16[512,128]{1,0:T(8,128)(2,1)S(1)}, bf16[512,128]{1,0:T(8,128)(2,1)S(1)}, u32[]{:S(2)}, u32[]{:S(2)}) collective-permute-start(bf16[512,128]{1,0:T(8,128)(2,1)S(1)} %get-tuple-element.68), channel_id=1, source_target_pairs={{0,96},{8,104},{16,112},{24,120},{32,0},{40,8},{48,16},{56,24},{64... | collective-permute-start | bytes 393224 | tf_op jit(solution)/shard_map/ppermute | solution.py:478
  92.0 0.9 collective-permute-start.17
  92.8 9.2 %collective-permute-done.14.rest_6_ = bf16[512,128]{1,0:T(8,128)(2,1)S(1)} collective-permute-done((bf16[512,128]{1,0:T(8,128)(2,1)S(1)}, bf16[512,128]{1,0:T(8,128)(2,1)S(1)}, u32[]{:S(2)}, u32[]{:S(2)}) %collective-permute-start.14) | collective-permute-done | bytes 131104 | tf_op jit(solution)/shard_map/ppermute | solution.py:478
  102.0 3.7 %collective-permute-done.15.rest_7_ = bf16[512,128]{1,0:T(8,128)(2,1)S(1)} collective-permute-done((bf16[512,128]{1,0:T(8,128)(2,1)S(1)}, bf16[512,128]{1,0:T(8,128)(2,1)S(1)}, u32[]{:S(2)}, u32[]{:S(2)}) %collective-permute-start.15) | collective-permute-done | bytes 131104 | tf_op jit(solution)/shard_map/ppermute | solution.py:478
  105.7 3.8 %collective-permute-done.17.rest_9_ = bf16[512,128]{1,0:T(8,128)(2,1)S(1)} collective-permute-done((bf16[512,128]{1,0:T(8,128)(2,1)S(1)}, bf16[512,128]{1,0:T(8,128)(2,1)S(1)}, u32[]{:S(2)}, u32[]{:S(2)}) %collective-permute-start.17) | collective-permute-done | bytes 131104 | tf_op jit(solution)/shard_map/ppermute | solution.py:478
  109.5 1.0 dense_layer.3
  110.5 3.1 %collective-permute-start.22 = (bf16[400,256]{1,0:T(8,128)(2,1)S(1)}, bf16[400,256]{1,0:T(8,128)(2,1)S(1)}, u32[]{:S(2)}, u32[]{:S(2)}) collective-permute-start(bf16[400,256]{1,0:T(8,128)(2,1)S(1)} %get-tuple-element.72.rest_2_), channel_id=1, source_target_pairs={{0,80},{8,88},{16,64},{24,72},{32,112},{40,120},{48,96},{56,104},{... | collective-permute-start | bytes 614408 | tf_op jit(solution)/shard_map/ppermute | solution.py:478
  114.0 3.8 %collective-permute-start.20 = (bf16[400,256]{1,0:T(8,128)(2,1)S(1)}, bf16[400,256]{1,0:T(8,128)(2,1)S(1)}, u32[]{:S(2)}, u32[]{:S(2)}) collective-permute-start(bf16[400,256]{1,0:T(8,128)(2,1)S(1)} %get-tuple-element.72.rest_2_), channel_id=1, source_target_pairs={{0,48},{8,56},{16,32},{24,40},{32,80},{40,88},{48,64},{56,72},{64,... | collective-permute-start | bytes 614408 | tf_op jit(solution)/shard_map/ppermute | solution.py:478
  117.8 1.3 collective-permute-start.19
  119.1 1.0 collective-permute-start.18
  120.1 2.4 %collective-permute-done.22.rest_7_ = bf16[400,256]{1,0:T(8,128)(2,1)S(1)} collective-permute-done((bf16[400,256]{1,0:T(8,128)(2,1)S(1)}, bf16[400,256]{1,0:T(8,128)(2,1)S(1)}, u32[]{:S(2)}, u32[]{:S(2)}) %collective-permute-start.22) | collective-permute-done | bytes 204832 | tf_op jit(solution)/shard_map/ppermute | solution.py:478
  122.5 1.8 collective-permute-done.21.rest_6_
  124.3 4.1 %collective-permute-done.20.rest_5_ = bf16[400,256]{1,0:T(8,128)(2,1)S(1)} collective-permute-done((bf16[400,256]{1,0:T(8,128)(2,1)S(1)}, bf16[400,256]{1,0:T(8,128)(2,1)S(1)}, u32[]{:S(2)}, u32[]{:S(2)}) %collective-permute-start.20) | collective-permute-done | bytes 204832 | tf_op jit(solution)/shard_map/ppermute | solution.py:478
  128.4 2.6 %collective-permute-done.19.rest_4_ = bf16[400,256]{1,0:T(8,128)(2,1)S(1)} collective-permute-done((bf16[400,256]{1,0:T(8,128)(2,1)S(1)}, bf16[400,256]{1,0:T(8,128)(2,1)S(1)}, u32[]{:S(2)}, u32[]{:S(2)}) %collective-permute-start.19) | collective-permute-done | bytes 204832 | tf_op jit(solution)/shard_map/ppermute | solution.py:478
  131.0 2.3 %collective-permute-start.25 = (bf16[400,256]{1,0:T(8,128)(2,1)S(1)}, bf16[400,256]{1,0:T(8,128)(2,1)S(1)}, u32[]{:S(2)}, u32[]{:S(2)}) collective-permute-start(bf16[400,256]{1,0:T(8,128)(2,1)S(1)} %get-tuple-element.72.rest_2_), channel_id=1, source_target_pairs={{0,112},{8,120},{16,96},{24,104},{32,16},{40,24},{48,0},{56,8},{64... | collective-permute-start | bytes 614408 | tf_op jit(solution)/shard_map/ppermute | solution.py:478
  133.3 2.4 %collective-permute-start.24 = (bf16[400,256]{1,0:T(8,128)(2,1)S(1)}, bf16[400,256]{1,0:T(8,128)(2,1)S(1)}, u32[]{:S(2)}, u32[]{:S(2)}) collective-permute-start(bf16[400,256]{1,0:T(8,128)(2,1)S(1)} %get-tuple-element.72.rest_2_), channel_id=1, source_target_pairs={{0,96},{8,104},{16,112},{24,120},{32,0},{40,8},{48,16},{56,24},{64... | collective-permute-start | bytes 614408 | tf_op jit(solution)/shard_map/ppermute | solution.py:478
  135.7 5.6 %collective-permute-done.25.rest_9_ = bf16[400,256]{1,0:T(8,128)(2,1)S(1)} collective-permute-done((bf16[400,256]{1,0:T(8,128)(2,1)S(1)}, bf16[400,256]{1,0:T(8,128)(2,1)S(1)}, u32[]{:S(2)}, u32[]{:S(2)}) %collective-permute-start.25) | collective-permute-done | bytes 204832 | tf_op jit(solution)/shard_map/ppermute | solution.py:478
  141.3 3.1 %collective-permute-done.24.rest_8_ = bf16[400,256]{1,0:T(8,128)(2,1)S(1)} collective-permute-done((bf16[400,256]{1,0:T(8,128)(2,1)S(1)}, bf16[400,256]{1,0:T(8,128)(2,1)S(1)}, u32[]{:S(2)}, u32[]{:S(2)}) %collective-permute-start.24) | collective-permute-done | bytes 204832 | tf_op jit(solution)/shard_map/ppermute | solution.py:478
  144.5 0.5 collective-permute-start.27
  145.0 0.5 collective-permute-start.29
  145.5 0.4 collective-permute-done.32.rest_16_
  146.8 0.6 collective-permute-done.30.rest_14_
  147.7 7.3 %backward_tiles.2 = (bf16[8,400,256]{2,1,0:T(8,128)(2,1)}, bf16[8192,256]{1,0:T(8,128)(2,1)}) custom-call(s32[1024]{0:T(1024)} %slot_lists.1.lists_ref, bf16[128,256,256]{2,1,0:T(8,128)(2,1)} %bitcast.16, bf16[8,256,256]{2,1,0:T(8,128)(2,1)S(1)} %all-to-all-done.1.rest_0_, bf16[8,256,256]{2,1,0:T(8,128)(2,1)S(1)} %collective-permute-done.23.rest_1_, ...), custom_call_target="tpu_custom_call" | custom-call | flops 1073741824 | bytes 20971520 | tf_op jit(solution)/shard_map/backward_tiles/pallas_call | solution.py:303
  154.9 8.0 %all-to-all-start.2 = ((bf16[8,400,256]{2,1,0:T(8,128)(2,1)}), bf16[8,400,256]{2,1,0:T(8,128)(2,1)S(1)}, u32[]{:S(2)}, u32[]{:S(2)}) async-start(bf16[8,400,256]{2,1,0:T(8,128)(2,1)} %get-tuple-element.79), calls=%async_computation.2 | async-start | bytes 3276800 | tf_op jit(solution)/shard_map/all_to_all | solution.py:462
  162.9 7.6 %backward_tiles.3 = (bf16[256,256]{1,0:T(8,128)(2,1)S(1)}, bf16[256,256]{1,0:T(8,128)(2,1)S(1)}, bf16[256,256]{1,0:T(8,128)(2,1)S(1)}, bf16[256,256]{1,0:T(8,128...) custom-call(s32[1024]{0:T(1024)} %slot_lists.1.lists_ref, ...), custom_call_target="tpu_custom_call" | custom-call | flops 1073741824 | bytes 20971520 | tf_op jit(solution)/shard_map/backward_tiles/pallas_call | solution.py:303
  170.6 0.6 collective-permute-start.35
  171.2 1.0 collective-permute-start.36
  172.2 4.6 %collective-permute-start.37 = (bf16[256,256]{1,0:T(8,128)(2,1)S(1)}, bf16[256,256]{1,0:T(8,128)(2,1)S(1)}, u32[]{:S(2)}, u32[]{:S(2)}) collective-permute-start(bf16[256,256]{1,0:T(8,128)(2,1)S(1)} %get-tuple-element.86), channel_id=1, source_target_pairs={{0,4},{1,5},{2,6},{3,7},{4,0},{5,1},{6,2},{7,3},{8,12},{9,13},{10,... | collective-permute-start | bytes 393224 | tf_op jit(solution)/shard_map/ppermute | solution.py:470
  176.8 0.6 collective-permute-start.38
  177.3 9.8 %collective-permute-done.34.rest_2_ = bf16[256,256]{1,0:T(8,128)(2,1)S(1)} collective-permute-done((bf16[256,256]{1,0:T(8,128)(2,1)S(1)}, bf16[256,256]{1,0:T(8,128)(2,1)S(1)}, u32[]{:S(2)}, u32[]{:S(2)}) %collective-permute-start.34) | collective-permute-done | bytes 131104 | tf_op jit(solution)/shard_map/ppermute | solution.py:470
  187.1 2.8 %collective-permute-start.39 = (bf16[256,256]{1,0:T(8,128)(2,1)S(1)}, bf16[256,256]{1,0:T(8,128)(2,1)S(1)}, u32[]{:S(2)}, u32[]{:S(2)}) collective-permute-start(bf16[256,256]{1,0:T(8,128)(2,1)S(1)} %get-tuple-element.88), channel_id=1, source_target_pairs={{0,6},{1,7},{2,0},{3,1},{4,2},{5,3},{6,4},{7,5},{8,14},{9,15},{10,... | collective-permute-start | bytes 393224 | tf_op jit(solution)/shard_map/ppermute | solution.py:470
  189.9 3.1 %collective-permute-done.35.rest_3_ = bf16[256,256]{1,0:T(8,128)(2,1)S(1)} collective-permute-done((bf16[256,256]{1,0:T(8,128)(2,1)S(1)}, bf16[256,256]{1,0:T(8,128)(2,1)S(1)}, u32[]{:S(2)}, u32[]{:S(2)}) %collective-permute-start.35) | collective-permute-done | bytes 131104 | tf_op jit(solution)/shard_map/ppermute | solution.py:470
  193.1 1.7 collective-permute-start.40
  194.8 0.9 last_sum.2
  195.7 3.2 %collective-permute-done.40.rest_8_ = bf16[256,256]{1,0:T(8,128)(2,1)S(1)} collective-permute-done((bf16[256,256]{1,0:T(8,128)(2,1)S(1)}, bf16[256,256]{1,0:T(8,128)(2,1)S(1)}, u32[]{:S(2)}, u32[]{:S(2)}) %collective-permute-start.40) | collective-permute-done | bytes 131104 | tf_op jit(solution)/shard_map/ppermute | solution.py:470
  198.9 0.9 last_sum.3
  (42 shorter events, 2.7 us)
Async XLA Ops:
  0.6 13.4 %collective-permute-start.6 = (bf16[1024,128]{1,0:T(8,128)(2,1)}, bf16[1024,128]{1,0:T(8,128)(2,1)S(1)}, u32[]{:S(2)}, u32[]{:S(2)}) collective-permute-start(bf16[1024,128]{1,0:T(8,128)(2,1)} %rest_0_.3), channel_id=1, source_target_pairs={{0,7},{1,6},{2,1},{3,0},{4,3},{5,2},{6,5},{7,4},{8,15},{9,14},{10,... | collective-permute-start | bytes 786440 | tf_op jit(solution)/shard_map/ppermute | solution.py:470
  5.8 22.6 %collective-permute-start.5 = (bf16[1024,128]{1,0:T(8,128)(2,1)}, bf16[1024,128]{1,0:T(8,128)(2,1)S(1)}, u32[]{:S(2)}, u32[]{:S(2)}) collective-permute-start(bf16[1024,128]{1,0:T(8,128)(2,1)} %rest_0_.3), channel_id=1, source_target_pairs={{0,6},{1,7},{2,0},{3,1},{4,2},{5,3},{6,4},{7,5},{8,14},{9,15},{10,... | collective-permute-start | bytes 786440 | tf_op jit(solution)/shard_map/ppermute | solution.py:470
  6.2 30.5 %collective-permute-start.4 = (bf16[1024,128]{1,0:T(8,128)(2,1)}, bf16[1024,128]{1,0:T(8,128)(2,1)S(1)}, u32[]{:S(2)}, u32[]{:S(2)}) collective-permute-start(bf16[1024,128]{1,0:T(8,128)(2,1)} %rest_0_.3), channel_id=1, source_target_pairs={{0,5},{1,4},{2,7},{3,6},{4,1},{5,0},{6,3},{7,2},{8,13},{9,12},{10,... | collective-permute-start | bytes 786440 | tf_op jit(solution)/shard_map/ppermute | solution.py:470
  6.2 30.5 %collective-permute-start.3 = (bf16[1024,128]{1,0:T(8,128)(2,1)}, bf16[1024,128]{1,0:T(8,128)(2,1)S(1)}, u32[]{:S(2)}, u32[]{:S(2)}) collective-permute-start(bf16[1024,128]{1,0:T(8,128)(2,1)} %rest_0_.3), channel_id=1, source_target_pairs={{0,4},{1,5},{2,6},{3,7},{4,0},{5,1},{6,2},{7,3},{8,12},{9,13},{10,... | collective-permute-start | bytes 786440 | tf_op jit(solution)/shard_map/ppermute | solution.py:470
  9.7 27.1 %collective-permute-start.2 = (bf16[1024,128]{1,0:T(8,128)(2,1)}, bf16[1024,128]{1,0:T(8,128)(2,1)S(1)}, u32[]{:S(2)}, u32[]{:S(2)}) collective-permute-start(bf16[1024,128]{1,0:T(8,128)(2,1)} %rest_0_.3), channel_id=1, source_target_pairs={{0,3},{1,2},{2,5},{3,4},{4,7},{5,6},{6,1},{7,0},{8,11},{9,10},{10,... | collective-permute-start | bytes 786440 | tf_op jit(solution)/shard_map/ppermute | solution.py:470
  14.1 22.7 %collective-permute-start.1 = (bf16[1024,128]{1,0:T(8,128)(2,1)}, bf16[1024,128]{1,0:T(8,128)(2,1)S(1)}, u32[]{:S(2)}, u32[]{:S(2)}) collective-permute-start(bf16[1024,128]{1,0:T(8,128)(2,1)} %rest_0_.3), channel_id=1, source_target_pairs={{0,2},{1,3},{2,4},{3,5},{4,6},{5,7},{6,0},{7,1},{8,10},{9,11},{10,... | collective-permute-start | bytes 786440 | tf_op jit(solution)/shard_map/ppermute | solution.py:470
  28.5 8.4 %collective-permute-start = (bf16[1024,128]{1,0:T(8,128)(2,1)}, bf16[1024,128]{1,0:T(8,128)(2,1)S(1)}, u32[]{:S(2)}, u32[]{:S(2)}) collective-permute-start(bf16[1024,128]{1,0:T(8,128)(2,1)} %rest_0_.3), channel_id=1, source_target_pairs={{0,1},{1,0},{2,3},{3,2},{4,5},{5,4},{6,7},{7,6},{8,9},{9,8},{10,11... | collective-permute-start | bytes 786440 | tf_op jit(solution)/shard_map/ppermute | solution.py:470
  44.2 2.0 collective-permute-start.7
  44.3 2.6 %collective-permute-start.8 = (bf16[4,512,128]{2,1,0:T(8,128)(2,1)S(1)}, bf16[4,512,128]{2,1,0:T(8,128)(2,1)S(1)}, u32[]{:S(2)}, u32[]{:S(2)}) collective-permute-start(bf16[4,512,128]{2,1,0:T(8,128)(2,1)S(1)} %get-tuple-element.50), channel_id=1, source_target_pairs={{0,8},{8,0},{16,24},{24,16},{32,40},{40,32},{48,56},{56,48},{64,72... | collective-permute-start | bytes 1572872 | tf_op jit(solution)/shard_map/ppermute | solution.py:454
  48.2 28.8 %all-to-all-start = ((bf16[8,512,128]{2,1,0:T(8,128)(2,1)}), bf16[8,512,128]{2,1,0:T(8,128)(2,1)S(1)}, u32[]{:S(2)}, u32[]{:S(2)}) async-start(bf16[8,512,128]{2,1,0:T(8,128)(2,1)} %pair_sum.2), calls=%async_computation | async-start | bytes 2097152 | tf_op jit(solution)/shard_map/all_to_all | solution.py:458
  53.5 23.5 %copy-start = (bf16[1024,128]{1,0:T(8,128)(2,1)S(1)}, bf16[1024,128]{1,0:T(8,128)(2,1)}, u32[]{:S(2)}) copy-start(bf16[1024,128]{1,0:T(8,128)(2,1)} %cot_ref.3) | copy-start | bytes 786436
  53.5 23.5 %copy-start.1 = (bf16[128,128]{1,0:T(8,128)(2,1)S(1)}, bf16[128,128]{1,0:T(8,128)(2,1)}, u32[]{:S(2)}) copy-start(bf16[128,128]{1,0:T(8,128)(2,1)} %weight_ref.3) | copy-start | bytes 98308
  53.5 23.5 %copy-start.2 = (f32[128]{0:T(128)S(1)}, f32[128]{0:T(128)}, u32[]{:S(2)}) copy-start(f32[128]{0:T(128)} %param.10) | copy-start | bytes 1540
  60.5 2.0 collective-permute-start.9
  60.6 2.6 %collective-permute-start.10 = (bf16[4,512,128]{2,1,0:T(8,128)(2,1)S(1)}, bf16[4,512,128]{2,1,0:T(8,128)(2,1)S(1)}, u32[]{:S(2)}, u32[]{:S(2)}) collective-permute-start(bf16[4,512,128]{2,1,0:T(8,128)(2,1)S(1)} %get-tuple-element.55), channel_id=1, source_target_pairs={{0,8},{8,0},{16,24},{24,16},{32,40},{40,32},{48,56},{56,48},{64,72... | collective-permute-start | bytes 1572872 | tf_op jit(solution)/shard_map/ppermute | solution.py:454
  63.5 8.9 %collective-permute-start.11 = (bf16[512,128]{1,0:T(8,128)(2,1)S(1)}, bf16[512,128]{1,0:T(8,128)(2,1)S(1)}, u32[]{:S(2)}, u32[]{:S(2)}) collective-permute-start(bf16[512,128]{1,0:T(8,128)(2,1)S(1)} %get-tuple-element.56), channel_id=1, source_target_pairs={{0,16},{8,24},{16,0},{24,8},{32,48},{40,56},{48,32},{56,40},{64,80... | collective-permute-start | bytes 393224 | tf_op jit(solution)/shard_map/ppermute | solution.py:478
  65.5 8.0 %collective-permute-start.12 = (bf16[512,128]{1,0:T(8,128)(2,1)S(1)}, bf16[512,128]{1,0:T(8,128)(2,1)S(1)}, u32[]{:S(2)}, u32[]{:S(2)}) collective-permute-start(bf16[512,128]{1,0:T(8,128)(2,1)S(1)} %get-tuple-element.57), channel_id=1, source_target_pairs={{0,32},{8,40},{16,48},{24,56},{32,64},{40,72},{48,80},{56,88},{64,... | collective-permute-start | bytes 393224 | tf_op jit(solution)/shard_map/ppermute | solution.py:478
  67.3 9.6 %collective-permute-start.13 = (bf16[512,128]{1,0:T(8,128)(2,1)S(1)}, bf16[512,128]{1,0:T(8,128)(2,1)S(1)}, u32[]{:S(2)}, u32[]{:S(2)}) collective-permute-start(bf16[512,128]{1,0:T(8,128)(2,1)S(1)} %get-tuple-element.58), channel_id=1, source_target_pairs={{0,48},{8,56},{16,32},{24,40},{32,80},{40,88},{48,64},{56,72},{64,... | collective-permute-start | bytes 393224 | tf_op jit(solution)/shard_map/ppermute | solution.py:478
  78.5 52.4 %all-to-all-start.1 = ((bf16[8,256,256]{2,1,0:T(8,128)(2,1)}), bf16[8,256,256]{2,1,0:T(8,128)(2,1)S(1)}, u32[]{:S(2)}, u32[]{:S(2)}) async-start(bf16[8,256,256]{2,1,0:T(8,128)(2,1)} %get-tuple-element.71), calls=%async_computation.1 | async-start | bytes 2097152 | tf_op jit(solution)/shard_map/all_to_all | solution.py:458
  82.8 19.2 %collective-permute-start.14 = (bf16[512,128]{1,0:T(8,128)(2,1)S(1)}, bf16[512,128]{1,0:T(8,128)(2,1)S(1)}, u32[]{:S(2)}, u32[]{:S(2)}) collective-permute-start(bf16[512,128]{1,0:T(8,128)(2,1)S(1)} %get-tuple-element.66), channel_id=1, source_target_pairs={{0,64},{8,72},{16,80},{24,88},{32,96},{40,104},{48,112},{56,120},{... | collective-permute-start | bytes 393224 | tf_op jit(solution)/shard_map/ppermute | solution.py:478
  86.3 19.4 %collective-permute-start.15 = (bf16[512,128]{1,0:T(8,128)(2,1)S(1)}, bf16[512,128]{1,0:T(8,128)(2,1)S(1)}, u32[]{:S(2)}, u32[]{:S(2)}) collective-permute-start(bf16[512,128]{1,0:T(8,128)(2,1)S(1)} %get-tuple-element.67), channel_id=1, source_target_pairs={{0,80},{8,88},{16,64},{24,72},{32,112},{40,120},{48,96},{56,104},{... | collective-permute-start | bytes 393224 | tf_op jit(solution)/shard_map/ppermute | solution.py:478
  89.3 16.4 %collective-permute-start.16 = (bf16[512,128]{1,0:T(8,128)(2,1)S(1)}, bf16[512,128]{1,0:T(8,128)(2,1)S(1)}, u32[]{:S(2)}, u32[]{:S(2)}) collective-permute-start(bf16[512,128]{1,0:T(8,128)(2,1)S(1)} %get-tuple-element.68), channel_id=1, source_target_pairs={{0,96},{8,104},{16,112},{24,120},{32,0},{40,8},{48,16},{56,24},{64... | collective-permute-start | bytes 393224 | tf_op jit(solution)/shard_map/ppermute | solution.py:478
  92.0 17.5 %collective-permute-start.17 = (bf16[512,128]{1,0:T(8,128)(2,1)S(1)}, bf16[512,128]{1,0:T(8,128)(2,1)S(1)}, u32[]{:S(2)}, u32[]{:S(2)}) collective-permute-start(bf16[512,128]{1,0:T(8,128)(2,1)S(1)} %get-tuple-element.69), channel_id=1, source_target_pairs={{0,112},{8,120},{16,96},{24,104},{32,16},{40,24},{48,0},{56,8},{64... | collective-permute-start | bytes 393224 | tf_op jit(solution)/shard_map/ppermute | solution.py:478
  110.5 12.0 %collective-permute-start.22 = (bf16[400,256]{1,0:T(8,128)(2,1)S(1)}, bf16[400,256]{1,0:T(8,128)(2,1)S(1)}, u32[]{:S(2)}, u32[]{:S(2)}) collective-permute-start(bf16[400,256]{1,0:T(8,128)(2,1)S(1)} %get-tuple-element.72.rest_2_), channel_id=1, source_target_pairs={{0,80},{8,88},{16,64},{24,72},{32,112},{40,120},{48,96},{56,104},{... | collective-permute-start | bytes 614408 | tf_op jit(solution)/shard_map/ppermute | solution.py:478
  113.6 10.7 %collective-permute-start.21 = (bf16[400,256]{1,0:T(8,128)(2,1)S(1)}, bf16[400,256]{1,0:T(8,128)(2,1)S(1)}, u32[]{:S(2)}, u32[]{:S(2)}) collective-permute-start(bf16[400,256]{1,0:T(8,128)(2,1)S(1)} %get-tuple-element.72.rest_2_), channel_id=1, source_target_pairs={{0,64},{8,72},{16,80},{24,88},{32,96},{40,104},{48,112},{56,120},{... | collective-permute-start | bytes 614408 | tf_op jit(solution)/shard_map/ppermute | solution.py:478
  114.0 14.3 %collective-permute-start.20 = (bf16[400,256]{1,0:T(8,128)(2,1)S(1)}, bf16[400,256]{1,0:T(8,128)(2,1)S(1)}, u32[]{:S(2)}, u32[]{:S(2)}) collective-permute-start(bf16[400,256]{1,0:T(8,128)(2,1)S(1)} %get-tuple-element.72.rest_2_), channel_id=1, source_target_pairs={{0,48},{8,56},{16,32},{24,40},{32,80},{40,88},{48,64},{56,72},{64,... | collective-permute-start | bytes 614408 | tf_op jit(solution)/shard_map/ppermute | solution.py:478
  117.8 13.1 %collective-permute-start.19 = (bf16[400,256]{1,0:T(8,128)(2,1)S(1)}, bf16[400,256]{1,0:T(8,128)(2,1)S(1)}, u32[]{:S(2)}, u32[]{:S(2)}) collective-permute-start(bf16[400,256]{1,0:T(8,128)(2,1)S(1)} %get-tuple-element.72.rest_2_), channel_id=1, source_target_pairs={{0,32},{8,40},{16,48},{24,56},{32,64},{40,72},{48,80},{56,88},{64,... | collective-permute-start | bytes 614408 | tf_op jit(solution)/shard_map/ppermute | solution.py:478
  119.1 11.9 %collective-permute-start.18 = (bf16[400,256]{1,0:T(8,128)(2,1)S(1)}, bf16[400,256]{1,0:T(8,128)(2,1)S(1)}, u32[]{:S(2)}, u32[]{:S(2)}) collective-permute-start(bf16[400,256]{1,0:T(8,128)(2,1)S(1)} %get-tuple-element.72.rest_2_), channel_id=1, source_target_pairs={{0,16},{8,24},{16,0},{24,8},{32,48},{40,56},{48,32},{56,40},{64,80... | collective-permute-start | bytes 614408 | tf_op jit(solution)/shard_map/ppermute | solution.py:478
  131.0 16.7 %collective-permute-start.23 = (bf16[8,256,256]{2,1,0:T(8,128)(2,1)S(1)}, bf16[8,256,256]{2,1,0:T(8,128)(2,1)S(1)}, u32[]{:S(2)}, u32[]{:S(2)}) collective-permute-start(bf16[8,256,256]{2,1,0:T(8,128)(2,1)S(1)} %all-to-all-done.1.rest_0_), channel_id=1, source_target_pairs={{0,8},{8,0},{16,24},{24,16},{32,40},{40,32},{48,56},{56,48},{64,72... | collective-permute-start | bytes 3145736 | tf_op jit(solution)/shard_map/ppermute | solution.py:454
  131.0 10.4 %collective-permute-start.25 = (bf16[400,256]{1,0:T(8,128)(2,1)S(1)}, bf16[400,256]{1,0:T(8,128)(2,1)S(1)}, u32[]{:S(2)}, u32[]{:S(2)}) collective-permute-start(bf16[400,256]{1,0:T(8,128)(2,1)S(1)} %get-tuple-element.72.rest_2_), channel_id=1, source_target_pairs={{0,112},{8,120},{16,96},{24,104},{32,16},{40,24},{48,0},{56,8},{64... | collective-permute-start | bytes 614408 | tf_op jit(solution)/shard_map/ppermute | solution.py:478
  133.3 11.2 %collective-permute-start.24 = (bf16[400,256]{1,0:T(8,128)(2,1)S(1)}, bf16[400,256]{1,0:T(8,128)(2,1)S(1)}, u32[]{:S(2)}, u32[]{:S(2)}) collective-permute-start(bf16[400,256]{1,0:T(8,128)(2,1)S(1)} %get-tuple-element.72.rest_2_), channel_id=1, source_target_pairs={{0,96},{8,104},{16,112},{24,120},{32,0},{40,8},{48,16},{56,24},{64... | collective-permute-start | bytes 614408 | tf_op jit(solution)/shard_map/ppermute | solution.py:478
  135.7 9.3 %collective-permute-start.26 = (bf16[400,256]{1,0:T(8,128)(2,1)S(1)}, bf16[400,256]{1,0:T(8,128)(2,1)S(1)}, u32[]{:S(2)}, u32[]{:S(2)}) collective-permute-start(bf16[400,256]{1,0:T(8,128)(2,1)S(1)} %get-tuple-element.72.rest_2_), channel_id=1, source_target_pairs={{0,8},{8,0},{16,24},{24,16},{32,40},{40,32},{48,56},{56,48},{64,72... | collective-permute-start | bytes 614408 | tf_op jit(solution)/shard_map/ppermute | solution.py:454
  141.3 3.7 %collective-permute-start.33 = (bf16[400,256]{1,0:T(8,128)(2,1)S(1)}, bf16[400,256]{1,0:T(8,128)(2,1)S(1)}, u32[]{:S(2)}, u32[]{:S(2)}) collective-permute-start(bf16[400,256]{1,0:T(8,128)(2,1)S(1)} %collective-permute-done.25.rest_9_), channel_id=1, source_target_pairs={{0,8},{8,0},{16,24},{24,16},{32,40},{40,32},{48,56},{56,48},{64,72... | collective-permute-start | bytes 614408 | tf_op jit(solution)/shard_map/ppermute | solution.py:454
  144.5 1.5 collective-permute-start.32
  144.5 1.7 collective-permute-start.27
  145.0 1.5 collective-permute-start.28
  145.0 1.8 collective-permute-start.29
  145.9 1.5 collective-permute-start.30
  146.2 1.5 collective-permute-start.31
  154.9 39.9 %all-to-all-start.2 = ((bf16[8,400,256]{2,1,0:T(8,128)(2,1)}), bf16[8,400,256]{2,1,0:T(8,128)(2,1)S(1)}, u32[]{:S(2)}, u32[]{:S(2)}) async-start(bf16[8,400,256]{2,1,0:T(8,128)(2,1)} %get-tuple-element.79), calls=%async_computation.2 | async-start | bytes 3276800 | tf_op jit(solution)/shard_map/all_to_all | solution.py:462
  170.5 16.6 %collective-permute-start.34 = (bf16[256,256]{1,0:T(8,128)(2,1)S(1)}, bf16[256,256]{1,0:T(8,128)(2,1)S(1)}, u32[]{:S(2)}, u32[]{:S(2)}) collective-permute-start(bf16[256,256]{1,0:T(8,128)(2,1)S(1)} %get-tuple-element.83), channel_id=1, source_target_pairs={{0,1},{1,0},{2,3},{3,2},{4,5},{5,4},{6,7},{7,6},{8,9},{9,8},{10,11... | collective-permute-start | bytes 393224 | tf_op jit(solution)/shard_map/ppermute | solution.py:470
  170.6 22.4 %collective-permute-start.35 = (bf16[256,256]{1,0:T(8,128)(2,1)S(1)}, bf16[256,256]{1,0:T(8,128)(2,1)S(1)}, u32[]{:S(2)}, u32[]{:S(2)}) collective-permute-start(bf16[256,256]{1,0:T(8,128)(2,1)S(1)} %get-tuple-element.84), channel_id=1, source_target_pairs={{0,2},{1,3},{2,4},{3,5},{4,6},{5,7},{6,0},{7,1},{8,10},{9,11},{10,... | collective-permute-start | bytes 393224 | tf_op jit(solution)/shard_map/ppermute | solution.py:470
  171.2 24.5 %collective-permute-start.36 = (bf16[256,256]{1,0:T(8,128)(2,1)S(1)}, bf16[256,256]{1,0:T(8,128)(2,1)S(1)}, u32[]{:S(2)}, u32[]{:S(2)}) collective-permute-start(bf16[256,256]{1,0:T(8,128)(2,1)S(1)} %get-tuple-element.85), channel_id=1, source_target_pairs={{0,3},{1,2},{2,5},{3,4},{4,7},{5,6},{6,1},{7,0},{8,11},{9,10},{10,... | collective-permute-start | bytes 393224 | tf_op jit(solution)/shard_map/ppermute | solution.py:470
  172.2 23.5 %collective-permute-start.37 = (bf16[256,256]{1,0:T(8,128)(2,1)S(1)}, bf16[256,256]{1,0:T(8,128)(2,1)S(1)}, u32[]{:S(2)}, u32[]{:S(2)}) collective-permute-start(bf16[256,256]{1,0:T(8,128)(2,1)S(1)} %get-tuple-element.86), channel_id=1, source_target_pairs={{0,4},{1,5},{2,6},{3,7},{4,0},{5,1},{6,2},{7,3},{8,12},{9,13},{10,... | collective-permute-start | bytes 393224 | tf_op jit(solution)/shard_map/ppermute | solution.py:470
  176.8 18.9 %collective-permute-start.38 = (bf16[256,256]{1,0:T(8,128)(2,1)S(1)}, bf16[256,256]{1,0:T(8,128)(2,1)S(1)}, u32[]{:S(2)}, u32[]{:S(2)}) collective-permute-start(bf16[256,256]{1,0:T(8,128)(2,1)S(1)} %get-tuple-element.87), channel_id=1, source_target_pairs={{0,5},{1,4},{2,7},{3,6},{4,1},{5,0},{6,3},{7,2},{8,13},{9,12},{10,... | collective-permute-start | bytes 393224 | tf_op jit(solution)/shard_map/ppermute | solution.py:470
  187.1 8.6 %collective-permute-start.39 = (bf16[256,256]{1,0:T(8,128)(2,1)S(1)}, bf16[256,256]{1,0:T(8,128)(2,1)S(1)}, u32[]{:S(2)}, u32[]{:S(2)}) collective-permute-start(bf16[256,256]{1,0:T(8,128)(2,1)S(1)} %get-tuple-element.88), channel_id=1, source_target_pairs={{0,6},{1,7},{2,0},{3,1},{4,2},{5,3},{6,4},{7,5},{8,14},{9,15},{10,... | collective-permute-start | bytes 393224 | tf_op jit(solution)/shard_map/ppermute | solution.py:470
  193.1 5.9 %collective-permute-start.40 = (bf16[256,256]{1,0:T(8,128)(2,1)S(1)}, bf16[256,256]{1,0:T(8,128)(2,1)S(1)}, u32[]{:S(2)}, u32[]{:S(2)}) collective-permute-start(bf16[256,256]{1,0:T(8,128)(2,1)S(1)} %get-tuple-element.89), channel_id=1, source_target_pairs={{0,7},{1,6},{2,1},{3,0},{4,3},{5,2},{6,5},{7,4},{8,15},{9,14},{10,... | collective-permute-start | bytes 393224 | tf_op jit(solution)/shard_map/ppermute | solution.py:470

commit v4 on v0

v4 whole, which is shorter than its diff:
```python
import functools
import math

import jax
import jax.numpy as jnp
from jax import lax
from jax.experimental import pallas as pl
from jax.experimental.pallas import tpu as pltpu
from jax.sharding import PartitionSpec as P

gelu_coef = 0.7978845608
cube_coef = 0.044715
TILE = 256
FEAT = 128
SLOTS = 128
NPEER = 8
LIST = 160
UNROLL = 8
DEPTH = 32
FWD_DUMMY = 32
BWD_DUMMY = 32
f32, bf16 = jnp.float32, jnp.bfloat16
VMEM_LIMIT = 28 * 2**20


def params():
    return pltpu.CompilerParams(vmem_limit_bytes=VMEM_LIMIT)


def vmem():
    return pl.BlockSpec(memory_space=pltpu.VMEM)


def smem():
    return pl.BlockSpec(memory_space=pltpu.SMEM)


def hbm():
    return pl.BlockSpec(memory_space=pl.ANY)


def prep_kernel(where_ref, out_ref, in_ref, count_ref, lists_ref):
    core, z, y = (where_ref[i] for i in range(3))

    def clear(i, carry):
        lists_ref[i] = FWD_DUMMY << 16
        lists_ref[LIST + i] = FWD_DUMMY << 16
        lists_ref[2 * LIST + i] = BWD_DUMMY << 16
        return carry

    lax.fori_loop(0, LIST, clear, 0)

    def place(k, carry):
        f0, f1 = carry
        t = out_ref[k]
        s = in_ref[k]
        rel = jnp.bitwise_xor((t >> 2) & 1, core)
        to_t = ((t >> 3) << 2) | (t & 3)
        dy, dz = ((s >> 2) + y) & 1, (z - (s >> 3)) & 3
        src_f = (((dz << 1) | dy) << 2) | (s & 3)
        at_f = jnp.where(rel == 0, f0, LIST + f1)
        lists_ref[at_f] = k | (src_f << 8) | (to_t << 16)
        lists_ref[2 * LIST + k] = k | ((rel * 32 + to_t) << 8) | (s << 16)
        return (f0 + 1 - rel, f1 + rel)

    zero = jnp.int32(0)
    count = count_ref[0]
    sizes = lax.fori_loop(0, count, place, (zero, zero))
    lists_ref[3 * LIST] = sizes[0]
    lists_ref[3 * LIST + 1] = sizes[1]
    lists_ref[3 * LIST + 2] = count


def prep(where, out_index, in_index, count):
    return pl.pallas_call(
        prep_kernel,
        out_shape=jax.ShapeDtypeStruct((1024,), jnp.int32),
        in_specs=[smem()] * 4,
        out_specs=smem(),
        name="slot_lists",
    )(where, out_index, in_index, count)


def tile_loop(which, lists_ref, vals, buf, sems, acc, ready, product):
    base = which * LIST
    groups = (lists_ref[3 * LIST + which] + (UNROLL - 1)) // UNROLL
    ahead = DEPTH // UNROLL

    def copy(g, u):
        slot = lists_ref[base + g * UNROLL + u] & 255
        at = lax.rem(g, ahead) * UNROLL + u
        return pltpu.make_async_copy(vals.at[slot], buf.at[at], sems.at[at])

    for g in range(ahead):

        @pl.when(g < groups)
        def _():
            for u in range(UNROLL):
                copy(g, u).start()

    ready()

    def body(g, carry):
        for u in range(UNROLL):
            copy(g, u).wait()
        todo = []
        for u in range(UNROLL):
            entry = lists_ref[base + g * UNROLL + u]
            at = lax.rem(g, ahead) * UNROLL + u
            todo.append((entry >> 16, product(buf[at], (entry >> 8) & 255)))
        for to, value in todo:
            acc[to] += value

        @pl.when(g + ahead < groups)
        def _():
            for u in range(UNROLL):
                copy(g + ahead, u).start()

        return carry

    lax.fori_loop(0, groups, body, 0)


def in_hbm(array):
    return pltpu.with_memory_space_constraint(array, pltpu.HBM)


TILES_COST = pl.CostEstimate(
    flops=2 * 64 * TILE * TILE * FEAT, bytes_accessed=16 * 2**20, transcendentals=0
)


def forward_kernel(which, lists_ref, vals, *rest):
    blocks = rest[:NPEER]
    out_ref, x, buf, acc, sems, own_sem = rest[NPEER:]
    own = pltpu.make_async_copy(blocks[0], x.at[pl.ds(0, 4 * TILE)], own_sem)
    own.start()

    def ready():
        def clear(i, carry):
            acc[i] = jnp.zeros((TILE, FEAT), f32)
            return carry

        lax.fori_loop(0, FWD_DUMMY, clear, 0)
        for k in range(1, NPEER):
            x[pl.ds(k * 4 * TILE, 4 * TILE), :] = blocks[k][...]
        own.wait()

    def product(tile, source):
        rows = x[pl.ds(pl.multiple_of(source * TILE, TILE), TILE), :]
        return jnp.dot(tile, rows, preferred_element_type=f32)

    tile_loop(which, lists_ref, vals, buf, sems, acc, ready, product)

    for i in range(4 * NPEER):
        out_ref[i // 4, pl.ds((i % 4) * TILE, TILE), :] = acc[i].astype(bf16)


def forward(which, lists, values, blocks):
    return pl.pallas_call(
        functools.partial(forward_kernel, which),
        out_shape=jax.ShapeDtypeStruct((NPEER, 4 * TILE, FEAT), bf16),
        in_specs=[smem(), hbm(), hbm()] + [vmem()] * (NPEER - 1),
        out_specs=vmem(),
        scratch_shapes=[
            pltpu.VMEM((NPEER * 4 * TILE, FEAT), bf16),
            pltpu.VMEM((DEPTH, TILE, TILE), bf16),
            pltpu.VMEM((FWD_DUMMY + 1, TILE, FEAT), f32),
            pltpu.SemaphoreType.DMA((DEPTH,)),
            pltpu.SemaphoreType.DMA,
        ],
        compiler_params=params(),
        cost_estimate=TILES_COST,
        name="forward_tiles",
    )(in_hbm(lists), in_hbm(values), in_hbm(blocks[0]), *blocks[1:])


def pair_sum_kernel(mine_ref, other_ref, out_ref):
    for k in range(NPEER):
        out_ref[k] = (mine_ref[k].astype(f32) + other_ref[k].astype(f32)).astype(bf16)


def pair_sum(mine, other):
    return pl.pallas_call(
        pair_sum_kernel,
        out_shape=jax.ShapeDtypeStruct(mine.shape, bf16),
        in_specs=[vmem()] * 2,
        out_specs=vmem(),
        compiler_params=params(),
        cost_estimate=pl.CostEstimate(flops=2**21, bytes_accessed=6 * 2**20, transcendentals=0),
        name="pair_sum",
    )(mine, other)


def backward_kernel(
    lists_ref, vals, mine_ref, other_ref, out_ref, g, out, buf, acc, sems, out_sems
):
    rows4 = 4 * FEAT

    def ready():
        def clear(i, carry):
            acc[i] = jnp.zeros((FEAT, TILE), f32)
            return carry

        lax.fori_loop(0, BWD_DUMMY, clear, 0)
        for p, ref in enumerate((mine_ref, other_ref)):
            for peer in range(NPEER):
                g[pl.ds((p * NPEER + peer) * rows4, rows4), :] = ref[peer]

    def product(tile, source):
        rows = g[pl.ds(pl.multiple_of(source * FEAT, FEAT), FEAT), :]
        return jnp.dot(rows, tile, preferred_element_type=f32)

    tile_loop(2, lists_ref, vals, buf, sems, acc, ready, product)

    copies = []
    for i in range(4 * NPEER):
        out[i // 4, pl.ds((i % 4) * FEAT, FEAT), :] = acc[i].astype(bf16)
        if i % 4 == 3:
            peer = i // 4
            copies.append(
                pltpu.make_async_copy(out.at[peer], out_ref.at[peer], out_sems.at[peer])
            )
            copies[-1].start()
    for copy in copies:
        copy.wait()


def backward(lists, values, mine, other):
    return pl.pallas_call(
        backward_kernel,
        out_shape=pltpu.HBM((NPEER, 4 * FEAT, TILE), bf16),
        in_specs=[smem(), hbm(), vmem(), vmem()],
        out_specs=hbm(),
        scratch_shapes=[
            pltpu.VMEM((2 * NPEER * 4 * FEAT, TILE), bf16),
            pltpu.VMEM((NPEER, 4 * FEAT, TILE), bf16),
            pltpu.VMEM((DEPTH, TILE, TILE), bf16),
            pltpu.VMEM((BWD_DUMMY + 1, FEAT, TILE), f32),
            pltpu.SemaphoreType.DMA((DEPTH,)),
            pltpu.SemaphoreType.DMA((NPEER,)),
        ],
        compiler_params=params(),
        cost_estimate=TILES_COST,
        name="backward_tiles",
    )(in_hbm(lists), in_hbm(values), mine, other)


def dense_kernel(
    recv_ref, weight_ref, bias_ref, cot_ref, hidden_ref, grad_ref, wsum_ref, one, sems
):
    copies = []
    weight = weight_ref[...]
    for part in range(2):
        here = pl.ds(part * 2 * TILE, 2 * TILE)
        total = recv_ref[0, here, :].astype(f32)
        for peer in range(1, NPEER):
            total += recv_ref[peer, here, :].astype(f32)
        agg = total.astype(bf16)
        v = jnp.dot(agg, weight, preferred_element_type=f32) + bias_ref[...]
        s = jnp.tanh(gelu_coef * (v + cube_coef * v * v * v))
        hidden_ref[here, :] = (0.5 * v * (1.0 + s)).astype(bf16)
        slope = 0.5 * (1.0 + s) + 0.5 * v * (1.0 - s * s) * gelu_coef * (
            1.0 + 3.0 * cube_coef * v * v
        )
        grad = (cot_ref[here, :].astype(f32) * slope).astype(bf16)
        wsum = lax.dot_general(agg, grad, (((0,), (0,)), ((), ())), preferred_element_type=f32)
        bsum = jnp.dot(jnp.ones((16, 2 * TILE), bf16), grad, preferred_element_type=f32)[:8]
        back = lax.dot_general(weight, grad, (((1,), (1,)), ((), ())), preferred_element_type=f32)
        back = back.astype(bf16)
        for sub in range(2):
            rows = pl.ds((part * 2 + sub) * FEAT, FEAT)
            one[rows, :] = back[:, sub * TILE : (sub + 1) * TILE]
        rows = pl.ds(part * 2 * FEAT, 2 * FEAT)
        for peer in range(NPEER):
            copies.append(
                pltpu.make_async_copy(
                    one.at[rows], grad_ref.at[peer, rows], sems.at[part * NPEER + peer]
                )
            )
            copies[-1].start()
        if part == 0:
            wsum_ref[pl.ds(0, FEAT), :] = wsum
            wsum_ref[pl.ds(FEAT, 8), :] = bsum
        else:
            wsum_ref[pl.ds(0, FEAT), :] += wsum
            wsum_ref[pl.ds(FEAT, 8), :] += bsum
    for copy in copies:
        copy.wait()


def dense(recv, weight, bias, cotangent):
    return pl.pallas_call(
        dense_kernel,
        out_shape=(
            jax.ShapeDtypeStruct((4 * TILE, FEAT), bf16),
            pltpu.HBM((NPEER, 4 * FEAT, TILE), bf16),
            jax.ShapeDtypeStruct((FEAT + 8, FEAT), f32),
        ),
        in_specs=[vmem()] * 4,
        out_specs=(vmem(), hbm(), vmem()),
        scratch_shapes=[
            pltpu.VMEM((4 * FEAT, TILE), bf16),
            pltpu.SemaphoreType.DMA((2 * NPEER,)),
        ],
        compiler_params=params(),
        cost_estimate=pl.CostEstimate(
            flops=6 * 1024 * FEAT * FEAT, bytes_accessed=5 * 2**20, transcendentals=1024 * FEAT
        ),
        name="dense_layer",
    )(recv, weight, bias, cotangent)


def last_kernel(recv_ref, grad_ref):
    for sub in range(4):
        rows = pl.ds(sub * FEAT, FEAT)
        total = recv_ref[0, rows, :].astype(f32)
        for peer in range(1, NPEER):
            total += recv_ref[peer, rows, :].astype(f32)
        grad_ref[pl.ds(sub * TILE, TILE), :] = total.T.astype(bf16)


def last(recv):
    return pl.pallas_call(
        last_kernel,
        out_shape=jax.ShapeDtypeStruct((4 * TILE, FEAT), bf16),
        in_specs=[vmem()],
        out_specs=vmem(),
        compiler_params=params(),
        cost_estimate=pl.CostEstimate(flops=2**20, bytes_accessed=3 * 2**20, transcendentals=0),
        name="last_sum",
    )(recv)


SAME_CORE = [[2 * j + core for j in range(NPEER)] for core in range(2)]
OTHER_CORE = [(r, r ^ 1) for r in range(16)]


def to_other_core(value):
    return lax.ppermute(value, "row", OTHER_CORE)


def row_exchange(value):
    return lax.all_to_all(value, "row", 0, 0, axis_index_groups=SAME_CORE)


def col_exchange(value):
    return lax.all_to_all(value, "col", 0, 0)


def col_shift(value, k):
    pairs = []
    for c in range(8):
        z, y = c // 2, c % 2
        pairs.append((c, ((z + k // 2) % 4) * 2 + (y + k) % 2))
    return lax.ppermute(value, "col", pairs)


def butterfly(value, axis, size, bits):
    for bit in bits:
        value = value + lax.ppermute(value, axis, [(i, i ^ bit) for i in range(size)])
    return value


def local(features, weight, layer_bias, cotangent, tile_out, tile_in, tile_vals, tile_count):
    values = tile_vals[0, 0]
    row, col = lax.axis_index("row"), lax.axis_index("col")
    where = jnp.stack([row & 1, col >> 1, col & 1]).astype(jnp.int32)
    lists = prep(where, tile_out[0, 0], tile_in[0, 0], tile_count[0])
    bias = layer_bias.reshape(1, FEAT)
    order = lax.optimization_barrier

    blocks = [features] + [col_shift(features, k) for k in range(1, NPEER)]

    other = forward(1, lists, values, blocks)
    other, lists = order((other, lists))
    mine = forward(0, lists, values, blocks)
    recv = row_exchange(pair_sum(mine, to_other_core(other)))
    hidden, grad, wsum = dense(recv, weight, bias, cotangent)
    grads = row_exchange(grad)
    wsum = butterfly(wsum, "row", 16, (1, 2, 4, 8))
    grads, wsum = order((grads, wsum))
    back = backward(lists, values, grads, to_other_core(grads))
    back = col_exchange(back)
    wsum = butterfly(wsum, "col", 8, (1, 2, 4))
    scale = 1.0 / math.sqrt(4 * TILE * 128)
    weight_grad = wsum[:FEAT] * scale
    bias_grad = wsum[FEAT] * scale
    back, weight_grad, bias_grad = order((back, weight_grad, bias_grad))
    feature_grad = last(back)
    return (hidden, feature_grad, weight_grad, bias_grad)


def solution(mesh):
    in_specs = (
        P(("row", "col"), None),
        P(),
        P(),
        P(("col", "row"), None),
        P("row", "col", None),
        P("row", "col", None),
        P("row", "col", None, None, None),
        P("row", "col"),
    )
    out_specs = (P(("col", "row"), None), P(("row", "col"), None), P(), P())
    return jax.shard_map(local, mesh=mesh, in_specs=in_specs, out_specs=out_specs, check_vma=False)
```

time: 497 us -> 186 us (0.37)
  the two profiles are of different devices: /device:TPU:0 before, /device:TPU:4 now
where the time goes in v4:
time: 186 us
  waiting for transfers between devices  88.6 us (48%)
  starting transfers between devices  40 us (22%)
  blocking collectives  34.7 us (19%)
  Pallas kernels  19.9 us (11%)
    ppermute x7, waiting for transfers between devices, butterfly(): lax.ppermute(value, axis, [(i, i ^ bit) for i in range(size)])  64.8 us
    all_to_all x1, blocking collectives, row_exchange(): return lax.all_to_all(value, 'row', 0, 0, axis_index_groups=SAME_CORE)  34.7 us
    ppermute x7, waiting for transfers between devices, col_shift(): return lax.ppermute(value, 'col', pairs)  19.7 us
    ppermute x7, starting transfers between devices, col_shift(): return lax.ppermute(value, 'col', pairs)  12.3 us
    ppermute x7, starting transfers between devices, butterfly(): lax.ppermute(value, axis, [(i, i ^ bit) for i in range(size)])  11.2 us
    all_to_all x1, starting transfers between devices, col_exchange(): return lax.all_to_all(value, 'col', 0, 0)  8.59 us
    pallas_call x2, Pallas kernels, forward(): pl.pallas_call(functools.partial(forward_kernel, which), out_shape=jax.Sh...  7.84 us
    all_to_all x1, starting transfers between devices, row_exchange(): return lax.all_to_all(value, 'row', 0, 0, axis_index_groups=SAME_CORE)  5.62 us
  transfers between devices with their start and end apart: 18, of which 11 were waited for; matrix products, arithmetic and copies ran while one was open for 1% of the time, Pallas kernels for 4%

profile of v4, /device:TPU:4, one launch (start us, length us, event | category | flops | bytes accessed | tf_op | source)
XLA Modules:
  0.0 186.4 jit_solution(1732713218104727200)
XLA Ops:
  0.6 5.1 %collective-permute-start.6 = (bf16[1024,128]{1,0:T(8,128)(2,1)}, bf16[1024,128]{1,0:T(8,128)(2,1)S(1)}, u32[]{:S(2)}, u32[]{:S(2)}) collective-permute-start(bf16[1024,128]{1,0:T(8,128)(2,1)} %rest_0_.3), channel_id=1, source_target_pairs={{0,7},{1,6},{2,1},{3,0},{4,3},{5,2},{6,5},{7,4},{8,15},{9,14},{10,... | collective-permute-start | bytes 786440 | tf_op jit(solution)/shard_map/ppermute | solution.py:356
  5.7 0.4 collective-permute-start.5
  6.2 0.0 collective-permute-start.4
  6.2 3.4 %collective-permute-start.3 = (bf16[1024,128]{1,0:T(8,128)(2,1)}, bf16[1024,128]{1,0:T(8,128)(2,1)S(1)}, u32[]{:S(2)}, u32[]{:S(2)}) collective-permute-start(bf16[1024,128]{1,0:T(8,128)(2,1)} %rest_0_.3), channel_id=1, source_target_pairs={{0,4},{1,5},{2,6},{3,7},{4,0},{5,1},{6,2},{7,3},{8,12},{9,13},{10,... | collective-permute-start | bytes 786440 | tf_op jit(solution)/shard_map/ppermute | solution.py:356
  9.6 2.6 %collective-permute-start.2 = (bf16[1024,128]{1,0:T(8,128)(2,1)}, bf16[1024,128]{1,0:T(8,128)(2,1)S(1)}, u32[]{:S(2)}, u32[]{:S(2)}) collective-permute-start(bf16[1024,128]{1,0:T(8,128)(2,1)} %rest_0_.3), channel_id=1, source_target_pairs={{0,3},{1,2},{2,5},{3,4},{4,7},{5,6},{6,1},{7,0},{8,11},{9,10},{10,... | collective-permute-start | bytes 786440 | tf_op jit(solution)/shard_map/ppermute | solution.py:356
  12.2 1.8 collective-permute-done.6.rest_7_
  14.0 0.0 collective-permute-start.1
  14.0 14.4 %collective-permute-done.5.rest_6_ = bf16[1024,128]{1,0:T(8,128)(2,1)S(1)} collective-permute-done((bf16[1024,128]{1,0:T(8,128)(2,1)}, bf16[1024,128]{1,0:T(8,128)(2,1)S(1)}, u32[]{:S(2)}, u32[]{:S(2)}) %collective-permute-start.5) | collective-permute-done | bytes 262176 | tf_op jit(solution)/shard_map/ppermute | solution.py:356
  28.4 0.8 collective-permute-start
  29.8 0.6 pad_add_fusion.where_ref
  30.4 2.9 %slot_lists.1.lists_ref = s32[1024]{0:T(1024)} custom-call(s32[3]{0:T(128)} %pad_add_fusion.where_ref, s32[128]{0:T(128)} %bitcast.15, s32[128]{0:T(128)} %bitcast.16, s32[1]{0:T(128)} %bitcast.10.count_ref), custom_call_target="tpu_custom_call" | custom-call | tf_op jit(solution)/shard_map/slot_lists/pallas_call | solution.py:75
  33.3 0.0 collective-permute-done.4.rest_5_
  33.3 0.0 collective-permute-done.3.rest_4_
  33.3 0.0 collective-permute-done.2.rest_3_
  33.3 0.0 collective-permute-done.1.rest_2_
  33.3 3.5 %collective-permute-done.rest_1_ = bf16[1024,128]{1,0:T(8,128)(2,1)S(1)} collective-permute-done((bf16[1024,128]{1,0:T(8,128)(2,1)}, bf16[1024,128]{1,0:T(8,128)(2,1)S(1)}, u32[]{:S(2)}, u32[]{:S(2)}) %collective-permute-start) | collective-permute-done | bytes 262176 | tf_op jit(solution)/shard_map/ppermute | solution.py:356
  36.8 4.0 %forward_tiles.2 = bf16[8,1024,128]{2,1,0:T(8,128)(2,1)S(1)} custom-call(s32[1024]{0:T(1024)} %slot_lists.1.lists_ref, bf16[128,256,256]{2,1,0:T(8,128)(2,1)} %bitcast.12, bf16[1024,128]{1,0:T(8,128)(2,1)} %rest_0_.3, bf16[1024,128]{1,0:T(8,128)(2,1)S(1)} %collective-permute-done.rest_1_, bf16[1024,128]{1,0:T(8,128)(2,1)S(1)} %collective-permute-done.1.rest_2_, ...), custom_call_target="tpu_custom_call" | custom-call | flops 1073741824 | bytes 16777216 | tf_op jit(solution)/shard_map/forward_tiles/pallas_call | solution.py:160
  40.8 2.2 %collective-permute-start.7 = (bf16[8,1024,128]{2,1,0:T(8,128)(2,1)S(1)}, bf16[8,1024,128]{2,1,0:T(8,128)(2,1)S(1)}, u32[]{:S(2)}, u32[]{:S(2)}) collective-permute-start(bf16[8,1024,128]{2,1,0:T(8,128)(2,1)S(1)} %forward_tiles.2), channel_id=1, source_target_pairs={{0,8},{8,0},{16,24},{24,16},{32,40},{40,32},{48,56},{56,48},{64,72... | collective-permute-start | bytes 6291464 | tf_op jit(solution)/shard_map/ppermute | solution.py:340
  43.0 3.9 %forward_tiles.3.mine_ref = bf16[8,1024,128]{2,1,0:T(8,128)(2,1)S(1)} custom-call(s32[1024]{0:T(1024)} %slot_lists.1.lists_ref, bf16[128,256,256]{2,1,0:T(8,128)(2,1)} %bitcast.13, bf16[1024,128]{1,0:T(8,128)(2,1)} %rest_0_.3, bf16[1024,128]{1,0:T(8,128)(2,1)S(1)} %collective-permute-done.rest_1_, bf16[1024,128]{1,0:T(8,128)(2,1)S(1)} %collective-permute-done.1.rest_2_, ...), custom_call_target="tpu_custom_call" | custom-call | flops 1073741824 | bytes 16777216 | tf_op jit(solution)/shard_map/forward_tiles/pallas_call | solution.py:160
  46.9 0.0 collective-permute-done.7.other_ref
  46.9 0.5 pair_sum.1
  47.4 0.0 copy-start
  47.4 0.0 copy-start.1
  47.4 0.0 copy-start.2
  47.4 34.7 %all_to_all.15.recv_ref = bf16[8,1024,128]{2,1,0:T(8,128)(2,1)S(1)} all-to-all(bf16[8,1024,128]{2,1,0:T(8,128)(2,1)S(1)} %pair_sum.1), channel_id=1, replica_groups={{0,16,32,48,64,80,96,112},{8,24,40,56,72,88,104,120},{1,17,33,49,65,81,..., dimensions={0} | all-to-all | bytes 4194304 | tf_op jit(solution)/shard_map/all_to_all | solution.py:344
  82.1 0.0 copy-done
  82.1 0.0 copy-done.1
  82.1 0.0 copy-done.2
  82.1 2.9 %dense_layer.1 = (bf16[1024,128]{1,0:T(8,128)(2,1)}, bf16[8,512,256]{2,1,0:T(8,128)(2,1)}, f32[136,128]{1,0:T(8,128)S(1)}) custom-call(bf16[8,1024,128]{2,1,0:T(8,128)(2,1)S(1)} %all_to_all.15.recv_ref, bf16[128,128]{1,0:T(8,128)(2,1)S(1)} %copy-done.1, f32[1,128]{1,0:T(1,128)S(1)} %bitcast.11, bf16[1024,128]{1,0:T(8,128)(2,1)S(1)} %copy-done), custom_call_target="tpu_custom_call" | custom-call | flops 100663296 | bytes 5242880 | tf_op jit(solution)/shard_map/dense_layer/pallas_call | solution.py:293
  85.1 5.6 %all-to-all-start.1 = ((bf16[8,512,256]{2,1,0:T(8,128)(2,1)}), bf16[8,512,256]{2,1,0:T(8,128)(2,1)S(1)}, u32[]{:S(2)}, u32[]{:S(2)}) async-start(bf16[8,512,256]{2,1,0:T(8,128)(2,1)} %get-tuple-element.17), calls=%async_computation.1 | async-start | bytes 4194304 | tf_op jit(solution)/shard_map/all_to_all | solution.py:344
  90.7 0.0 collective-permute-start.8
  90.7 1.3 collective-permute-done.8
  91.9 3.1 %collective-permute-start.9 = (f32[136,128]{1,0:T(8,128)S(1)}, f32[136,128]{1,0:T(8,128)S(1)}, u32[]{:S(2)}, u32[]{:S(2)}) collective-permute-start(f32[136,128]{1,0:T(8,128)S(1)} %add.21), channel_id=1, source_target_pairs={{0,16},{8,24},{16,0},{24,8},{32,48},{40,56},{48,32},{56,40},{64,80... | collective-permute-start | bytes 208904 | tf_op jit(solution)/shard_map/ppermute | solution.py:361
  95.0 22.7 %collective-permute-done.9 = f32[136,128]{1,0:T(8,128)S(1)} collective-permute-done((f32[136,128]{1,0:T(8,128)S(1)}, f32[136,128]{1,0:T(8,128)S(1)}, u32[]{:S(2)}, u32[]{:S(2)}) %collective-permute-start.9) | collective-permute-done | bytes 69664 | tf_op jit(solution)/shard_map/ppermute | solution.py:361
  117.7 1.7 collective-permute-start.10
  119.4 2.7 %collective-permute-done.10 = f32[136,128]{1,0:T(8,128)S(1)} collective-permute-done((f32[136,128]{1,0:T(8,128)S(1)}, f32[136,128]{1,0:T(8,128)S(1)}, u32[]{:S(2)}, u32[]{:S(2)}) %collective-permute-start.10) | collective-permute-done | bytes 69664 | tf_op jit(solution)/shard_map/ppermute | solution.py:361
  122.1 1.0 collective-permute-start.11
  123.1 4.9 %collective-permute-done.11 = f32[136,128]{1,0:T(8,128)S(1)} collective-permute-done((f32[136,128]{1,0:T(8,128)S(1)}, f32[136,128]{1,0:T(8,128)S(1)}, u32[]{:S(2)}, u32[]{:S(2)}) %collective-permute-start.11) | collective-permute-done | bytes 69664 | tf_op jit(solution)/shard_map/ppermute | solution.py:361
  128.0 0.0 all-to-all-done.1.mine_ref
  128.0 0.1 collective-permute-start.12
  128.1 4.1 %collective-permute-done.12.other_ref = bf16[8,512,256]{2,1,0:T(8,128)(2,1)S(1)} collective-permute-done((bf16[8,512,256]{2,1,0:T(8,128)(2,1)S(1)}, bf16[8,512,256]{2,1,0:T(8,128)(2,1)S(1)}, u32[]{:S(2)}, u32[]{:S(2)}) %collective-permute-start.12) | collective-permute-done | bytes 2097184 | tf_op jit(solution)/shard_map/ppermute | solution.py:340
  132.3 4.7 %backward_tiles.1 = bf16[8,512,256]{2,1,0:T(8,128)(2,1)} custom-call(s32[1024]{0:T(1024)} %slot_lists.1.lists_ref, bf16[128,256,256]{2,1,0:T(8,128)(2,1)} %bitcast.14, bf16[8,512,256]{2,1,0:T(8,128)(2,1)S(1)} %all-to-all-done.1.mine_ref, bf16[8,512,256]{2,1,0:T(8,128)(2,1)S(1)} %collective-permute-done.12.other_ref), custom_call_target="tpu_custom_call" | custom-call | flops 1073741824 | bytes 16777216 | tf_op jit(solution)/shard_map/backward_tiles/pallas_call | solution.py:230
  137.0 8.6 %all-to-all-start.2 = ((bf16[8,512,256]{2,1,0:T(8,128)(2,1)}), bf16[8,512,256]{2,1,0:T(8,128)(2,1)S(1)}, u32[]{:S(2)}, u32[]{:S(2)}) async-start(bf16[8,512,256]{2,1,0:T(8,128)(2,1)} %backward_tiles.1), calls=%async_computation.2 | async-start | bytes 4194304 | tf_op jit(solution)/shard_map/all_to_all | solution.py:348
  145.6 2.0 %collective-permute-start.13 = (f32[136,128]{1,0:T(8,128)S(1)}, f32[136,128]{1,0:T(8,128)S(1)}, u32[]{:S(2)}, u32[]{:S(2)}) collective-permute-start(f32[136,128]{1,0:T(8,128)S(1)} %add.24), channel_id=1, source_target_pairs={{0,1},{1,0},{2,3},{3,2},{4,5},{5,4},{6,7},{7,6},{8,9},{9,8},{10,11... | collective-permute-start | bytes 208904 | tf_op jit(solution)/shard_map/ppermute | solution.py:361
  147.6 26.3 %collective-permute-done.13 = f32[136,128]{1,0:T(8,128)S(1)} collective-permute-done((f32[136,128]{1,0:T(8,128)S(1)}, f32[136,128]{1,0:T(8,128)S(1)}, u32[]{:S(2)}, u32[]{:S(2)}) %collective-permute-start.13) | collective-permute-done | bytes 69664 | tf_op jit(solution)/shard_map/ppermute | solution.py:361
  173.9 0.6 collective-permute-start.14
  174.6 3.7 %collective-permute-done.14 = f32[136,128]{1,0:T(8,128)S(1)} collective-permute-done((f32[136,128]{1,0:T(8,128)S(1)}, f32[136,128]{1,0:T(8,128)S(1)}, u32[]{:S(2)}, u32[]{:S(2)}) %collective-permute-start.14) | collective-permute-done | bytes 69664 | tf_op jit(solution)/shard_map/ppermute | solution.py:361
  178.3 2.8 %collective-permute-start.15 = (f32[136,128]{1,0:T(8,128)S(1)}, f32[136,128]{1,0:T(8,128)S(1)}, u32[]{:S(2)}, u32[]{:S(2)}) collective-permute-start(f32[136,128]{1,0:T(8,128)S(1)} %add.26), channel_id=1, source_target_pairs={{0,4},{1,5},{2,6},{3,7},{4,0},{5,1},{6,2},{7,3},{8,12},{9,13},{10,... | collective-permute-start | bytes 208904 | tf_op jit(solution)/shard_map/ppermute | solution.py:361
  181.1 3.1 %collective-permute-done.15 = f32[136,128]{1,0:T(8,128)S(1)} collective-permute-done((f32[136,128]{1,0:T(8,128)S(1)}, f32[136,128]{1,0:T(8,128)S(1)}, u32[]{:S(2)}, u32[]{:S(2)}) %collective-permute-start.15) | collective-permute-done | bytes 69664 | tf_op jit(solution)/shard_map/ppermute | solution.py:361
  184.2 0.5 fusion
  184.8 0.6 slice_multiply_fusion
  185.4 0.0 all-to-all-done.2.recv_ref
  185.4 1.0 last_sum.1
  (7 shorter events, 0.1 us)
Async XLA Ops:
  0.6 13.4 %collective-permute-start.6 = (bf16[1024,128]{1,0:T(8,128)(2,1)}, bf16[1024,128]{1,0:T(8,128)(2,1)S(1)}, u32[]{:S(2)}, u32[]{:S(2)}) collective-permute-start(bf16[1024,128]{1,0:T(8,128)(2,1)} %rest_0_.3), channel_id=1, source_target_pairs={{0,7},{1,6},{2,1},{3,0},{4,3},{5,2},{6,5},{7,4},{8,15},{9,14},{10,... | collective-permute-start | bytes 786440 | tf_op jit(solution)/shard_map/ppermute | solution.py:356
  5.7 22.6 %collective-permute-start.5 = (bf16[1024,128]{1,0:T(8,128)(2,1)}, bf16[1024,128]{1,0:T(8,128)(2,1)S(1)}, u32[]{:S(2)}, u32[]{:S(2)}) collective-permute-start(bf16[1024,128]{1,0:T(8,128)(2,1)} %rest_0_.3), channel_id=1, source_target_pairs={{0,6},{1,7},{2,0},{3,1},{4,2},{5,3},{6,4},{7,5},{8,14},{9,15},{10,... | collective-permute-start | bytes 786440 | tf_op jit(solution)/shard_map/ppermute | solution.py:356
  6.2 27.1 %collective-permute-start.4 = (bf16[1024,128]{1,0:T(8,128)(2,1)}, bf16[1024,128]{1,0:T(8,128)(2,1)S(1)}, u32[]{:S(2)}, u32[]{:S(2)}) collective-permute-start(bf16[1024,128]{1,0:T(8,128)(2,1)} %rest_0_.3), channel_id=1, source_target_pairs={{0,5},{1,4},{2,7},{3,6},{4,1},{5,0},{6,3},{7,2},{8,13},{9,12},{10,... | collective-permute-start | bytes 786440 | tf_op jit(solution)/shard_map/ppermute | solution.py:356
  6.2 27.1 %collective-permute-start.3 = (bf16[1024,128]{1,0:T(8,128)(2,1)}, bf16[1024,128]{1,0:T(8,128)(2,1)S(1)}, u32[]{:S(2)}, u32[]{:S(2)}) collective-permute-start(bf16[1024,128]{1,0:T(8,128)(2,1)} %rest_0_.3), channel_id=1, source_target_pairs={{0,4},{1,5},{2,6},{3,7},{4,0},{5,1},{6,2},{7,3},{8,12},{9,13},{10,... | collective-permute-start | bytes 786440 | tf_op jit(solution)/shard_map/ppermute | solution.py:356
  9.6 23.7 %collective-permute-start.2 = (bf16[1024,128]{1,0:T(8,128)(2,1)}, bf16[1024,128]{1,0:T(8,128)(2,1)S(1)}, u32[]{:S(2)}, u32[]{:S(2)}) collective-permute-start(bf16[1024,128]{1,0:T(8,128)(2,1)} %rest_0_.3), channel_id=1, source_target_pairs={{0,3},{1,2},{2,5},{3,4},{4,7},{5,6},{6,1},{7,0},{8,11},{9,10},{10,... | collective-permute-start | bytes 786440 | tf_op jit(solution)/shard_map/ppermute | solution.py:356
  14.0 19.3 %collective-permute-start.1 = (bf16[1024,128]{1,0:T(8,128)(2,1)}, bf16[1024,128]{1,0:T(8,128)(2,1)S(1)}, u32[]{:S(2)}, u32[]{:S(2)}) collective-permute-start(bf16[1024,128]{1,0:T(8,128)(2,1)} %rest_0_.3), channel_id=1, source_target_pairs={{0,2},{1,3},{2,4},{3,5},{4,6},{5,7},{6,0},{7,1},{8,10},{9,11},{10,... | collective-permute-start | bytes 786440 | tf_op jit(solution)/shard_map/ppermute | solution.py:356
  28.4 8.4 %collective-permute-start = (bf16[1024,128]{1,0:T(8,128)(2,1)}, bf16[1024,128]{1,0:T(8,128)(2,1)S(1)}, u32[]{:S(2)}, u32[]{:S(2)}) collective-permute-start(bf16[1024,128]{1,0:T(8,128)(2,1)} %rest_0_.3), channel_id=1, source_target_pairs={{0,1},{1,0},{2,3},{3,2},{4,5},{5,4},{6,7},{7,6},{8,9},{9,8},{10,11... | collective-permute-start | bytes 786440 | tf_op jit(solution)/shard_map/ppermute | solution.py:356
  40.8 6.1 %collective-permute-start.7 = (bf16[8,1024,128]{2,1,0:T(8,128)(2,1)S(1)}, bf16[8,1024,128]{2,1,0:T(8,128)(2,1)S(1)}, u32[]{:S(2)}, u32[]{:S(2)}) collective-permute-start(bf16[8,1024,128]{2,1,0:T(8,128)(2,1)S(1)} %forward_tiles.2), channel_id=1, source_target_pairs={{0,8},{8,0},{16,24},{24,16},{32,40},{40,32},{48,56},{56,48},{64,72... | collective-permute-start | bytes 6291464 | tf_op jit(solution)/shard_map/ppermute | solution.py:340
  47.4 34.7 %copy-start = (bf16[1024,128]{1,0:T(8,128)(2,1)S(1)}, bf16[1024,128]{1,0:T(8,128)(2,1)}, u32[]{:S(2)}) copy-start(bf16[1024,128]{1,0:T(8,128)(2,1)} %cot_ref.1) | copy-start | bytes 786436
  47.4 34.7 %copy-start.1 = (bf16[128,128]{1,0:T(8,128)(2,1)S(1)}, bf16[128,128]{1,0:T(8,128)(2,1)}, u32[]{:S(2)}) copy-start(bf16[128,128]{1,0:T(8,128)(2,1)} %weight_ref.1) | copy-start | bytes 98308
  47.4 34.7 %copy-start.2 = (f32[128]{0:T(128)S(1)}, f32[128]{0:T(128)}, u32[]{:S(2)}) copy-start(f32[128]{0:T(128)} %param.10) | copy-start | bytes 1540
  85.1 43.0 %all-to-all-start.1 = ((bf16[8,512,256]{2,1,0:T(8,128)(2,1)}), bf16[8,512,256]{2,1,0:T(8,128)(2,1)S(1)}, u32[]{:S(2)}, u32[]{:S(2)}) async-start(bf16[8,512,256]{2,1,0:T(8,128)(2,1)} %get-tuple-element.17), calls=%async_computation.1 | async-start | bytes 4194304 | tf_op jit(solution)/shard_map/all_to_all | solution.py:344
  90.7 1.3 collective-permute-start.8
  91.9 25.7 %collective-permute-start.9 = (f32[136,128]{1,0:T(8,128)S(1)}, f32[136,128]{1,0:T(8,128)S(1)}, u32[]{:S(2)}, u32[]{:S(2)}) collective-permute-start(f32[136,128]{1,0:T(8,128)S(1)} %add.21), channel_id=1, source_target_pairs={{0,16},{8,24},{16,0},{24,8},{32,48},{40,56},{48,32},{56,40},{64,80... | collective-permute-start | bytes 208904 | tf_op jit(solution)/shard_map/ppermute | solution.py:361
  117.7 4.4 %collective-permute-start.10 = (f32[136,128]{1,0:T(8,128)S(1)}, f32[136,128]{1,0:T(8,128)S(1)}, u32[]{:S(2)}, u32[]{:S(2)}) collective-permute-start(f32[136,128]{1,0:T(8,128)S(1)} %add.22), channel_id=1, source_target_pairs={{0,32},{8,40},{16,48},{24,56},{32,0},{40,8},{48,16},{56,24},{64,96... | collective-permute-start | bytes 208904 | tf_op jit(solution)/shard_map/ppermute | solution.py:361
  122.1 5.9 %collective-permute-start.11 = (f32[136,128]{1,0:T(8,128)S(1)}, f32[136,128]{1,0:T(8,128)S(1)}, u32[]{:S(2)}, u32[]{:S(2)}) collective-permute-start(f32[136,128]{1,0:T(8,128)S(1)} %add.23), channel_id=1, source_target_pairs={{0,64},{8,72},{16,80},{24,88},{32,96},{40,104},{48,112},{56,120},{... | collective-permute-start | bytes 208904 | tf_op jit(solution)/shard_map/ppermute | solution.py:361
  128.0 4.2 %collective-permute-start.12 = (bf16[8,512,256]{2,1,0:T(8,128)(2,1)S(1)}, bf16[8,512,256]{2,1,0:T(8,128)(2,1)S(1)}, u32[]{:S(2)}, u32[]{:S(2)}) collective-permute-start(bf16[8,512,256]{2,1,0:T(8,128)(2,1)S(1)} %all-to-all-done.1.mine_ref), channel_id=1, source_target_pairs={{0,8},{8,0},{16,24},{24,16},{32,40},{40,32},{48,56},{56,48},{64,72... | collective-permute-start | bytes 6291464 | tf_op jit(solution)/shard_map/ppermute | solution.py:340
  137.0 48.4 %all-to-all-start.2 = ((bf16[8,512,256]{2,1,0:T(8,128)(2,1)}), bf16[8,512,256]{2,1,0:T(8,128)(2,1)S(1)}, u32[]{:S(2)}, u32[]{:S(2)}) async-start(bf16[8,512,256]{2,1,0:T(8,128)(2,1)} %backward_tiles.1), calls=%async_computation.2 | async-start | bytes 4194304 | tf_op jit(solution)/shard_map/all_to_all | solution.py:348
  145.6 28.4 %collective-permute-start.13 = (f32[136,128]{1,0:T(8,128)S(1)}, f32[136,128]{1,0:T(8,128)S(1)}, u32[]{:S(2)}, u32[]{:S(2)}) collective-permute-start(f32[136,128]{1,0:T(8,128)S(1)} %add.24), channel_id=1, source_target_pairs={{0,1},{1,0},{2,3},{3,2},{4,5},{5,4},{6,7},{7,6},{8,9},{9,8},{10,11... | collective-permute-start | bytes 208904 | tf_op jit(solution)/shard_map/ppermute | solution.py:361
  173.9 4.4 %collective-permute-start.14 = (f32[136,128]{1,0:T(8,128)S(1)}, f32[136,128]{1,0:T(8,128)S(1)}, u32[]{:S(2)}, u32[]{:S(2)}) collective-permute-start(f32[136,128]{1,0:T(8,128)S(1)} %add.25), channel_id=1, source_target_pairs={{0,2},{1,3},{2,0},{3,1},{4,6},{5,7},{6,4},{7,5},{8,10},{9,11},{10,... | collective-permute-start | bytes 208904 | tf_op jit(solution)/shard_map/ppermute | solution.py:361
  178.3 5.9 %collective-permute-start.15 = (f32[136,128]{1,0:T(8,128)S(1)}, f32[136,128]{1,0:T(8,128)S(1)}, u32[]{:S(2)}, u32[]{:S(2)}) collective-permute-start(f32[136,128]{1,0:T(8,128)S(1)} %add.26), channel_id=1, source_target_pairs={{0,4},{1,5},{2,6},{3,7},{4,0},{5,1},{6,2},{7,3},{8,12},{9,13},{10,... | collective-permute-start | bytes 208904 | tf_op jit(solution)/shard_map/ppermute | solution.py:361

commit v5 on v4

--- a/solution.py
+++ b/solution.py
@@ -40,7 +40,7 @@
 
 
 def prep_kernel(where_ref, out_ref, in_ref, count_ref, lists_ref):
-    core, z, y = (where_ref[i] for i in range(3))
+    core = where_ref[0]
 
     def clear(i, carry):
         lists_ref[i] = FWD_DUMMY << 16
@@ -56,10 +56,8 @@
         s = in_ref[k]
         rel = jnp.bitwise_xor((t >> 2) & 1, core)
         to_t = ((t >> 3) << 2) | (t & 3)
-        dy, dz = ((s >> 2) + y) & 1, (z - (s >> 3)) & 3
-        src_f = (((dz << 1) | dy) << 2) | (s & 3)
         at_f = jnp.where(rel == 0, f0, LIST + f1)
-        lists_ref[at_f] = k | (src_f << 8) | (to_t << 16)
+        lists_ref[at_f] = k | (s << 8) | (to_t << 16)
         lists_ref[2 * LIST + k] = k | ((rel * 32 + to_t) << 8) | (s << 16)
         return (f0 + 1 - rel, f1 + rel)
 
@@ -130,25 +128,17 @@
 )
 
 
-def forward_kernel(which, lists_ref, vals, *rest):
-    blocks = rest[:NPEER]
-    out_ref, x, buf, acc, sems, own_sem = rest[NPEER:]
-    own = pltpu.make_async_copy(blocks[0], x.at[pl.ds(0, 4 * TILE)], own_sem)
-    own.start()
-
+def forward_kernel(which, lists_ref, vals, x, out_ref, buf, acc, sems):
     def ready():
         def clear(i, carry):
             acc[i] = jnp.zeros((TILE, FEAT), f32)
             return carry
 
         lax.fori_loop(0, FWD_DUMMY, clear, 0)
-        for k in range(1, NPEER):
-            x[pl.ds(k * 4 * TILE, 4 * TILE), :] = blocks[k][...]
-        own.wait()
 
     def product(tile, source):
-        rows = x[pl.ds(pl.multiple_of(source * TILE, TILE), TILE), :]
-        return jnp.dot(tile, rows, preferred_element_type=f32)
+        rows = pl.ds(pl.multiple_of((source & 3) * TILE, TILE), TILE)
+        return jnp.dot(tile, x[source >> 2, rows, :], preferred_element_type=f32)
 
     tile_loop(which, lists_ref, vals, buf, sems, acc, ready, product)
 
@@ -156,23 +146,21 @@
         out_ref[i // 4, pl.ds((i % 4) * TILE, TILE), :] = acc[i].astype(bf16)
 
 
-def forward(which, lists, values, blocks):
+def forward(which, lists, values, sources):
     return pl.pallas_call(
         functools.partial(forward_kernel, which),
         out_shape=jax.ShapeDtypeStruct((NPEER, 4 * TILE, FEAT), bf16),
-        in_specs=[smem(), hbm(), hbm()] + [vmem()] * (NPEER - 1),
+        in_specs=[smem(), hbm(), vmem()],
         out_specs=vmem(),
         scratch_shapes=[
-            pltpu.VMEM((NPEER * 4 * TILE, FEAT), bf16),
             pltpu.VMEM((DEPTH, TILE, TILE), bf16),
             pltpu.VMEM((FWD_DUMMY + 1, TILE, FEAT), f32),
             pltpu.SemaphoreType.DMA((DEPTH,)),
-            pltpu.SemaphoreType.DMA,
         ],
         compiler_params=params(),
         cost_estimate=TILES_COST,
         name="forward_tiles",
-    )(in_hbm(lists), in_hbm(values), in_hbm(blocks[0]), *blocks[1:])
+    )(in_hbm(lists), in_hbm(values), sources)
 
 
 def pair_sum_kernel(mine_ref, other_ref, out_ref):
@@ -348,44 +336,42 @@
     return lax.all_to_all(value, "col", 0, 0)
 
 
-def col_shift(value, k):
-    pairs = []
-    for c in range(8):
-        z, y = c // 2, c % 2
-        pairs.append((c, ((z + k // 2) % 4) * 2 + (y + k) % 2))
-    return lax.ppermute(value, "col", pairs)
-
-
-def butterfly(value, axis, size, bits):
-    for bit in bits:
-        value = value + lax.ppermute(value, axis, [(i, i ^ bit) for i in range(size)])
-    return value
+def partner(value, axis, size, bit):
+    return lax.ppermute(value, axis, [(i, i ^ bit) for i in range(size)])
 
 
 def local(features, weight, layer_bias, cotangent, tile_out, tile_in, tile_vals, tile_count):
     values = tile_vals[0, 0]
-    row, col = lax.axis_index("row"), lax.axis_index("col")
-    where = jnp.stack([row & 1, col >> 1, col & 1]).astype(jnp.int32)
+    where = (lax.axis_index("row") & 1).astype(jnp.int32).reshape(1)
     lists = prep(where, tile_out[0, 0], tile_in[0, 0], tile_count[0])
     bias = layer_bias.reshape(1, FEAT)
     order = lax.optimization_barrier
 
-    blocks = [features] + [col_shift(features, k) for k in range(1, NPEER)]
-
-    other = forward(1, lists, values, blocks)
+    sources = col_exchange(jnp.broadcast_to(features, (NPEER, 4 * TILE, FEAT)))
+    other = forward(1, lists, values, sources)
     other, lists = order((other, lists))
-    mine = forward(0, lists, values, blocks)
+    mine = forward(0, lists, values, sources)
     recv = row_exchange(pair_sum(mine, to_other_core(other)))
-    hidden, grad, wsum = dense(recv, weight, bias, cotangent)
+    hidden, grad, total = dense(recv, weight, bias, cotangent)
+
     grads = row_exchange(grad)
-    wsum = butterfly(wsum, "row", 16, (1, 2, 4, 8))
-    grads, wsum = order((grads, wsum))
-    back = backward(lists, values, grads, to_other_core(grads))
+    for bit in (2, 4):
+        total = total + partner(total, "col", 8, bit)
+    total = total + partner(total, "row", 16, 1)
+    grads, total = order((grads, total))
+    other = to_other_core(grads)
+    total = total + partner(total, "col", 8, 1)
+    other, total = order((other, total))
+    second = partner(total, "row", 16, 2)
+    back = backward(lists, values, grads, other)
+    back, second = order((back, second))
+    total = total + second
     back = col_exchange(back)
-    wsum = butterfly(wsum, "col", 8, (1, 2, 4))
+    for bit in (4, 8):
+        total = total + partner(total, "row", 16, bit)
     scale = 1.0 / math.sqrt(4 * TILE * 128)
-    weight_grad = wsum[:FEAT] * scale
-    bias_grad = wsum[FEAT] * scale
+    weight_grad = total[:FEAT] * scale
+    bias_grad = total[FEAT] * scale
     back, weight_grad, bias_grad = order((back, weight_grad, bias_grad))
     feature_grad = last(back)
     return (hidden, feature_grad, weight_grad, bias_grad)

time: 186 us -> 167 us (0.90)
  the two profiles are of different devices: /device:TPU:4 before, /device:TPU:1 now
where the time goes in v5:
time: 167 us; the launch traced here: 164 us
  waiting for transfers between devices  61.9 us (37%)
  starting transfers between devices  40 us (24%)
  blocking collectives  29.2 us (17%)
  Pallas kernels  28.2 us (17%)
  local copies, waits for them, and re-layouts  2.58 us (2%)
    all_to_all x2, waiting for transfers between devices, col_exchange(): return lax.all_to_all(value, 'col', 0, 0)  37.7 us
    all_to_all x1, blocking collectives, row_exchange(): return lax.all_to_all(value, 'row', 0, 0, axis_index_groups=SAME_CORE)  29.2 us
    ppermute x7, starting transfers between devices, partner(): return lax.ppermute(value, axis, [(i, i ^ bit) for i in range(size)])  18.4 us
    all_to_all x2, starting transfers between devices, col_exchange(): return lax.all_to_all(value, 'col', 0, 0)  14 us
    ppermute x7, waiting for transfers between devices, partner(): return lax.ppermute(value, axis, [(i, i ^ bit) for i in range(size)])  12.6 us
    all_to_all x1, waiting for transfers between devices, row_exchange(): return lax.all_to_all(value, 'row', 0, 0, axis_index_groups=SAME_CORE)  11.5 us
    pallas_call x2, Pallas kernels, forward(): pl.pallas_call(functools.partial(forward_kernel, which), out_shape=jax.Sh...  10.8 us
    pallas_call x1, Pallas kernels, backward(): pl.pallas_call(backward_kernel, out_shape=pltpu.HBM((NPEER, 4 * FEAT, TIL...  8.83 us
  transfers between devices with their start and end apart: 12, of which 9 were waited for; matrix products, arithmetic and copies ran while one was open for 1% of the time, Pallas kernels for 11%

profile of v5, /device:TPU:1, one launch (start us, length us, event | category | flops | bytes accessed | tf_op | source)
XLA Modules:
  0.0 164.5 jit_solution(188848010709415979)
XLA Ops:
  0.6 2.6 %broadcast_in_dim.3 = bf16[8,1024,128]{2,1,0:T(8,128)(2,1)} broadcast(bf16[1024,128]{1,0:T(8,128)(2,1)} %param.8), dimensions={1,2} | broadcast | bytes 2359296 | tf_op jit(solution)/shard_map/broadcast_in_dim | solution.py:350
  3.2 6.9 %all-to-all-start = ((bf16[8,1024,128]{2,1,0:T(8,128)(2,1)}), bf16[8,1024,128]{2,1,0:T(8,128)(2,1)S(1)}, u32[]{:S(2)}, u32[]{:S(2)}) async-start(bf16[8,1024,128]{2,1,0:T(8,128)(2,1)} %broadcast_in_dim.3), calls=%async_computation | async-start | bytes 4194304 | tf_op jit(solution)/shard_map/all_to_all | solution.py:336
  10.7 4.0 %slot_lists.1.lists_ref = s32[1024]{0:T(1024)} custom-call(s32[1]{0:T(128)} %bitcast.where_ref, s32[128]{0:T(128)} %bitcast.13, s32[128]{0:T(128)} %bitcast.14, s32[1]{0:T(128)} %bitcast.8.count_ref), custom_call_target="tpu_custom_call" | custom-call | tf_op jit(solution)/shard_map/slot_lists/pallas_call | solution.py:73
  14.8 21.4 %all-to-all-done.x = bf16[8,1024,128]{2,1,0:T(8,128)(2,1)S(1)} async-done(((bf16[8,1024,128]{2,1,0:T(8,128)(2,1)}), bf16[8,1024,128]{2,1,0:T(8,128)(2,1)S(1)}, u32[]{:S(2)}, u32[]{:S(2)}) %all-to-all-start) | async-done | bytes 2097184 | tf_op jit(solution)/shard_map/all_to_all | solution.py:336
  36.1 5.2 %forward_tiles.2 = bf16[8,1024,128]{2,1,0:T(8,128)(2,1)S(1)} custom-call(s32[1024]{0:T(1024)} %slot_lists.1.lists_ref, bf16[128,256,256]{2,1,0:T(8,128)(2,1)} %bitcast.10, bf16[8,1024,128]{2,1,0:T(8,128)(2,1)S(1)} %all-to-all-done.x), custom_call_target="tpu_custom_call" | custom-call | flops 1073741824 | bytes 16777216 | tf_op jit(solution)/shard_map/forward_tiles/pallas_call | solution.py:150
  41.3 1.0 collective-permute-start
  42.4 5.6 %forward_tiles.3.mine_ref = bf16[8,1024,128]{2,1,0:T(8,128)(2,1)S(1)} custom-call(s32[1024]{0:T(1024)} %slot_lists.1.lists_ref, bf16[128,256,256]{2,1,0:T(8,128)(2,1)} %bitcast.11, bf16[8,1024,128]{2,1,0:T(8,128)(2,1)S(1)} %all-to-all-done.x), custom_call_target="tpu_custom_call" | custom-call | flops 1073741824 | bytes 16777216 | tf_op jit(solution)/shard_map/forward_tiles/pallas_call | solution.py:150
  48.0 0.0 collective-permute-done.other_ref
  48.0 0.5 pair_sum.1
  48.5 0.0 copy-start
  48.5 0.0 copy-start.1
  48.6 0.0 copy-start.2
  48.6 29.2 %all_to_all.20.recv_ref = bf16[8,1024,128]{2,1,0:T(8,128)(2,1)S(1)} all-to-all(bf16[8,1024,128]{2,1,0:T(8,128)(2,1)S(1)} %pair_sum.1), channel_id=1, replica_groups={{0,16,32,48,64,80,96,112},{8,24,40,56,72,88,104,120},{1,17,33,49,65,81,..., dimensions={0} | all-to-all | bytes 4194304 | tf_op jit(solution)/shard_map/all_to_all | solution.py:332
  77.8 0.0 copy-done
  77.8 0.0 copy-done.1
  77.8 0.0 copy-done.2
  77.8 2.9 %dense_layer.1 = (bf16[1024,128]{1,0:T(8,128)(2,1)}, bf16[8,512,256]{2,1,0:T(8,128)(2,1)}, f32[136,128]{1,0:T(8,128)S(1)}) custom-call(bf16[8,1024,128]{2,1,0:T(8,128)(2,1)S(1)} %all_to_all.20.recv_ref, bf16[128,128]{1,0:T(8,128)(2,1)S(1)} %copy-done.1, f32[1,128]{1,0:T(1,128)S(1)} %bitcast.9, bf16[1024,128]{1,0:T(8,128)(2,1)S(1)} %copy-done), custom_call_target="tpu_custom_call" | custom-call | flops 100663296 | bytes 5242880 | tf_op jit(solution)/shard_map/dense_layer/pallas_call | solution.py:281
  80.7 3.6 %all-to-all-start.2 = ((bf16[8,512,256]{2,1,0:T(8,128)(2,1)}), bf16[8,512,256]{2,1,0:T(8,128)(2,1)S(1)}, u32[]{:S(2)}, u32[]{:S(2)}) async-start(bf16[8,512,256]{2,1,0:T(8,128)(2,1)} %get-tuple-element.21), calls=%async_computation.2 | async-start | bytes 4194304 | tf_op jit(solution)/shard_map/all_to_all | solution.py:332
  84.3 2.3 %collective-permute-start.1 = (f32[136,128]{1,0:T(8,128)S(1)}, f32[136,128]{1,0:T(8,128)S(1)}, u32[]{:S(2)}, u32[]{:S(2)}) collective-permute-start(f32[136,128]{1,0:T(8,128)S(1)} %get-tuple-element.22), channel_id=1, source_target_pairs={{0,2},{1,3},{2,0},{3,1},{4,6},{5,7},{6,4},{7,5},{8,10},{9,11},{10,... | collective-permute-start | bytes 208904 | tf_op jit(solution)/shard_map/ppermute | solution.py:340
  86.7 1.7 %collective-permute-done.1 = f32[136,128]{1,0:T(8,128)S(1)} collective-permute-done((f32[136,128]{1,0:T(8,128)S(1)}, f32[136,128]{1,0:T(8,128)S(1)}, u32[]{:S(2)}, u32[]{:S(2)}) %collective-permute-start.1) | collective-permute-done | bytes 69664 | tf_op jit(solution)/shard_map/ppermute | solution.py:340
  88.4 4.5 %collective-permute-start.2 = (f32[136,128]{1,0:T(8,128)S(1)}, f32[136,128]{1,0:T(8,128)S(1)}, u32[]{:S(2)}, u32[]{:S(2)}) collective-permute-start(f32[136,128]{1,0:T(8,128)S(1)} %add.21), channel_id=1, source_target_pairs={{0,4},{1,5},{2,6},{3,7},{4,0},{5,1},{6,2},{7,3},{8,12},{9,13},{10,... | collective-permute-start | bytes 208904 | tf_op jit(solution)/shard_map/ppermute | solution.py:340
  92.9 2.1 %collective-permute-done.2 = f32[136,128]{1,0:T(8,128)S(1)} collective-permute-done((f32[136,128]{1,0:T(8,128)S(1)}, f32[136,128]{1,0:T(8,128)S(1)}, u32[]{:S(2)}, u32[]{:S(2)}) %collective-permute-start.2) | collective-permute-done | bytes 69664 | tf_op jit(solution)/shard_map/ppermute | solution.py:340
  95.0 3.9 %collective-permute-start.3 = (f32[136,128]{1,0:T(8,128)S(1)}, f32[136,128]{1,0:T(8,128)S(1)}, u32[]{:S(2)}, u32[]{:S(2)}) collective-permute-start(f32[136,128]{1,0:T(8,128)S(1)} %add.22), channel_id=1, source_target_pairs={{0,8},{8,0},{16,24},{24,16},{32,40},{40,32},{48,56},{56,48},{64,72... | collective-permute-start | bytes 208904 | tf_op jit(solution)/shard_map/ppermute | solution.py:340
  99.0 0.9 collective-permute-done.3
  99.9 11.5 %all-to-all-done.2.mine_ref = bf16[8,512,256]{2,1,0:T(8,128)(2,1)S(1)} async-done(((bf16[8,512,256]{2,1,0:T(8,128)(2,1)}), bf16[8,512,256]{2,1,0:T(8,128)(2,1)S(1)}, u32[]{:S(2)}, u32[]{:S(2)}) %all-to-all-start.2) | async-done | bytes 2097184 | tf_op jit(solution)/shard_map/all_to_all | solution.py:332
  111.4 3.0 %collective-permute-start.4 = (bf16[8,512,256]{2,1,0:T(8,128)(2,1)S(1)}, bf16[8,512,256]{2,1,0:T(8,128)(2,1)S(1)}, u32[]{:S(2)}, u32[]{:S(2)}) collective-permute-start(bf16[8,512,256]{2,1,0:T(8,128)(2,1)S(1)} %all-to-all-done.2.mine_ref), channel_id=1, source_target_pairs={{0,8},{8,0},{16,24},{24,16},{32,40},{40,32},{48,56},{56,48},{64,72... | collective-permute-start | bytes 6291464 | tf_op jit(solution)/shard_map/ppermute | solution.py:328
  114.4 3.1 %collective-permute-start.5 = (f32[136,128]{1,0:T(8,128)S(1)}, f32[136,128]{1,0:T(8,128)S(1)}, u32[]{:S(2)}, u32[]{:S(2)}) collective-permute-start(f32[136,128]{1,0:T(8,128)S(1)} %add.23), channel_id=1, source_target_pairs={{0,1},{1,0},{2,3},{3,2},{4,5},{5,4},{6,7},{7,6},{8,9},{9,8},{10,11... | collective-permute-start | bytes 208904 | tf_op jit(solution)/shard_map/ppermute | solution.py:340
  117.5 2.6 %collective-permute-done.5 = f32[136,128]{1,0:T(8,128)S(1)} collective-permute-done((f32[136,128]{1,0:T(8,128)S(1)}, f32[136,128]{1,0:T(8,128)S(1)}, u32[]{:S(2)}, u32[]{:S(2)}) %collective-permute-start.5) | collective-permute-done | bytes 69664 | tf_op jit(solution)/shard_map/ppermute | solution.py:340
  120.1 0.0 collective-permute-done.4.other_ref
  120.1 0.9 collective-permute-start.6
  121.0 8.8 %backward_tiles.1 = bf16[8,512,256]{2,1,0:T(8,128)(2,1)} custom-call(s32[1024]{0:T(1024)} %slot_lists.1.lists_ref, bf16[128,256,256]{2,1,0:T(8,128)(2,1)} %bitcast.12, bf16[8,512,256]{2,1,0:T(8,128)(2,1)S(1)} %all-to-all-done.2.mine_ref, bf16[8,512,256]{2,1,0:T(8,128)(2,1)S(1)} %collective-permute-done.4.other_ref), custom_call_target="tpu_custom_call" | custom-call | flops 1073741824 | bytes 16777216 | tf_op jit(solution)/shard_map/backward_tiles/pallas_call | solution.py:218
  129.8 0.0 collective-permute-done.6
  129.8 7.1 %all-to-all-start.3 = ((bf16[8,512,256]{2,1,0:T(8,128)(2,1)}), bf16[8,512,256]{2,1,0:T(8,128)(2,1)S(1)}, u32[]{:S(2)}, u32[]{:S(2)}) async-start(bf16[8,512,256]{2,1,0:T(8,128)(2,1)} %backward_tiles.1), calls=%async_computation.3 | async-start | bytes 4194304 | tf_op jit(solution)/shard_map/all_to_all | solution.py:336
  137.0 1.7 %collective-permute-start.7 = (f32[136,128]{1,0:T(8,128)S(1)}, f32[136,128]{1,0:T(8,128)S(1)}, u32[]{:S(2)}, u32[]{:S(2)}) collective-permute-start(f32[136,128]{1,0:T(8,128)S(1)} %add.25), channel_id=1, source_target_pairs={{0,32},{8,40},{16,48},{24,56},{32,0},{40,8},{48,16},{56,24},{64,96... | collective-permute-start | bytes 208904 | tf_op jit(solution)/shard_map/ppermute | solution.py:340
  138.6 2.2 %collective-permute-done.7 = f32[136,128]{1,0:T(8,128)S(1)} collective-permute-done((f32[136,128]{1,0:T(8,128)S(1)}, f32[136,128]{1,0:T(8,128)S(1)}, u32[]{:S(2)}, u32[]{:S(2)}) %collective-permute-start.7) | collective-permute-done | bytes 69664 | tf_op jit(solution)/shard_map/ppermute | solution.py:340
  140.9 1.9 %collective-permute-start.8 = (f32[136,128]{1,0:T(8,128)S(1)}, f32[136,128]{1,0:T(8,128)S(1)}, u32[]{:S(2)}, u32[]{:S(2)}) collective-permute-start(f32[136,128]{1,0:T(8,128)S(1)} %add.26), channel_id=1, source_target_pairs={{0,64},{8,72},{16,80},{24,88},{32,96},{40,104},{48,112},{56,120},{... | collective-permute-start | bytes 208904 | tf_op jit(solution)/shard_map/ppermute | solution.py:340
  142.8 3.1 %collective-permute-done.8 = f32[136,128]{1,0:T(8,128)S(1)} collective-permute-done((f32[136,128]{1,0:T(8,128)S(1)}, f32[136,128]{1,0:T(8,128)S(1)}, u32[]{:S(2)}, u32[]{:S(2)}) %collective-permute-start.8) | collective-permute-done | bytes 69664 | tf_op jit(solution)/shard_map/ppermute | solution.py:340
  145.9 0.5 fusion
  146.4 0.6 slice_multiply_fusion
  147.1 16.4 %all-to-all-done.3.recv_ref = bf16[8,512,256]{2,1,0:T(8,128)(2,1)S(1)} async-done(((bf16[8,512,256]{2,1,0:T(8,128)(2,1)}), bf16[8,512,256]{2,1,0:T(8,128)(2,1)S(1)}, u32[]{:S(2)}, u32[]{:S(2)}) %all-to-all-start.3) | async-done | bytes 2097184 | tf_op jit(solution)/shard_map/all_to_all | solution.py:336
  163.5 1.0 last_sum.1
  (7 shorter events, 0.1 us)
Async XLA Ops:
  3.2 32.9 %all-to-all-start = ((bf16[8,1024,128]{2,1,0:T(8,128)(2,1)}), bf16[8,1024,128]{2,1,0:T(8,128)(2,1)S(1)}, u32[]{:S(2)}, u32[]{:S(2)}) async-start(bf16[8,1024,128]{2,1,0:T(8,128)(2,1)} %broadcast_in_dim.3), calls=%async_computation | async-start | bytes 4194304 | tf_op jit(solution)/shard_map/all_to_all | solution.py:336
  41.3 6.7 %collective-permute-start = (bf16[8,1024,128]{2,1,0:T(8,128)(2,1)S(1)}, bf16[8,1024,128]{2,1,0:T(8,128)(2,1)S(1)}, u32[]{:S(2)}, u32[]{:S(2)}) collective-permute-start(bf16[8,1024,128]{2,1,0:T(8,128)(2,1)S(1)} %forward_tiles.2), channel_id=1, source_target_pairs={{0,8},{8,0},{16,24},{24,16},{32,40},{40,32},{48,56},{56,48},{64,72... | collective-permute-start | bytes 6291464 | tf_op jit(solution)/shard_map/ppermute | solution.py:328
  48.5 29.2 %copy-start = (bf16[1024,128]{1,0:T(8,128)(2,1)S(1)}, bf16[1024,128]{1,0:T(8,128)(2,1)}, u32[]{:S(2)}) copy-start(bf16[1024,128]{1,0:T(8,128)(2,1)} %cot_ref.1) | copy-start | bytes 786436
  48.5 29.2 %copy-start.1 = (bf16[128,128]{1,0:T(8,128)(2,1)S(1)}, bf16[128,128]{1,0:T(8,128)(2,1)}, u32[]{:S(2)}) copy-start(bf16[128,128]{1,0:T(8,128)(2,1)} %weight_ref.1) | copy-start | bytes 98308
  48.6 29.2 %copy-start.2 = (f32[128]{0:T(128)S(1)}, f32[128]{0:T(128)}, u32[]{:S(2)}) copy-start(f32[128]{0:T(128)} %param.10) | copy-start | bytes 1540
  80.7 30.7 %all-to-all-start.2 = ((bf16[8,512,256]{2,1,0:T(8,128)(2,1)}), bf16[8,512,256]{2,1,0:T(8,128)(2,1)S(1)}, u32[]{:S(2)}, u32[]{:S(2)}) async-start(bf16[8,512,256]{2,1,0:T(8,128)(2,1)} %get-tuple-element.21), calls=%async_computation.2 | async-start | bytes 4194304 | tf_op jit(solution)/shard_map/all_to_all | solution.py:332
  84.3 4.0 %collective-permute-start.1 = (f32[136,128]{1,0:T(8,128)S(1)}, f32[136,128]{1,0:T(8,128)S(1)}, u32[]{:S(2)}, u32[]{:S(2)}) collective-permute-start(f32[136,128]{1,0:T(8,128)S(1)} %get-tuple-element.22), channel_id=1, source_target_pairs={{0,2},{1,3},{2,0},{3,1},{4,6},{5,7},{6,4},{7,5},{8,10},{9,11},{10,... | collective-permute-start | bytes 208904 | tf_op jit(solution)/shard_map/ppermute | solution.py:340
  88.4 6.7 %collective-permute-start.2 = (f32[136,128]{1,0:T(8,128)S(1)}, f32[136,128]{1,0:T(8,128)S(1)}, u32[]{:S(2)}, u32[]{:S(2)}) collective-permute-start(f32[136,128]{1,0:T(8,128)S(1)} %add.21), channel_id=1, source_target_pairs={{0,4},{1,5},{2,6},{3,7},{4,0},{5,1},{6,2},{7,3},{8,12},{9,13},{10,... | collective-permute-start | bytes 208904 | tf_op jit(solution)/shard_map/ppermute | solution.py:340
  95.0 4.9 %collective-permute-start.3 = (f32[136,128]{1,0:T(8,128)S(1)}, f32[136,128]{1,0:T(8,128)S(1)}, u32[]{:S(2)}, u32[]{:S(2)}) collective-permute-start(f32[136,128]{1,0:T(8,128)S(1)} %add.22), channel_id=1, source_target_pairs={{0,8},{8,0},{16,24},{24,16},{32,40},{40,32},{48,56},{56,48},{64,72... | collective-permute-start | bytes 208904 | tf_op jit(solution)/shard_map/ppermute | solution.py:340
  111.4 8.7 %collective-permute-start.4 = (bf16[8,512,256]{2,1,0:T(8,128)(2,1)S(1)}, bf16[8,512,256]{2,1,0:T(8,128)(2,1)S(1)}, u32[]{:S(2)}, u32[]{:S(2)}) collective-permute-start(bf16[8,512,256]{2,1,0:T(8,128)(2,1)S(1)} %all-to-all-done.2.mine_ref), channel_id=1, source_target_pairs={{0,8},{8,0},{16,24},{24,16},{32,40},{40,32},{48,56},{56,48},{64,72... | collective-permute-start | bytes 6291464 | tf_op jit(solution)/shard_map/ppermute | solution.py:328
  114.4 5.7 %collective-permute-start.5 = (f32[136,128]{1,0:T(8,128)S(1)}, f32[136,128]{1,0:T(8,128)S(1)}, u32[]{:S(2)}, u32[]{:S(2)}) collective-permute-start(f32[136,128]{1,0:T(8,128)S(1)} %add.23), channel_id=1, source_target_pairs={{0,1},{1,0},{2,3},{3,2},{4,5},{5,4},{6,7},{7,6},{8,9},{9,8},{10,11... | collective-permute-start | bytes 208904 | tf_op jit(solution)/shard_map/ppermute | solution.py:340
  120.1 9.7 %collective-permute-start.6 = (f32[136,128]{1,0:T(8,128)S(1)}, f32[136,128]{1,0:T(8,128)S(1)}, u32[]{:S(2)}, u32[]{:S(2)}) collective-permute-start(f32[136,128]{1,0:T(8,128)S(1)} %add.24), channel_id=1, source_target_pairs={{0,16},{8,24},{16,0},{24,8},{32,48},{40,56},{48,32},{56,40},{64,80... | collective-permute-start | bytes 208904 | tf_op jit(solution)/shard_map/ppermute | solution.py:340
  129.8 33.6 %all-to-all-start.3 = ((bf16[8,512,256]{2,1,0:T(8,128)(2,1)}), bf16[8,512,256]{2,1,0:T(8,128)(2,1)S(1)}, u32[]{:S(2)}, u32[]{:S(2)}) async-start(bf16[8,512,256]{2,1,0:T(8,128)(2,1)} %backward_tiles.1), calls=%async_computation.3 | async-start | bytes 4194304 | tf_op jit(solution)/shard_map/all_to_all | solution.py:336
  137.0 3.9 %collective-permute-start.7 = (f32[136,128]{1,0:T(8,128)S(1)}, f32[136,128]{1,0:T(8,128)S(1)}, u32[]{:S(2)}, u32[]{:S(2)}) collective-permute-start(f32[136,128]{1,0:T(8,128)S(1)} %add.25), channel_id=1, source_target_pairs={{0,32},{8,40},{16,48},{24,56},{32,0},{40,8},{48,16},{56,24},{64,96... | collective-permute-start | bytes 208904 | tf_op jit(solution)/shard_map/ppermute | solution.py:340
  140.9 5.0 %collective-permute-start.8 = (f32[136,128]{1,0:T(8,128)S(1)}, f32[136,128]{1,0:T(8,128)S(1)}, u32[]{:S(2)}, u32[]{:S(2)}) collective-permute-start(f32[136,128]{1,0:T(8,128)S(1)} %add.26), channel_id=1, source_target_pairs={{0,64},{8,72},{16,80},{24,88},{32,96},{40,104},{48,112},{56,120},{... | collective-permute-start | bytes 208904 | tf_op jit(solution)/shard_map/ppermute | solution.py:340
